TPU v7x, 32 devices: a whole 2x2x4 slice. The times are simulated.
32 devices in a mesh: grp: 4 (over y, core), sub: 8 (over z, x).
Axes of the slice: x: 2, y: 2, z: 4, core: 2. Of those that a mesh axis runs over, the one named last changes fastest.
Arguments:
- right_side: float32 [8192, 2048], P(('grp', 'sub'))
- schur: bfloat16 [16384, 512], P(('grp', 'sub'))
- inv_factor: bfloat16 [16384, 512], P(('grp', 'sub'))
- coarse_inverse: float32 [256, 64], P('grp')
- primal_index: int32 [32, 8], P(('grp', 'sub')), may hold values from 0 to 255
- phase: int32 [8192], P(('grp', 'sub')), may hold values from 0 to 3
- phase_coef: float32 [4], replicated, may hold values from 0.5 to 4
Outputs:
- solution: float32 [8192, 2048], P(('grp', 'sub'))
- residual: float32 [8192, 2048], P(('grp', 'sub'))
All inputs are finite; a program needn't handle non-finite values.
Results may differ from a plain program's by a relative error of at most 0.0056.
Values may be sent and summed in bfloat16 or wider, within the bound.
No kernel may reach another device: no remote copies, remote signals or barrier semaphores. Data moves between devices by JAX's collectives and lax.ppermute only.
A program may use at most 64 MiB of HBM per device.

v0:
```python
import jax
import jax.numpy as jnp
from jax import lax
from jax.sharding import PartitionSpec as P


def shifted(value, axis, steps):
    count = lax.axis_size(axis)
    pairs = [(source, (source + steps) % count) for source in range(count)]
    return lax.ppermute(value, axis, pairs)


def transposed(matrix, operand):
    return lax.dot_general(
        matrix, operand, (((0,), (0,)), ((), ())), preferred_element_type=jnp.float32
    )


def body(right_side, schur, inv_factor, coarse_inverse, primal_index, phase, phase_coef):
    highest = lax.Precision.HIGHEST
    face_rows = right_side.shape[0]
    columns = jnp.arange(face_rows, dtype=jnp.int32)
    onehot = (primal_index[0][:, None] == columns[None, :]).astype(jnp.float32)
    primal_count = onehot.shape[0]
    resid_b = right_side.astype(jnp.bfloat16)
    left_resid = shifted(resid_b, "sub", 1)
    local_resid = jnp.concatenate([left_resid, resid_b], axis=0)
    first = jnp.dot(inv_factor, local_resid, preferred_element_type=jnp.float32).astype(
        jnp.bfloat16
    )
    second = transposed(inv_factor, first).astype(jnp.bfloat16)
    upper = second[:face_rows]
    from_right = shifted(upper, "sub", -1)
    lower = second[face_rows:]
    local_part = lower.astype(jnp.float32) + from_right.astype(jnp.float32)
    own_primal = jnp.dot(onehot, right_side, precision=highest)
    position = lax.axis_index("sub")
    group_primal = lax.all_gather(own_primal, "sub", axis=0, tiled=True)
    my_rows = lax.dynamic_slice_in_dim(coarse_inverse, position * primal_count, primal_count, 0)
    solved = jnp.dot(my_rows, group_primal, precision=highest)
    summed = lax.psum(solved, "grp")
    correction = solved + summed / lax.axis_size("grp")
    scattered = lax.dot_general(onehot, correction, (((0,), (0,)), ((), ())), precision=highest)
    direction = 0.5 * local_part + scattered
    dir_b = direction.astype(jnp.bfloat16)
    rz_part = jnp.sum(right_side * direction, axis=0)
    left_dir = shifted(dir_b, "sub", 1)
    image = jnp.dot(
        schur, jnp.concatenate([left_dir, dir_b], axis=0), preferred_element_type=jnp.float32
    ).astype(jnp.bfloat16)
    image_up = image[:face_rows]
    image_right = shifted(image_up, "sub", -1)
    image_low = image[face_rows:]
    phase_table = (
        phase[:, None] == jnp.arange(phase_coef.shape[0], dtype=jnp.int32)[None, :]
    ).astype(jnp.float32)
    coef_rows = jnp.dot(phase_table, phase_coef, precision=highest)
    dir_f = dir_b.astype(jnp.float32)
    qvec = (
        image_low.astype(jnp.float32) + image_right.astype(jnp.float32) + coef_rows[:, None] * dir_f
    )
    pq_part = jnp.sum(dir_f * qvec, axis=0)
    rz_total, pq_total = lax.psum((rz_part, pq_part), ("grp", "sub"))
    alpha = rz_total / pq_total
    return (alpha * dir_f, right_side - alpha * qvec)


def solution(mesh):
    in_specs = (
        P(("grp", "sub"), None),
        P(("grp", "sub"), None),
        P(("grp", "sub"), None),
        P("grp", None),
        P(("grp", "sub"), None),
        P(("grp", "sub")),
        P(),
    )
    out_specs = (P(("grp", "sub"), None), P(("grp", "sub"), None))
    return jax.shard_map(body, mesh=mesh, in_specs=in_specs, out_specs=out_specs, check_vma=False)
```

profile of v0, /device:TPU:0, one launch (start us, length us, event | category | flops | bytes accessed | tf_op | source)
XLA Modules:
  0.0 235.5 jit_solution(18217417016584110574)
XLA Ops:
  7.2 0.0 all-reduce.3.cloned.1.call-start
  7.2 1.8 convert_element_type.39
  9.0 3.0 %collective-permute-start = (bf16[256,2048]{1,0:T(8,128)(2,1)S(1)}, bf16[256,2048]{1,0:T(8,128)(2,1)S(1)}, u32[]{:S(2)}, u32[]{:S(2)}) collective-permute-start(bf16[256,2048]{1,0:T(8,128)(2,1)S(1)} %convert_element_type.39), channel_id=1, source_target_pairs={{0,1},{1,2},{2,3},{3,4},{4,5},{5,6},{6,7},{7,0},{8,9},{9,10},{10,1... | collective-permute-start | bytes 3145736 | tf_op jit(solution)/shard_map/ppermute | solution.py:10
  12.0 26.2 %collective-permute-done = bf16[256,2048]{1,0:T(8,128)(2,1)S(1)} collective-permute-done((bf16[256,2048]{1,0:T(8,128)(2,1)S(1)}, bf16[256,2048]{1,0:T(8,128)(2,1)S(1)}, u32[]{:S(2)}, u32[]{:S(2)}) %collective-permute-start) | collective-permute-done | bytes 1048608 | tf_op jit(solution)/shard_map/ppermute | solution.py:10
  38.2 3.7 %fusion = bf16[512,2048]{1,0:T(8,128)(2,1)} fusion(bf16[512,512]{1,0:T(8,128)(2,1)S(1)} %copy-done, bf16[256,2048]{1,0:T(8,128)(2,1)S(1)} %convert_element_type.39, bf16[256,2048]{1,0:T(8,128)(2,1)S(1)} %collective-permute-done), kind=kOutput, calls=%fused_computation.6 | convolution fusion | flops 2153775104 | bytes 4718592 | tf_op jit(solution)/shard_map/dot_general | solution.py:14
  41.9 2.5 %slice.17 = bf16[256,2048]{1,0:T(8,128)(2,1)} slice(bf16[512,2048]{1,0:T(8,128)(2,1)} %fusion), slice={[0:256], [0:2048]} | slice | bytes 2097152 | tf_op jit(solution)/shard_map/slice | solution.py:32
  44.4 1.7 collective-permute-start.1
  46.1 0.8 fusion.19
  46.9 47.7 %all_gather.3 = f32[64,2048]{1,0:T(8,128)S(1)} all-gather(f32[8,2048]{1,0:T(8,128)S(1)} %fusion.19), channel_id=1, replica_groups=mesh['grp'=4,'sub'=8] {'sub'}, dimensions={0}, use_global_device_ids=true | all-gather | bytes 589824 | tf_op jit(solution)/shard_map/all_gather | solution.py:38
  94.6 1.7 fusion.20
  96.3 32.0 %all-reduce.3.cloned.1.call-done = f32[8,2048]{1,0:T(8,128)} async-done(((f32[8,2048]{1,0:T(8,128)}), f32[8,2048]{1,0:T(8,128)}) %all-reduce.3.cloned.1.call-update) | async-done | bytes 65552 | tf_op jit(solution)/shard_map/psum | solution.py:41
  128.3 2.1 fusion.15
  130.5 1.9 multiply_reduce_fusion
  132.4 1.5 collective-permute-start.2
  133.9 24.9 %collective-permute-done.2 = bf16[256,2048]{1,0:T(8,128)(2,1)S(1)} collective-permute-done((bf16[256,2048]{1,0:T(8,128)(2,1)S(1)}, bf16[256,2048]{1,0:T(8,128)(2,1)S(1)}, u32[]{:S(2)}, u32[]{:S(2)}) %collective-permute-start.2) | collective-permute-done | bytes 1048608 | tf_op jit(solution)/shard_map/ppermute | solution.py:10
  158.8 1.3 fusion.1
  160.1 0.1 slice.19
  160.2 1.8 collective-permute-start.3
  162.0 0.2 fusion.13
  162.2 20.8 %collective-permute-done.3 = bf16[256,2048]{1,0:T(8,128)(2,1)S(1)} collective-permute-done((bf16[256,2048]{1,0:T(8,128)(2,1)S(1)}, bf16[256,2048]{1,0:T(8,128)(2,1)S(1)}, u32[]{:S(2)}, u32[]{:S(2)}) %collective-permute-start.3) | collective-permute-done | bytes 1048608 | tf_op jit(solution)/shard_map/ppermute | solution.py:10
  183.0 0.7 fusion.3
  183.7 0.3 copy-done.4
  184.0 39.8 %all-reduce = (f32[2048]{0:T(1024)S(1)}, f32[2048]{0:T(1024)S(1)}) all-reduce(f32[2048]{0:T(1024)S(1)} %get-tuple-element.4, f32[2048]{0:T(1024)S(1)} %fusion.3), channel_id=1, replica_groups=mesh['grp'=4,'sub'=8] {'grp','sub'}, use_global_device_ids=true, to_apply=%region_2.0 | all-reduce | flops 4096 | bytes 32768 | tf_op jit(solution)/shard_map/psum | solution.py:63
  223.9 4.8 %multiply_subtract_fusion = (f32[256,2048]{1,0:T(8,128)}, f32[256,2048]{1,0:T(8,128)}) fusion(f32[256,2048]{1,0:T(8,128)S(1)} %copy-done.1, bf16[256,2048]{1,0:T(8,128)(2,1)} %copy-done.2, bf16[256,2048]{1,0:T(8,128)(2,1)} %copy-done.4, f32[2048]{0:T(1024)S(1)} %div.11, f32[256]{0:T(256)S(1)} %bitcast.15, bf16[512,2048]{1,0:T(8,128)(2,1)} %copy-done.3), kind=kLoop, calls=%fused_computation.16 | loop fusion | flops 4718592 | bytes 9446400 | tf_op jit(solution)/shard_map/sub | solution.py:65
  (22 shorter events, 0.1 us)
Async XLA Ops:
  7.2 31.0 %copy-start = (bf16[512,512]{1,0:T(8,128)(2,1)S(1)}, bf16[512,512]{1,0:T(8,128)(2,1)}, u32[]{:S(2)}) copy-start(bf16[512,512]{1,0:T(8,128)(2,1)} %param.9) | copy-start | bytes 1572868
  7.2 121.1 %all-reduce.3.cloned.1.call-start = ((), (), s32[]{:S(2)}) async-start(), calls=%async_computation | async-start | bytes 131072 | tf_op jit(solution)/shard_map/psum | solution.py:41
  9.0 29.2 %collective-permute-start = (bf16[256,2048]{1,0:T(8,128)(2,1)S(1)}, bf16[256,2048]{1,0:T(8,128)(2,1)S(1)}, u32[]{:S(2)}, u32[]{:S(2)}) collective-permute-start(bf16[256,2048]{1,0:T(8,128)(2,1)S(1)} %convert_element_type.39), channel_id=1, source_target_pairs={{0,1},{1,2},{2,3},{3,4},{4,5},{5,6},{6,7},{7,0},{8,9},{9,10},{10,1... | collective-permute-start | bytes 3145736 | tf_op jit(solution)/shard_map/ppermute | solution.py:10
  41.9 4.2 %copy-start.1 = (f32[256,2048]{1,0:T(8,128)S(1)}, f32[256,2048]{1,0:T(8,128)}, u32[]{:S(2)}) copy-start(f32[256,2048]{1,0:T(8,128)} %param.7) | copy-start | bytes 6291460
  41.9 4.2 %copy-start.6 = (s32[1,8]{1,0:T(1,128)S(1)}, s32[1,8]{1,0:T(1,128)}, u32[]{:S(2)}) copy-start(s32[1,8]{1,0:T(1,128)} %param.11) | copy-start | bytes 100
  44.4 86.1 %collective-permute-start.1 = (bf16[256,2048]{1,0:T(8,128)(2,1)}, bf16[256,2048]{1,0:T(8,128)(2,1)}, u32[]{:S(2)}, u32[]{:S(2)}) collective-permute-start(bf16[256,2048]{1,0:T(8,128)(2,1)} %slice.17), channel_id=1, source_target_pairs={{0,7},{1,0},{2,1},{3,2},{4,3},{5,4},{6,5},{7,6},{8,15},{9,8},{10,9... | collective-permute-start | bytes 3145736 | tf_op jit(solution)/shard_map/ppermute | solution.py:10
  128.3 2.1 copy-start.5
  130.4 28.4 %copy-start.7 = (bf16[512,512]{1,0:T(8,128)(2,1)S(1)}, bf16[512,512]{1,0:T(8,128)(2,1)}, u32[]{:S(2)}) copy-start(bf16[512,512]{1,0:T(8,128)(2,1)} %param.8) | copy-start | bytes 1572868
  132.4 50.7 %copy-start.2 = (bf16[256,2048]{1,0:T(8,128)(2,1)}, bf16[256,2048]{1,0:T(8,128)(2,1)S(1)}, u32[]{:S(2)}) copy-start(bf16[256,2048]{1,0:T(8,128)(2,1)S(1)} %get-tuple-element.5) | copy-start | bytes 3145732
  132.4 26.4 %collective-permute-start.2 = (bf16[256,2048]{1,0:T(8,128)(2,1)S(1)}, bf16[256,2048]{1,0:T(8,128)(2,1)S(1)}, u32[]{:S(2)}, u32[]{:S(2)}) collective-permute-start(bf16[256,2048]{1,0:T(8,128)(2,1)S(1)} %get-tuple-element.5), channel_id=1, source_target_pairs={{0,1},{1,2},{2,3},{3,4},{4,5},{5,6},{6,7},{7,0},{8,9},{9,10},{10,1... | collective-permute-start | bytes 3145736 | tf_op jit(solution)/shard_map/ppermute | solution.py:10
  160.1 23.7 %copy-start.3 = (bf16[512,2048]{1,0:T(8,128)(2,1)}, bf16[512,2048]{1,0:T(8,128)(2,1)S(1)}, u32[]{:S(2)}) copy-start(bf16[512,2048]{1,0:T(8,128)(2,1)S(1)} %fusion.1) | copy-start | bytes 6291460
  160.1 1.9 copy-start.8
  160.1 1.9 copy-start.9
  160.2 22.8 %collective-permute-start.3 = (bf16[256,2048]{1,0:T(8,128)(2,1)S(1)}, bf16[256,2048]{1,0:T(8,128)(2,1)S(1)}, u32[]{:S(2)}, u32[]{:S(2)}) collective-permute-start(bf16[256,2048]{1,0:T(8,128)(2,1)S(1)} %slice.19), channel_id=1, source_target_pairs={{0,7},{1,0},{2,1},{3,2},{4,3},{5,4},{6,5},{7,6},{8,15},{9,8},{10,9... | collective-permute-start | bytes 3145736 | tf_op jit(solution)/shard_map/ppermute | solution.py:10
  183.0 1.0 copy-start.4
Sparse Core Ops, SparseCore 0:
  96.4 31.8 all-reduce.2
where the time goes:
time: 236 us; the launch traced here: 235 us
  waiting for transfers between devices  104 us (44%)
  blocking collectives  87.5 us (37%)
  between operations  14.1 us (6%)
  matrix products  9.74 us (4%)
  other arithmetic  9.16 us (4%)
  starting transfers between devices  8.08 us (3%)
  local copies, waits for them, and re-layouts  2.87 us (1%)
    ppermute x4, waiting for transfers between devices, shifted(): return lax.ppermute(value, axis, pairs)  71.9 us
    all_gather x1, blocking collectives, body(): group_primal = lax.all_gather(own_primal, 'sub', axis=0, tiled=True)  47.7 us
    psum x1, blocking collectives, body(): rz_total, pq_total = lax.psum((rz_part, pq_part), ('grp', 'sub'))  39.8 us
    psum x1, waiting for transfers between devices, body(): summed = lax.psum(solved, 'grp')  32 us
    ppermute x4, starting transfers between devices, shifted(): return lax.ppermute(value, axis, pairs)  8.04 us
    sub x1, other arithmetic, body(): return (alpha * dir_f, right_side - alpha * qvec)  4.77 us
  transfers between devices with their start and end apart: 5, of which 4 were waited for; matrix products, arithmetic and copies ran while one was open for 2% of the time, Pallas kernels for 0%

commit v1 on v0

v1 whole, which is shorter than its diff:
```python
import functools

import jax
import jax.numpy as jnp
from jax import lax
from jax.experimental import pallas as pl
from jax.experimental.pallas import tpu as pltpu
from jax.sharding import PartitionSpec as P

HIGHEST = lax.Precision.HIGHEST
VMEM = pltpu.VMEM
SMEM = pltpu.SMEM
F32 = jnp.float32
BF16 = jnp.bfloat16


def widths(columns):
    return [columns // 4] * 4


def starts(sizes):
    return [sum(sizes[:i]) for i in range(len(sizes))]


def params():
    return pltpu.CompilerParams(vmem_limit_bytes=40 * 1024 * 1024)


def whole(space=VMEM):
    return pl.BlockSpec(memory_space=space)


def pair_swap(value):
    count = lax.axis_size("sub")
    return lax.ppermute(value, "sub", [(j, j ^ 1) for j in range(count)])


def pass_on(value):
    count = lax.axis_size("sub")
    pairs = [(j, (j + (2 if j % 2 == 0 else -2)) % count) for j in range(count)]
    return lax.ppermute(value, "sub", pairs)


def to_left(value):
    count = lax.axis_size("sub")
    return lax.ppermute(value, "sub", [(j, (j - 1) % count) for j in range(count)])


def summed_over(value, axis):
    count = lax.axis_size(axis)
    if count & (count - 1):
        return lax.psum(value, axis)
    step = 1
    while step < count:
        value = value + lax.ppermute(value, axis, [(i, i ^ step) for i in range(count)])
        step *= 2
    return value


def from_all(value):
    devices = lax.axis_size("grp") * lax.axis_size("sub")
    copies = jnp.broadcast_to(value[None], (devices,) + value.shape)
    return lax.all_to_all(copies, ("grp", "sub"), 0, 0, tiled=True)


def split_kernel(sizes, index_ref, right_ref, primal_ref, *chunk_refs):
    for k in range(primal_ref.shape[0]):
        primal_ref[k : k + 1, :] = right_ref[pl.ds(index_ref[0, k], 1), :]
    for begin, size, chunk_ref in zip(starts(sizes), sizes, chunk_refs):
        chunk_ref[...] = right_ref[:, begin : begin + size].astype(BF16)


def split(right_side, primal_index, sizes):
    rows, columns = right_side.shape
    outs = [jax.ShapeDtypeStruct((primal_index.shape[1], columns), F32)]
    outs += [jax.ShapeDtypeStruct((rows, size), BF16) for size in sizes]
    out = pl.pallas_call(
        functools.partial(split_kernel, sizes),
        out_shape=outs,
        in_specs=[whole(SMEM), whole()],
        out_specs=[whole()] * len(outs),
        compiler_params=params(),
        name="split",
    )(primal_index, right_side)
    return out[0], list(out[1:])


def gram_kernel(factor_ref, upper_ref, lower_ref):
    half = upper_ref.shape[0]
    dims = (((0,), (0,)), ((), ()))
    factor = factor_ref[...]
    product = lax.dot_general(factor, factor, dims, preferred_element_type=F32)
    upper_ref[...] = product[:half].astype(BF16)
    lower_ref[...] = product[half:].astype(BF16)


def gram(factor):
    size = factor.shape[0]
    out = jax.ShapeDtypeStruct((size // 2, size), BF16)
    return pl.pallas_call(
        gram_kernel,
        out_shape=[out, out],
        in_specs=[whole()],
        out_specs=[whole(), whole()],
        compiler_params=params(),
        name="gram",
    )(factor)


def stencil(parity, low, up, swapped, own, passed):
    half = low.shape[0]
    even = parity == 0
    for_swapped = jnp.where(even, up[:, half:], low[:, :half])
    for_passed = jnp.where(even, low[:, :half], up[:, half:])
    dot = functools.partial(jnp.dot, preferred_element_type=F32)
    total = dot(low[:, half:], own) + dot(up[:, :half], own)
    total = total + dot(for_swapped, swapped)
    return total + dot(for_passed, passed)


def direction_kernel(
    parity_ref, index_ref, low_ref, up_ref, swapped_ref, own_ref, passed_ref, right_ref, corr_ref,
    dir_ref, rz_ref, full_ref,
):
    full_ref[...] = 0.5 * stencil(
        parity_ref[0], low_ref[...], up_ref[...], swapped_ref[...], own_ref[...], passed_ref[...]
    )
    for k in range(corr_ref.shape[0]):
        row = pl.ds(index_ref[0, k], 1)
        full_ref[row, :] = full_ref[row, :] + corr_ref[k : k + 1, :]
    full = full_ref[...]
    dir_ref[...] = full.astype(BF16)
    rz_ref[...] = jnp.sum(right_ref[...] * full, axis=0, keepdims=True)


def direction_chunk(parity, index, low, up, swapped, own, passed, right_side, corr, begin):
    rows, size = own.shape
    block = begin // size
    full = lambda a: pl.BlockSpec(a.shape, lambda i: (0,) * a.ndim)
    part = lambda a: pl.BlockSpec((a.shape[0], size), lambda i: (0, block))
    return pl.pallas_call(
        direction_kernel,
        grid=(1,),
        out_shape=[
            jax.ShapeDtypeStruct((rows, size), BF16),
            jax.ShapeDtypeStruct((1, size), F32),
        ],
        in_specs=[whole(SMEM), whole(SMEM)]
        + [full(a) for a in (low, up, swapped, own, passed)]
        + [part(right_side), part(corr)],
        out_specs=[
            pl.BlockSpec((rows, size), lambda i: (0, 0)),
            pl.BlockSpec((1, size), lambda i: (0, 0)),
        ],
        scratch_shapes=[pltpu.VMEM((rows, size), F32)],
        compiler_params=params(),
        name="direction",
    )(parity, index, low, up, swapped, own, passed, right_side, corr)


def image_kernel(
    parity_ref, panel_ref, up_ref, swapped_ref, own_ref, passed_ref, coef_ref, q_ref, pq_ref
):
    own = own_ref[...]
    total = stencil(
        parity_ref[0], panel_ref[...], up_ref[...], swapped_ref[...], own, passed_ref[...]
    )
    own_f = own.astype(F32)
    q = total + coef_ref[:, :1] * own_f
    q_ref[...] = q
    pq_ref[...] = jnp.sum(own_f * q, axis=0, keepdims=True)


def image_chunk(parity, schur, up, swapped, own, passed, coef):
    rows, size = own.shape
    full = lambda a: pl.BlockSpec(a.shape, lambda i: (0,) * a.ndim)
    return pl.pallas_call(
        image_kernel,
        grid=(1,),
        out_shape=[
            jax.ShapeDtypeStruct((rows, size), F32),
            jax.ShapeDtypeStruct((1, size), F32),
        ],
        in_specs=[
            whole(SMEM),
            pl.BlockSpec((rows, 2 * rows), lambda i: (1, 0)),
        ]
        + [full(a) for a in (up, swapped, own, passed, coef)],
        out_specs=[
            pl.BlockSpec((rows, size), lambda i: (0, 0)),
            pl.BlockSpec((1, size), lambda i: (0, 0)),
        ],
        compiler_params=params(),
        name="image",
    )(parity, schur, up, swapped, own, passed, coef)


def update_kernel(sizes, sums_ref, last_ref, right_ref, *refs):
    count = len(sizes)
    dirs, qs, (solution_ref, residual_ref) = refs[:count], refs[count : 2 * count], refs[2 * count :]
    for i, (begin, size) in enumerate(zip(starts(sizes), sizes)):
        if i < count - 1:
            sums = sums_ref[:, begin : begin + size]
        else:
            sums = jnp.sum(last_ref[...], axis=0)
        alpha = sums[0:1] / sums[1:2]
        cols = slice(begin, begin + size)
        solution_ref[:, cols] = alpha * dirs[i][...].astype(F32)
        residual_ref[:, cols] = right_ref[:, cols] - alpha * qs[i][...]


def update(sums, last, right_side, dirs, qs, sizes):
    out = jax.ShapeDtypeStruct(right_side.shape, F32)
    return pl.pallas_call(
        functools.partial(update_kernel, sizes),
        out_shape=[out, out],
        in_specs=[whole()] * (3 + 2 * len(sizes)),
        out_specs=[whole(), whole()],
        compiler_params=params(),
        name="update",
    )(sums, last, right_side, *dirs, *qs)


def body(right_side, schur, inv_factor, coarse_inverse, primal_index, phase, phase_coef):
    face_rows, columns = right_side.shape
    sizes = widths(columns)
    begins = starts(sizes)
    parity = (lax.axis_index("sub") % 2).astype(jnp.int32)[None]

    own_primal, resid = split(right_side, primal_index, sizes)
    swapped = [pair_swap(c) for c in resid]
    gram_up, gram_low = gram(inv_factor)
    gram_next = to_left(gram_up)
    schur_next = to_left(schur[:face_rows])
    passed = [pass_on(c) for c in swapped]

    group_primal = lax.all_to_all(own_primal, "sub", 1, 0, tiled=True)
    solved = jnp.dot(coarse_inverse, group_primal, precision=HIGHEST)
    mean = summed_over(solved, "grp") / lax.axis_size("grp")
    correction = lax.all_to_all(solved + mean, "sub", 0, 1, tiled=True)

    dirs, rzs = [], []
    for i, begin in enumerate(begins):
        d, rz = direction_chunk(
            parity, primal_index, gram_low, gram_next, swapped[i], resid[i], passed[i],
            right_side, correction, begin,
        )
        dirs.append(d)
        rzs.append(rz)
    dir_swapped = [pair_swap(d) for d in dirs]
    dir_passed = [pass_on(d) for d in dir_swapped]

    labels = jnp.arange(phase_coef.shape[0], dtype=jnp.int32)
    coef = jnp.sum(
        jnp.where(phase[:, None] == labels[None, :], phase_coef[None, :], 0.0), axis=1
    )
    coef = jnp.broadcast_to(coef[:, None], (face_rows, 128))

    qs, parts = [], []
    for i in range(len(sizes)):
        q, pq = image_chunk(parity, schur, schur_next, dir_swapped[i], dirs[i], dir_passed[i], coef)
        qs.append(q)
        parts.append(jnp.concatenate([rzs[i], pq], axis=0))
    early = jnp.concatenate(parts[:-1], axis=1)
    early = summed_over(summed_over(early, "grp"), "sub")
    last = from_all(parts[-1])
    return update(early, last, right_side, dirs, qs, sizes)


def solution(mesh):
    in_specs = (
        P(("grp", "sub"), None),
        P(("grp", "sub"), None),
        P(("grp", "sub"), None),
        P("grp", None),
        P(("grp", "sub"), None),
        P(("grp", "sub")),
        P(),
    )
    out_specs = (P(("grp", "sub"), None), P(("grp", "sub"), None))
    return jax.shard_map(body, mesh=mesh, in_specs=in_specs, out_specs=out_specs, check_vma=False)
```

time: 236 us -> 126 us (0.53)
  blocking collectives: 87.5 us -> 0 us
  waiting for transfers between devices: 104 us -> 47.4 us
  starting transfers between devices: 8.08 us -> 51.8 us
  Pallas kernels: 0 us -> 14.1 us
  between operations: 14.1 us -> 0.94 us
  matrix products: 9.74 us -> 0.2 us
  other arithmetic: 9.16 us -> 0.81 us
  local copies, waits for them, and re-layouts: 2.87 us -> 10.6 us
    all_gather x1 -> x0, blocking collectives: 47.7 us -> none  [body(): group_primal = lax.all_gather(own_primal, 'sub', axis=0, tiled=True)]
    psum x1 -> x0, blocking collectives: 39.8 us -> none  [body(): rz_total, pq_total = lax.psum((rz_part, pq_part), ('grp', 'sub'))]
    ppermute x4 -> x25, waiting for transfers between devices: 71.9 us -> 34.5 us  [the longest x8 19.9 us: pair_swap(): return lax.ppermute(value, 'sub', [(j, j ^ 1) for j in range(count)])]
    psum x1 -> x0, waiting for transfers between devices: 32 us -> none  [body(): summed = lax.psum(solved, 'grp')]
    ppermute x4 -> x25, starting transfers between devices: 8.04 us -> 31.7 us  [the longest x8 13 us: pass_on(): return lax.ppermute(value, 'sub', pairs)]
    all_to_all x0 -> x3, starting transfers between devices: none -> 20.1 us  [the longest x1 7.25 us: body(): group_primal = lax.all_to_all(own_primal, 'sub', 1, 0, tiled=True)]
    pallas_call x0 -> x11, Pallas kernels: none -> 14.1 us  [the longest x4 6.43 us: direction_chunk(): pl.pallas_call(direction_kernel, grid=(1,), out_shape=[jax.ShapeDtypeStru...]
    all_to_all x0 -> x3, waiting for transfers between devices: none -> 12.9 us  [the longest x1 9.96 us: body(): correction = lax.all_to_all(solved + mean, 'sub', 0, 1, tiled=True)]
  transfers between devices with their start and end apart: 5 -> 28, of which waited for: 4 -> 14; matrix products, arithmetic and copies ran while one was open for 2% -> 1% of each run, Pallas kernels for 0% -> 7%
where the time goes in v1:
time: 126 us
  starting transfers between devices  51.8 us (41%)
  waiting for transfers between devices  47.4 us (38%)
  Pallas kernels  14.1 us (11%)
  local copies, waits for them, and re-layouts  10.6 us (8%)
    ppermute x8, waiting for transfers between devices, pair_swap(): return lax.ppermute(value, 'sub', [(j, j ^ 1) for j in range(count)])  19.9 us
    ppermute x8, starting transfers between devices, pass_on(): return lax.ppermute(value, 'sub', pairs)  13 us
    all_to_all x1, waiting for transfers between devices, body(): correction = lax.all_to_all(solved + mean, 'sub', 0, 1, tiled=True)  9.96 us
    unnamed x42, local copies, waits for them, and re-layouts  9.78 us
    ppermute x8, starting transfers between devices, pair_swap(): return lax.ppermute(value, 'sub', [(j, j ^ 1) for j in range(count)])  8.65 us
    ppermute x7, starting transfers between devices, summed_over(): lax.ppermute(value, axis, [(i, i ^ step) for i in range(count)])  8.62 us
    ppermute x7, waiting for transfers between devices, summed_over(): lax.ppermute(value, axis, [(i, i ^ step) for i in range(count)])  7.55 us
    all_to_all x1, starting transfers between devices, body(): group_primal = lax.all_to_all(own_primal, 'sub', 1, 0, tiled=True)  7.25 us
  transfers between devices with their start and end apart: 28, of which 14 were waited for; matrix products, arithmetic and copies ran while one was open for 1% of the time, Pallas kernels for 7%

profile of v1, /device:TPU:0, one launch (start us, length us, event | category | flops | bytes accessed | tf_op | source)
XLA Modules:
  0.0 125.8 jit_solution(9662881175307202487)
XLA Ops:
  4.3 7.3 %all-to-all-start = ((f32[8,8,256]{2,0,1:T(8,128)}), f32[8,8,256]{2,0,1:T(8,128)S(1)}, u32[]{:S(2)}, u32[]{:S(2)}) async-start(f32[8,8,256]{2,0,1:T(8,128)} %bitcast.1), calls=%async_computation | async-start | bytes 131072 | tf_op jit(solution)/shard_map/all_to_all | solution.py:237
  11.5 2.0 %collective-permute-start.1 = (bf16[256,512]{1,0:T(8,128)(2,1)}, bf16[256,512]{1,0:T(8,128)(2,1)}, u32[]{:S(2)}, u32[]{:S(2)}) collective-permute-start(bf16[256,512]{1,0:T(8,128)(2,1)} %get-tuple-element.27.own_ref), channel_id=1, source_target_pairs={{0,1},{1,0},{2,3},{3,2},{4,5},{5,4},{6,7},{7,6},{8,9},{9,8},{10,11... | collective-permute-start | bytes 786440 | tf_op jit(solution)/shard_map/ppermute | solution.py:35
  13.6 2.0 %collective-permute-start.12 = (bf16[256,512]{1,0:T(8,128)(2,1)S(1)}, bf16[256,512]{1,0:T(8,128)(2,1)}, u32[]{:S(2)}, u32[]{:S(2)}) collective-permute-start(bf16[256,512]{1,0:T(8,128)(2,1)S(1)} %get-tuple-element.36.own_ref), channel_id=1, source_target_pairs={{0,1},{1,0},{2,3},{3,2},{4,5},{5,4},{6,7},{7,6},{8,9},{9,8},{10,11... | collective-permute-start | bytes 786440 | tf_op jit(solution)/shard_map/ppermute | solution.py:35
  15.6 3.0 %all-to-all-done = f32[8,8,256]{2,0,1:T(8,128)S(1)} async-done(((f32[8,8,256]{2,0,1:T(8,128)}), f32[8,8,256]{2,0,1:T(8,128)S(1)}, u32[]{:S(2)}, u32[]{:S(2)}) %all-to-all-start) | async-done | bytes 65568 | tf_op jit(solution)/shard_map/all_to_all | solution.py:237
  27.3 5.2 %collective-permute-start.9 = (bf16[256,512]{1,0:T(8,128)(2,1)}, bf16[256,512]{1,0:T(8,128)(2,1)}, u32[]{:S(2)}, u32[]{:S(2)}) collective-permute-start(bf16[256,512]{1,0:T(8,128)(2,1)} %collective-permute-done.8.swapped_ref), channel_id=1, source_target_pairs={{0,2},{1,7},{2,4},{3,1},{4,6},{5,3},{6,0},{7,5},{8,10},{9,15},{10,... | collective-permute-start | bytes 786440 | tf_op jit(solution)/shard_map/ppermute | solution.py:41
  32.5 5.0 %collective-permute-done.12.swapped_ref = bf16[256,512]{1,0:T(8,128)(2,1)} collective-permute-done((bf16[256,512]{1,0:T(8,128)(2,1)S(1)}, bf16[256,512]{1,0:T(8,128)(2,1)}, u32[]{:S(2)}, u32[]{:S(2)}) %collective-permute-start.12) | collective-permute-done | bytes 262176 | tf_op jit(solution)/shard_map/ppermute | solution.py:35
  39.6 5.6 %all-to-all-start.1 = ((f32[8,8,256]{2,1,0:T(8,128)}), f32[8,8,256]{2,1,0:T(8,128)S(1)}, u32[]{:S(2)}, u32[]{:S(2)}) async-start(f32[8,8,256]{2,1,0:T(8,128)} %add_bitcast_fusion), calls=%async_computation.1 | async-start | bytes 131072 | tf_op jit(solution)/shard_map/all_to_all | solution.py:240
  45.1 2.0 %collective-permute-start.22 = (bf16[256,512]{1,0:T(8,128)(2,1)}, bf16[256,512]{1,0:T(8,128)(2,1)}, u32[]{:S(2)}, u32[]{:S(2)}) collective-permute-start(bf16[256,512]{1,0:T(8,128)(2,1)} %collective-permute-done.21.swapped_ref), channel_id=1, source_target_pairs={{0,2},{1,7},{2,4},{3,1},{4,6},{5,3},{6,0},{7,5},{8,10},{9,15},{10,... | collective-permute-start | bytes 786440 | tf_op jit(solution)/shard_map/ppermute | solution.py:41
  47.2 10.0 %all-to-all-done.1 = f32[8,8,256]{2,1,0:T(8,128)S(1)} async-done(((f32[8,8,256]{2,1,0:T(8,128)}), f32[8,8,256]{2,1,0:T(8,128)S(1)}, u32[]{:S(2)}, u32[]{:S(2)}) %all-to-all-start.1) | async-done | bytes 65568 | tf_op jit(solution)/shard_map/all_to_all | solution.py:240
  68.1 2.8 %collective-permute-start.7 = (bf16[256,512]{1,0:T(8,128)(2,1)S(1)}, bf16[256,512]{1,0:T(8,128)(2,1)S(1)}, u32[]{:S(2)}, u32[]{:S(2)}) collective-permute-start(bf16[256,512]{1,0:T(8,128)(2,1)S(1)} %collective-permute-done.6.swapped_ref), channel_id=1, source_target_pairs={{0,2},{1,7},{2,4},{3,1},{4,6},{5,3},{6,0},{7,5},{8,10},{9,15},{10,... | collective-permute-start | bytes 786440 | tf_op jit(solution)/shard_map/ppermute | solution.py:41
  70.9 5.6 %collective-permute-done.10.swapped_ref = bf16[256,512]{1,0:T(8,128)(2,1)S(1)} collective-permute-done((bf16[256,512]{1,0:T(8,128)(2,1)S(1)}, bf16[256,512]{1,0:T(8,128)(2,1)S(1)}, u32[]{:S(2)}, u32[]{:S(2)}) %collective-permute-start.10) | collective-permute-done | bytes 262176 | tf_op jit(solution)/shard_map/ppermute | solution.py:35
  76.5 5.9 %collective-permute-done.14.swapped_ref = bf16[256,512]{1,0:T(8,128)(2,1)S(1)} collective-permute-done((bf16[256,512]{1,0:T(8,128)(2,1)S(1)}, bf16[256,512]{1,0:T(8,128)(2,1)S(1)}, u32[]{:S(2)}, u32[]{:S(2)}) %collective-permute-start.14) | collective-permute-done | bytes 262176 | tf_op jit(solution)/shard_map/ppermute | solution.py:35
  82.4 3.4 %collective-permute-done.23.swapped_ref = bf16[256,512]{1,0:T(8,128)(2,1)S(1)} collective-permute-done((bf16[256,512]{1,0:T(8,128)(2,1)S(1)}, bf16[256,512]{1,0:T(8,128)(2,1)S(1)}, u32[]{:S(2)}, u32[]{:S(2)}) %collective-permute-start.23) | collective-permute-done | bytes 262176 | tf_op jit(solution)/shard_map/ppermute | solution.py:35
  85.9 3.6 %collective-permute-done.5.up_ref = bf16[256,512]{1,0:T(8,128)(2,1)S(1)} collective-permute-done((bf16[256,512]{1,0:T(8,128)(2,1)S(1)}, bf16[256,512]{1,0:T(8,128)(2,1)S(1)}, u32[]{:S(2)}, u32[]{:S(2)}) %collective-permute-start.5) | collective-permute-done | bytes 262176 | tf_op jit(solution)/shard_map/ppermute | solution.py:46
  91.4 1.7 %collective-permute-done.15.passed_ref = bf16[256,512]{1,0:T(8,128)(2,1)S(1)} collective-permute-done((bf16[256,512]{1,0:T(8,128)(2,1)S(1)}, bf16[256,512]{1,0:T(8,128)(2,1)S(1)}, u32[]{:S(2)}, u32[]{:S(2)}) %collective-permute-start.15) | collective-permute-done | bytes 262176 | tf_op jit(solution)/shard_map/ppermute | solution.py:41
  94.4 1.8 %collective-permute-done.24.passed_ref = bf16[256,512]{1,0:T(8,128)(2,1)S(1)} collective-permute-done((bf16[256,512]{1,0:T(8,128)(2,1)S(1)}, bf16[256,512]{1,0:T(8,128)(2,1)S(1)}, u32[]{:S(2)}, u32[]{:S(2)}) %collective-permute-start.24) | collective-permute-done | bytes 262176 | tf_op jit(solution)/shard_map/ppermute | solution.py:41
  98.9 7.2 %all-to-all-start.2 = ((f32[32,2,512]{2,1,0:T(2,128)}), f32[32,2,512]{2,1,0:T(2,128)}, u32[]{:S(2)}, u32[]{:S(2)}) async-start(f32[32,2,512]{2,1,0:T(2,128)} %broadcast_in_dim.34), calls=%async_computation.2 | async-start | bytes 262144 | tf_op jit(solution)/shard_map/all_to_all | solution.py:63
  106.2 1.8 %collective-permute-start.18 = (f32[2,1536]{1,0:T(2,128)S(1)}, f32[2,1536]{1,0:T(2,128)S(1)}, u32[]{:S(2)}, u32[]{:S(2)}) collective-permute-start(f32[2,1536]{1,0:T(2,128)S(1)} %fusion.3), channel_id=1, source_target_pairs={{0,1},{1,0},{2,3},{3,2},{4,5},{5,4},{6,7},{7,6},{8,9},{9,8},{10,11... | collective-permute-start | bytes 36872 | tf_op jit(solution)/shard_map/ppermute | solution.py:55
  107.9 2.0 %collective-permute-done.18 = f32[2,1536]{1,0:T(2,128)S(1)} collective-permute-done((f32[2,1536]{1,0:T(2,128)S(1)}, f32[2,1536]{1,0:T(2,128)S(1)}, u32[]{:S(2)}, u32[]{:S(2)}) %collective-permute-start.18) | collective-permute-done | bytes 12320 | tf_op jit(solution)/shard_map/ppermute | solution.py:55
  110.0 1.8 %collective-permute-start.19 = (f32[2,1536]{1,0:T(2,128)S(1)}, f32[2,1536]{1,0:T(2,128)S(1)}, u32[]{:S(2)}, u32[]{:S(2)}) collective-permute-start(f32[2,1536]{1,0:T(2,128)S(1)} %add.34), channel_id=1, source_target_pairs={{0,2},{1,3},{2,0},{3,1},{4,6},{5,7},{6,4},{7,5},{8,10},{9,11},{10,... | collective-permute-start | bytes 36872 | tf_op jit(solution)/shard_map/ppermute | solution.py:55
  111.7 2.0 %collective-permute-done.19 = f32[2,1536]{1,0:T(2,128)S(1)} collective-permute-done((f32[2,1536]{1,0:T(2,128)S(1)}, f32[2,1536]{1,0:T(2,128)S(1)}, u32[]{:S(2)}, u32[]{:S(2)}) %collective-permute-start.19) | collective-permute-done | bytes 12320 | tf_op jit(solution)/shard_map/ppermute | solution.py:55
  113.7 2.7 %collective-permute-start.20 = (f32[2,1536]{1,0:T(2,128)S(1)}, f32[2,1536]{1,0:T(2,128)S(1)}, u32[]{:S(2)}, u32[]{:S(2)}) collective-permute-start(f32[2,1536]{1,0:T(2,128)S(1)} %add.35), channel_id=1, source_target_pairs={{0,4},{1,5},{2,6},{3,7},{4,0},{5,1},{6,2},{7,3},{8,12},{9,13},{10,... | collective-permute-start | bytes 36872 | tf_op jit(solution)/shard_map/ppermute | solution.py:55
  116.4 2.0 %collective-permute-done.20 = f32[2,1536]{1,0:T(2,128)S(1)} collective-permute-done((f32[2,1536]{1,0:T(2,128)S(1)}, f32[2,1536]{1,0:T(2,128)S(1)}, u32[]{:S(2)}, u32[]{:S(2)}) %collective-permute-start.20) | collective-permute-done | bytes 12320 | tf_op jit(solution)/shard_map/ppermute | solution.py:55
  122.5 3.3 %update.1 = (f32[256,2048]{1,0:T(8,128)}, f32[256,2048]{1,0:T(8,128)}) custom-call(f32[2,1536]{1,0:T(2,128)S(1)} %add.36.sums_ref, f32[32,2,512]{2,1,0:T(2,128)} %all-to-all-done.2.last_ref, f32[256,2048]{1,0:T(8,128)S(1)} %copy-done.2, bf16[256,512]{1,0:T(8,128)(2,1)S(1)} %get-tuple-element.30.own_ref.refs_0_, ...), custom_call_target="tpu_custom_call" | custom-call | tf_op jit(solution)/shard_map/update/pallas_call | solution.py:214
  (99 shorter events, 35.4 us)
Async XLA Ops:
  4.3 14.3 %all-to-all-start = ((f32[8,8,256]{2,0,1:T(8,128)}), f32[8,8,256]{2,0,1:T(8,128)S(1)}, u32[]{:S(2)}, u32[]{:S(2)}) async-start(f32[8,8,256]{2,0,1:T(8,128)} %bitcast.1), calls=%async_computation | async-start | bytes 131072 | tf_op jit(solution)/shard_map/all_to_all | solution.py:237
  11.5 14.2 %collective-permute-start.1 = (bf16[256,512]{1,0:T(8,128)(2,1)}, bf16[256,512]{1,0:T(8,128)(2,1)}, u32[]{:S(2)}, u32[]{:S(2)}) collective-permute-start(bf16[256,512]{1,0:T(8,128)(2,1)} %get-tuple-element.27.own_ref), channel_id=1, source_target_pairs={{0,1},{1,0},{2,3},{3,2},{4,5},{5,4},{6,7},{7,6},{8,9},{9,8},{10,11... | collective-permute-start | bytes 786440 | tf_op jit(solution)/shard_map/ppermute | solution.py:35
  13.5 13.8 %collective-permute-start.8 = (bf16[256,512]{1,0:T(8,128)(2,1)S(1)}, bf16[256,512]{1,0:T(8,128)(2,1)}, u32[]{:S(2)}, u32[]{:S(2)}) collective-permute-start(bf16[256,512]{1,0:T(8,128)(2,1)S(1)} %get-tuple-element.32.own_ref), channel_id=1, source_target_pairs={{0,1},{1,0},{2,3},{3,2},{4,5},{5,4},{6,7},{7,6},{8,9},{9,8},{10,11... | collective-permute-start | bytes 786440 | tf_op jit(solution)/shard_map/ppermute | solution.py:35
  13.6 23.9 %collective-permute-start.12 = (bf16[256,512]{1,0:T(8,128)(2,1)S(1)}, bf16[256,512]{1,0:T(8,128)(2,1)}, u32[]{:S(2)}, u32[]{:S(2)}) collective-permute-start(bf16[256,512]{1,0:T(8,128)(2,1)S(1)} %get-tuple-element.36.own_ref), channel_id=1, source_target_pairs={{0,1},{1,0},{2,3},{3,2},{4,5},{5,4},{6,7},{7,6},{8,9},{9,8},{10,11... | collective-permute-start | bytes 786440 | tf_op jit(solution)/shard_map/ppermute | solution.py:35
  20.1 4.3 %collective-permute-start.4 = (f32[64,256]{1,0:T(8,128)S(1)}, f32[64,256]{1,0:T(8,128)S(1)}, u32[]{:S(2)}, u32[]{:S(2)}) collective-permute-start(f32[64,256]{1,0:T(8,128)S(1)} %add.29), channel_id=1, source_target_pairs={{0,16},{8,24},{16,0},{24,8},{1,17},{9,25},{17,1},{25,9},{2,18},{10... | collective-permute-start | bytes 196616 | tf_op jit(solution)/shard_map/ppermute | solution.py:55
  21.7 23.5 %collective-permute-start.21 = (bf16[256,512]{1,0:T(8,128)(2,1)S(1)}, bf16[256,512]{1,0:T(8,128)(2,1)}, u32[]{:S(2)}, u32[]{:S(2)}) collective-permute-start(bf16[256,512]{1,0:T(8,128)(2,1)S(1)} %get-tuple-element.40.own_ref), channel_id=1, source_target_pairs={{0,1},{1,0},{2,3},{3,2},{4,5},{5,4},{6,7},{7,6},{8,9},{9,8},{10,11... | collective-permute-start | bytes 786440 | tf_op jit(solution)/shard_map/ppermute | solution.py:35
  24.4 22.8 %collective-permute-start = (bf16[256,512]{1,0:T(8,128)(2,1)}, bf16[256,512]{1,0:T(8,128)(2,1)S(1)}, u32[]{:S(2)}, u32[]{:S(2)}) collective-permute-start(bf16[256,512]{1,0:T(8,128)(2,1)} %get-tuple-element.26), channel_id=1, source_target_pairs={{0,7},{1,0},{2,1},{3,2},{4,3},{5,4},{6,5},{7,6},{8,15},{9,8},{10,9... | collective-permute-start | bytes 786440 | tf_op jit(solution)/shard_map/ppermute | solution.py:46
  25.8 31.4 %collective-permute-start.2 = (bf16[256,512]{1,0:T(8,128)(2,1)}, bf16[256,512]{1,0:T(8,128)(2,1)}, u32[]{:S(2)}, u32[]{:S(2)}) collective-permute-start(bf16[256,512]{1,0:T(8,128)(2,1)} %collective-permute-done.1.swapped_ref), channel_id=1, source_target_pairs={{0,2},{1,7},{2,4},{3,1},{4,6},{5,3},{6,0},{7,5},{8,10},{9,15},{10,... | collective-permute-start | bytes 786440 | tf_op jit(solution)/shard_map/ppermute | solution.py:41
  27.3 33.0 %collective-permute-start.9 = (bf16[256,512]{1,0:T(8,128)(2,1)}, bf16[256,512]{1,0:T(8,128)(2,1)}, u32[]{:S(2)}, u32[]{:S(2)}) collective-permute-start(bf16[256,512]{1,0:T(8,128)(2,1)} %collective-permute-done.8.swapped_ref), channel_id=1, source_target_pairs={{0,2},{1,7},{2,4},{3,1},{4,6},{5,3},{6,0},{7,5},{8,10},{9,15},{10,... | collective-permute-start | bytes 786440 | tf_op jit(solution)/shard_map/ppermute | solution.py:41
  37.5 25.1 %collective-permute-start.13 = (bf16[256,512]{1,0:T(8,128)(2,1)}, bf16[256,512]{1,0:T(8,128)(2,1)}, u32[]{:S(2)}, u32[]{:S(2)}) collective-permute-start(bf16[256,512]{1,0:T(8,128)(2,1)} %collective-permute-done.12.swapped_ref), channel_id=1, source_target_pairs={{0,2},{1,7},{2,4},{3,1},{4,6},{5,3},{6,0},{7,5},{8,10},{9,15},{10,... | collective-permute-start | bytes 786440 | tf_op jit(solution)/shard_map/ppermute | solution.py:41
  39.6 17.6 %all-to-all-start.1 = ((f32[8,8,256]{2,1,0:T(8,128)}), f32[8,8,256]{2,1,0:T(8,128)S(1)}, u32[]{:S(2)}, u32[]{:S(2)}) async-start(f32[8,8,256]{2,1,0:T(8,128)} %add_bitcast_fusion), calls=%async_computation.1 | async-start | bytes 131072 | tf_op jit(solution)/shard_map/all_to_all | solution.py:240
  45.1 20.5 %collective-permute-start.22 = (bf16[256,512]{1,0:T(8,128)(2,1)}, bf16[256,512]{1,0:T(8,128)(2,1)}, u32[]{:S(2)}, u32[]{:S(2)}) collective-permute-start(bf16[256,512]{1,0:T(8,128)(2,1)} %collective-permute-done.21.swapped_ref), channel_id=1, source_target_pairs={{0,2},{1,7},{2,4},{3,1},{4,6},{5,3},{6,0},{7,5},{8,10},{9,15},{10,... | collective-permute-start | bytes 786440 | tf_op jit(solution)/shard_map/ppermute | solution.py:41
  58.8 9.3 %collective-permute-start.6 = (bf16[256,512]{1,0:T(8,128)(2,1)S(1)}, bf16[256,512]{1,0:T(8,128)(2,1)S(1)}, u32[]{:S(2)}, u32[]{:S(2)}) collective-permute-start(bf16[256,512]{1,0:T(8,128)(2,1)S(1)} %get-tuple-element.30.own_ref.refs_0_), channel_id=1, source_target_pairs={{0,1},{1,0},{2,3},{3,2},{4,5},{5,4},{6,7},{7,6},{8,9},{9,8},{10,11... | collective-permute-start | bytes 786440 | tf_op jit(solution)/shard_map/ppermute | solution.py:35
  61.9 14.6 %collective-permute-start.10 = (bf16[256,512]{1,0:T(8,128)(2,1)S(1)}, bf16[256,512]{1,0:T(8,128)(2,1)S(1)}, u32[]{:S(2)}, u32[]{:S(2)}) collective-permute-start(bf16[256,512]{1,0:T(8,128)(2,1)S(1)} %get-tuple-element.34.own_ref.refs_1_), channel_id=1, source_target_pairs={{0,1},{1,0},{2,3},{3,2},{4,5},{5,4},{6,7},{7,6},{8,9},{9,8},{10,11... | collective-permute-start | bytes 786440 | tf_op jit(solution)/shard_map/ppermute | solution.py:35
  64.2 18.2 %collective-permute-start.14 = (bf16[256,512]{1,0:T(8,128)(2,1)S(1)}, bf16[256,512]{1,0:T(8,128)(2,1)S(1)}, u32[]{:S(2)}, u32[]{:S(2)}) collective-permute-start(bf16[256,512]{1,0:T(8,128)(2,1)S(1)} %get-tuple-element.38.own_ref.refs_2_), channel_id=1, source_target_pairs={{0,1},{1,0},{2,3},{3,2},{4,5},{5,4},{6,7},{7,6},{8,9},{9,8},{10,11... | collective-permute-start | bytes 786440 | tf_op jit(solution)/shard_map/ppermute | solution.py:35
  67.3 18.5 %collective-permute-start.23 = (bf16[256,512]{1,0:T(8,128)(2,1)S(1)}, bf16[256,512]{1,0:T(8,128)(2,1)S(1)}, u32[]{:S(2)}, u32[]{:S(2)}) collective-permute-start(bf16[256,512]{1,0:T(8,128)(2,1)S(1)} %get-tuple-element.42.own_ref.refs_3_), channel_id=1, source_target_pairs={{0,1},{1,0},{2,3},{3,2},{4,5},{5,4},{6,7},{7,6},{8,9},{9,8},{10,11... | collective-permute-start | bytes 786440 | tf_op jit(solution)/shard_map/ppermute | solution.py:35
  68.0 21.5 %collective-permute-start.5 = (bf16[256,512]{1,0:T(8,128)(2,1)S(1)}, bf16[256,512]{1,0:T(8,128)(2,1)S(1)}, u32[]{:S(2)}, u32[]{:S(2)}) collective-permute-start(bf16[256,512]{1,0:T(8,128)(2,1)S(1)} %slice.3), channel_id=1, source_target_pairs={{0,7},{1,0},{2,1},{3,2},{4,3},{5,4},{6,5},{7,6},{8,15},{9,8},{10,9... | collective-permute-start | bytes 786440 | tf_op jit(solution)/shard_map/ppermute | solution.py:46
  68.1 21.4 %collective-permute-start.7 = (bf16[256,512]{1,0:T(8,128)(2,1)S(1)}, bf16[256,512]{1,0:T(8,128)(2,1)S(1)}, u32[]{:S(2)}, u32[]{:S(2)}) collective-permute-start(bf16[256,512]{1,0:T(8,128)(2,1)S(1)} %collective-permute-done.6.swapped_ref), channel_id=1, source_target_pairs={{0,2},{1,7},{2,4},{3,1},{4,6},{5,3},{6,0},{7,5},{8,10},{9,15},{10,... | collective-permute-start | bytes 786440 | tf_op jit(solution)/shard_map/ppermute | solution.py:41
  76.5 13.6 %collective-permute-start.11 = (bf16[256,512]{1,0:T(8,128)(2,1)S(1)}, bf16[256,512]{1,0:T(8,128)(2,1)S(1)}, u32[]{:S(2)}, u32[]{:S(2)}) collective-permute-start(bf16[256,512]{1,0:T(8,128)(2,1)S(1)} %collective-permute-done.10.swapped_ref), channel_id=1, source_target_pairs={{0,2},{1,7},{2,4},{3,1},{4,6},{5,3},{6,0},{7,5},{8,10},{9,15},{10,... | collective-permute-start | bytes 786440 | tf_op jit(solution)/shard_map/ppermute | solution.py:41
  82.4 10.6 %collective-permute-start.15 = (bf16[256,512]{1,0:T(8,128)(2,1)S(1)}, bf16[256,512]{1,0:T(8,128)(2,1)S(1)}, u32[]{:S(2)}, u32[]{:S(2)}) collective-permute-start(bf16[256,512]{1,0:T(8,128)(2,1)S(1)} %collective-permute-done.14.swapped_ref), channel_id=1, source_target_pairs={{0,2},{1,7},{2,4},{3,1},{4,6},{5,3},{6,0},{7,5},{8,10},{9,15},{10,... | collective-permute-start | bytes 786440 | tf_op jit(solution)/shard_map/ppermute | solution.py:41
  85.8 10.4 %collective-permute-start.24 = (bf16[256,512]{1,0:T(8,128)(2,1)S(1)}, bf16[256,512]{1,0:T(8,128)(2,1)S(1)}, u32[]{:S(2)}, u32[]{:S(2)}) collective-permute-start(bf16[256,512]{1,0:T(8,128)(2,1)S(1)} %collective-permute-done.23.swapped_ref), channel_id=1, source_target_pairs={{0,2},{1,7},{2,4},{3,1},{4,6},{5,3},{6,0},{7,5},{8,10},{9,15},{10,... | collective-permute-start | bytes 786440 | tf_op jit(solution)/shard_map/ppermute | solution.py:41
  97.5 8.6 %collective-permute-start.17 = (f32[2,1536]{1,0:T(2,128)S(1)}, f32[2,1536]{1,0:T(2,128)S(1)}, u32[]{:S(2)}, u32[]{:S(2)}) collective-permute-start(f32[2,1536]{1,0:T(2,128)S(1)} %fusion.2), channel_id=1, source_target_pairs={{0,16},{8,24},{16,0},{24,8},{1,17},{9,25},{17,1},{25,9},{2,18},{10... | collective-permute-start | bytes 36872 | tf_op jit(solution)/shard_map/ppermute | solution.py:55
  98.9 19.5 %all-to-all-start.2 = ((f32[32,2,512]{2,1,0:T(2,128)}), f32[32,2,512]{2,1,0:T(2,128)}, u32[]{:S(2)}, u32[]{:S(2)}) async-start(f32[32,2,512]{2,1,0:T(2,128)} %broadcast_in_dim.34), calls=%async_computation.2 | async-start | bytes 262144 | tf_op jit(solution)/shard_map/all_to_all | solution.py:63
  113.7 4.7 %collective-permute-start.20 = (f32[2,1536]{1,0:T(2,128)S(1)}, f32[2,1536]{1,0:T(2,128)S(1)}, u32[]{:S(2)}, u32[]{:S(2)}) collective-permute-start(f32[2,1536]{1,0:T(2,128)S(1)} %add.35), channel_id=1, source_target_pairs={{0,4},{1,5},{2,6},{3,7},{4,0},{5,1},{6,2},{7,3},{8,12},{9,13},{10,... | collective-permute-start | bytes 36872 | tf_op jit(solution)/shard_map/ppermute | solution.py:55
  (25 other events, 339.1 us)

commit v2 on v1

v2 whole, which is shorter than its diff:
```python
import functools

import jax
import jax.numpy as jnp
from jax import lax
from jax.experimental import pallas as pl
from jax.experimental.pallas import tpu as pltpu
from jax.sharding import PartitionSpec as P

HIGHEST = lax.Precision.HIGHEST
VMEM = pltpu.VMEM
SMEM = pltpu.SMEM
F32 = jnp.float32
BF16 = jnp.bfloat16

EIGHTHS = (2, 2, 2, 2)
TIES = {
    "d0": ("s2",),
    "d3": ("n",),
    "e": ("s0",),
    "g": ("e", "c"),
    "h": ("m", "p1", "s1"),
    "i0": ("x1",),
    "i1": ("x2",),
    "i2": ("x3",),
    "n": ("h",),
    "s1": ("s0",),
    "s2": ("c", "s0"),
    "s3": ("m",),
    "t": ("s1",),
    "u": ("p0",),
    "x0": ("s3",),
    "y0": ("d1",),
}


def widths(columns):
    return [columns // 8 * part for part in EIGHTHS]


def starts(sizes):
    return [sum(sizes[:i]) for i in range(len(sizes))]


def params(mebibytes):
    return pltpu.CompilerParams(vmem_limit_bytes=mebibytes * 1024 * 1024)


def whole(space=VMEM):
    return pl.BlockSpec(memory_space=space)


def shape(rows, columns, dtype):
    return jax.ShapeDtypeStruct((rows, columns), dtype)


def after(value, *others):
    return lax.optimization_barrier((value,) + others)[0]


def exchange(value, axis, step):
    count = lax.axis_size(axis)
    return lax.ppermute(value, axis, [(i, i ^ step) for i in range(count)])


def pair_swap(value):
    return exchange(value, "sub", 1)


def pass_on(value):
    count = lax.axis_size("sub")
    pairs = [(j, (j + (2 if j % 2 == 0 else -2)) % count) for j in range(count)]
    return lax.ppermute(value, "sub", pairs)


def to_left(value):
    count = lax.axis_size("sub")
    return lax.ppermute(value, "sub", [(j, (j - 1) % count) for j in range(count)])


def powers(low, count):
    return [1 << b for b in range(low, count.bit_length() - 1)]


def step_length(rzs, pqs, odd):
    groups, subs = lax.axis_size("grp"), lax.axis_size("sub")
    parts = jnp.concatenate([jnp.concatenate(p, axis=1) for p in (rzs, pqs)], axis=0)
    half = parts.shape[1] // 2
    low, high = parts[:, :half], parts[:, half:]
    mine = jnp.where(odd, high, low) + exchange(jnp.where(odd, low, high), "grp", 1)
    same = [[g * subs + j for g in range(p, groups, 2) for j in range(subs)] for p in range(2)]
    copies = jnp.broadcast_to(mine[None], (len(same[0]),) + mine.shape)
    sums = lax.all_to_all(copies, ("grp", "sub"), 0, 0, axis_index_groups=same, tiled=True)
    alpha = quotient(sums)
    other = exchange(alpha, "grp", 1)
    return jnp.concatenate([jnp.where(odd, other, alpha), jnp.where(odd, alpha, other)], axis=1)


def first_kernel(place_ref, index_ref, right_ref, chunk_ref, primal_ref, face, blocks, sems):
    rank = primal_ref.shape[0]
    size = chunk_ref.shape[1]
    copies = [pltpu.make_async_copy(right_ref.at[:, :size], face, sems.at[rank])]
    for k in range(rank):
        begin = pl.multiple_of((index_ref[0, k] >> 3) << 3, 8)
        source = right_ref.at[pl.ds(begin, 8), :]
        copies.append(pltpu.make_async_copy(source, blocks.at[k], sems.at[k]))
    for copy in copies:
        copy.start()
    copies[0].wait()
    chunk_ref[...] = face[...].astype(BF16)
    for k in range(rank):
        copies[k + 1].wait()
        primal_ref[k : k + 1, :] = blocks[k, pl.ds(index_ref[0, k] & 7, 1), :]


def first_chunk(place, right_side, primal_index, size):
    rows, columns = right_side.shape
    rank = primal_index.shape[1]
    return pl.pallas_call(
        first_kernel,
        out_shape=[shape(rows, size, BF16), shape(rank, columns, F32)],
        in_specs=[whole(SMEM), whole(SMEM), whole(pl.ANY)],
        out_specs=[whole(), whole()],
        scratch_shapes=[
            pltpu.VMEM((rows, size), F32),
            pltpu.VMEM((rank, 8, columns), F32),
            pltpu.SemaphoreType.DMA((rank + 1,)),
        ],
        compiler_params=params(8),
        name="first",
    )(place, primal_index, pltpu.with_memory_space_constraint(right_side, pltpu.HBM))


def split_kernel(sizes, right_ref, after_ref, *chunk_refs):
    for begin, size, chunk_ref in zip(starts(sizes)[1:], sizes[1:], chunk_refs):
        chunk_ref[...] = right_ref[:, begin : begin + size].astype(BF16)


def split(right_side, first, sizes):
    rows = right_side.shape[0]
    outs = [shape(rows, size, BF16) for size in sizes[1:]]
    out = pl.pallas_call(
        functools.partial(split_kernel, sizes),
        out_shape=outs,
        in_specs=[whole(), whole(pl.ANY)],
        out_specs=[whole()] * len(outs),
        compiler_params=params(8),
        name="split",
    )(right_side, first)
    return [first] + list(out)


def gram_kernel(factor_ref, upper_ref, lower_ref):
    half = upper_ref.shape[0]
    dims = (((0,), (0,)), ((), ()))
    factor = factor_ref[...]
    product = lax.dot_general(factor, factor, dims, preferred_element_type=F32)
    upper_ref[...] = product[:half].astype(BF16)
    lower_ref[...] = product[half:].astype(BF16)


def gram(factor):
    size = factor.shape[0]
    out = shape(size // 2, size, BF16)
    return pl.pallas_call(
        gram_kernel,
        out_shape=[out, out],
        in_specs=[whole()],
        out_specs=[whole(), whole()],
        compiler_params=params(8),
        name="gram",
    )(factor)


def solve_kernel(masks, place_ref, matrix_ref, *refs):
    pieces, (own_ref, partner_ref, sorted_ref, rows_ref) = refs[: len(masks)], refs[len(masks) :]
    rank = own_ref.shape[0]
    position = place_ref[2]
    sorted_ref[...] = jnp.zeros_like(sorted_ref)
    for mask, piece in zip(masks, pieces):
        begin = pl.multiple_of((position ^ mask) * rank, rank)
        sorted_ref[pl.ds(begin, rank), :] = piece[...]
    for k, target in enumerate((position, position ^ 1)):
        rows = pl.ds(pl.multiple_of(target * rank, rank), rank)
        rows_ref[k * rank : (k + 1) * rank, :] = matrix_ref[rows, :]
    both = jnp.dot(
        rows_ref[...], sorted_ref[...], precision=HIGHEST, preferred_element_type=F32
    )
    own_ref[...] = both[:rank]
    partner_ref[...] = both[rank:]


def solve(place, matrix, pieces, masks):
    rank, columns = pieces[0].shape
    out = shape(rank, columns, F32)
    return pl.pallas_call(
        functools.partial(solve_kernel, masks),
        out_shape=[out, out],
        in_specs=[whole(SMEM)] + [whole()] * (1 + len(pieces)),
        out_specs=[whole(), whole()],
        scratch_shapes=[
            pltpu.VMEM((matrix.shape[1], columns), F32),
            pltpu.VMEM((2 * rank, matrix.shape[1]), F32),
        ],
        compiler_params=params(8),
        name="solve",
    )(place, matrix, *pieces)


def stencil(parity, low, up, swapped, own, passed):
    half = low.shape[0]
    even = parity == 0
    for_swapped = jnp.where(even, up[:, half:], low[:, :half])
    for_passed = jnp.where(even, low[:, :half], up[:, half:])
    dot = functools.partial(jnp.dot, preferred_element_type=F32)
    total = dot(low[:, half:], own) + dot(up[:, :half], own)
    total = total + dot(for_swapped, swapped)
    return total + dot(for_passed, passed)


def direction_kernel(
    cols, place_ref, index_ref, low_ref, up_ref, swapped_ref, own_ref, passed_ref, right_ref,
    corr_ref, dir_ref, rz_ref, full_ref,
):
    full_ref[...] = 0.5 * stencil(
        place_ref[0], low_ref[...], up_ref[...], swapped_ref[...], own_ref[...], passed_ref[...]
    )
    for k in range(corr_ref.shape[0]):
        row = pl.ds(index_ref[0, k], 1)
        full_ref[row, :] = full_ref[row, :] + corr_ref[k : k + 1, cols]
    full = full_ref[...]
    dir_ref[...] = full.astype(BF16)
    rz_ref[...] = jnp.sum(right_ref[:, cols] * full, axis=0, keepdims=True)


def direction_chunk(place, index, low, up, swapped, own, passed, right_side, corr, begin):
    rows, size = own.shape
    return pl.pallas_call(
        functools.partial(direction_kernel, slice(begin, begin + size)),
        out_shape=[shape(rows, size, BF16), shape(1, size, F32)],
        in_specs=[whole(SMEM)] * 2 + [whole()] * 7,
        out_specs=[whole(), whole()],
        scratch_shapes=[pltpu.VMEM((rows, size), F32)],
        compiler_params=params(12),
        name="direction",
    )(place, index, low, up, swapped, own, passed, right_side, corr)


def image_kernel(
    place_ref, panel_ref, up_ref, swapped_ref, own_ref, passed_ref, coef_ref, q_ref, pq_ref
):
    own = own_ref[...]
    half = own.shape[0]
    total = stencil(
        place_ref[0], panel_ref[half:, :], up_ref[...], swapped_ref[...], own, passed_ref[...]
    )
    own_f = own.astype(F32)
    q = total + coef_ref[:, :1] * own_f
    q_ref[...] = q
    pq_ref[...] = jnp.sum(own_f * q, axis=0, keepdims=True)


def image_chunk(place, schur, up, swapped, own, passed, coef):
    rows, size = own.shape
    return pl.pallas_call(
        image_kernel,
        out_shape=[pltpu.VMEM((rows, size), F32), shape(1, size, F32)],
        in_specs=[whole(SMEM)] + [whole()] * 6,
        out_specs=[whole(), whole()],
        compiler_params=params(12),
        name="image",
    )(place, schur, up, swapped, own, passed, coef)


def quotient_kernel(sums_ref, alpha_ref):
    sums = jnp.sum(sums_ref[...], axis=0)
    alpha_ref[...] = sums[0:1] / sums[1:2]


def quotient(sums):
    return pl.pallas_call(
        quotient_kernel,
        out_shape=shape(1, sums.shape[2], F32),
        in_specs=[whole()],
        out_specs=whole(),
        compiler_params=params(8),
        name="quotient",
    )(sums)


def update_kernel(sizes, alpha_ref, right_ref, *refs):
    count = len(sizes)
    dirs, qs = refs[:count], refs[count : 2 * count]
    solution_ref, residual_ref, solution_buf, residual_buf, sems = refs[2 * count :]
    copies = []
    for i, (begin, size) in enumerate(zip(starts(sizes), sizes)):
        cols = slice(begin, begin + size)
        alpha = alpha_ref[:, cols]
        solution_buf[:, cols] = alpha * dirs[i][...].astype(F32)
        residual_buf[:, cols] = right_ref[:, cols] - alpha * qs[i][...]
        for k, (buf, ref) in enumerate(
            ((solution_buf, solution_ref), (residual_buf, residual_ref))
        ):
            copy = pltpu.make_async_copy(buf.at[:, cols], ref.at[:, cols], sems.at[2 * i + k])
            copy.start()
            copies.append(copy)
    for copy in copies:
        copy.wait()


def update(alpha, right_side, dirs, qs, sizes):
    rows, columns = right_side.shape
    out = shape(rows, columns, F32)
    return pl.pallas_call(
        functools.partial(update_kernel, sizes),
        out_shape=[out, out],
        in_specs=[whole()] * (2 + 2 * len(sizes)),
        out_specs=[whole(pl.ANY)] * 2,
        scratch_shapes=[pltpu.VMEM((rows, columns), F32)] * 2
        + [pltpu.SemaphoreType.DMA((2 * len(sizes),))],
        compiler_params=params(12),
        name="update",
    )(alpha, right_side, *dirs, *qs)


def body(right_side, schur, inv_factor, coarse_inverse, primal_index, phase, phase_coef):
    face_rows, columns = right_side.shape
    sizes = widths(columns)
    begins = starts(sizes)
    chunks = range(len(sizes))
    subs, groups = lax.axis_size("sub"), lax.axis_size("grp")
    rank = primal_index.shape[1]
    position, group = lax.axis_index("sub"), lax.axis_index("grp")
    place = jnp.stack([position % 2, group % 2, position]).astype(jnp.int32)
    place = lax.optimization_barrier(place)

    known = {}

    def get(name):
        if name not in known:
            known[name] = None
            known[name] = made[name[0]](*([int(name[1:])] if name[1:] else []))
        assert known[name] is not None
        return known[name]

    def tied(name, value):
        others = [get(other) for other in TIES.get(name, ())]
        return after(value, *others) if others else value

    primal_index = pltpu.with_memory_space_constraint(primal_index, pltpu.HBM)
    first, own_primal = first_chunk(place, right_side, primal_index, sizes[0])
    resid = split(right_side, first, sizes)

    masks = range(0, subs, 2)
    def gather(i):
        return exchange(tied(f"a{i}", own_primal), "sub", masks[i])

    def solved():
        pieces = [tied("e", own_primal)] + [get(f"a{i}") for i in range(1, len(masks))]
        return solve(place, coarse_inverse, pieces, masks)

    def coarse():
        own, partner = get("e")
        return own + pair_swap(tied("c", partner))

    def total():
        value = tied("t", get("c"))
        for step in powers(0, groups):
            value = value + exchange(value, "grp", step)
            if step == 1:
                value = tied("u", value)
        return get("c") + value / groups

    def direction(i):
        own = tied(f"d{i}", resid[i])
        if i:
            own = after(own, get(f"d{i - 1}")[0])
        return direction_chunk(
            place, primal_index, get("g")[1], get("m"), get(f"s{i}"), own, get(f"p{i}"), right_side,
            get("h"), begins[i],
        )

    def coefficients():
        labels = jnp.arange(phase_coef.shape[0], dtype=jnp.int32)
        coef = jnp.sum(
            jnp.where(phase[:, None] == labels[None, :], phase_coef[None, :], 0.0), axis=1
        )
        return jnp.broadcast_to(coef[:, None], (face_rows, 128))

    def image(i):
        own = tied(f"i{i}", get(f"d{i}")[0])
        if i:
            own = after(own, get(f"i{i - 1}")[1])
        return image_chunk(
            place, schur, get("n"), get(f"x{i}"), own, get(f"y{i}"), get("k")
        )

    made = {
        "a": gather,
        "s": lambda i: pair_swap(tied(f"s{i}", resid[i])),
        "p": lambda i: pass_on(tied(f"p{i}", get(f"s{i}"))),
        "g": lambda: gram(tied("g", inv_factor)),
        "m": lambda: to_left(get("g")[0]),
        "n": lambda: to_left(tied("n", schur)[:face_rows]),
        "e": solved,
        "c": coarse,
        "h": lambda: tied("h", total()),
        "d": direction,
        "x": lambda i: pair_swap(tied(f"x{i}", get(f"d{i}")[0])),
        "y": lambda i: pass_on(tied(f"y{i}", get(f"x{i}"))),
        "k": coefficients,
        "i": image,
    }
    images = [get(f"i{i}") for i in chunks]
    dirs = [get(f"d{i}") for i in chunks]
    alpha = step_length([d[1] for d in dirs], [i[1] for i in images], place[1] == 1)
    return update(alpha, right_side, [d[0] for d in dirs], [i[0] for i in images], sizes)


def solution(mesh):
    in_specs = (
        P(("grp", "sub"), None),
        P(("grp", "sub"), None),
        P(("grp", "sub"), None),
        P("grp", None),
        P(("grp", "sub"), None),
        P(("grp", "sub")),
        P(),
    )
    out_specs = (P(("grp", "sub"), None), P(("grp", "sub"), None))
    return jax.shard_map(body, mesh=mesh, in_specs=in_specs, out_specs=out_specs, check_vma=False)
```

time: 126 us -> 100 us (0.79)
  starting transfers between devices: 51.8 us -> 29.5 us
  blocking collectives: 0 us -> 11.7 us
  local copies, waits for them, and re-layouts: 10.6 us -> 0.75 us
  waiting for transfers between devices: 47.4 us -> 41.9 us
    all_to_all x3 -> x0, starting transfers between devices: 20.1 us -> none  [the longest x1 7.25 us: body(): group_primal = lax.all_to_all(own_primal, 'sub', 1, 0, tiled=True)]
    all_to_all x3 -> x0, waiting for transfers between devices: 12.9 us -> none  [the longest x1 9.96 us: body(): correction = lax.all_to_all(solved + mean, 'sub', 0, 1, tiled=True)]
    all_to_all x0 -> x1, blocking collectives: none -> 11.7 us  [step_length(): lax.all_to_all(copies, ('grp', 'sub'), 0, 0, axis_index_groups=same, tile...]
    ppermute x8, waiting for transfers between devices: 3.48 us -> 13.9 us  [pass_on(): return lax.ppermute(value, 'sub', pairs)]
    unnamed x42 -> x12, local copies, waits for them, and re-layouts: 9.78 us -> 0.03 us
    ppermute x8, starting transfers between devices: 13 us -> 5.99 us  [pass_on(): return lax.ppermute(value, 'sub', pairs)]
    ppermute x2, starting transfers between devices: 1.42 us -> 6.36 us  [to_left(): lax.ppermute(value, 'sub', [(j, (j - 1) % count) for j in range(count)])]
    pallas_call x8 -> x11, Pallas kernels: 8.33 us -> 11.9 us  [the longest x4 4.85 us: direction_chunk(): pl.pallas_call(functools.partial(direction_kernel, slice(begin, begin + s...]
  transfers between devices with their start and end apart: 28 -> 26, of which waited for: 14 -> 17; matrix products, arithmetic and copies ran while one was open for 1% -> 1% of each run, Pallas kernels for 7% -> 9%
where the time goes in v2:
time: 100 us
  waiting for transfers between devices  41.9 us (42%)
  starting transfers between devices  29.5 us (30%)
  Pallas kernels  14.6 us (15%)
  blocking collectives  11.7 us (12%)
  between operations  1.57 us (2%)
    ppermute x16, waiting for transfers between devices, exchange(): return lax.ppermute(value, axis, [(i, i ^ step) for i in range(count)])  26.4 us
    ppermute x16, starting transfers between devices, exchange(): return lax.ppermute(value, axis, [(i, i ^ step) for i in range(count)])  17.1 us
    ppermute x8, waiting for transfers between devices, pass_on(): return lax.ppermute(value, 'sub', pairs)  13.9 us
    all_to_all x1, blocking collectives, step_length(): lax.all_to_all(copies, ('grp', 'sub'), 0, 0, axis_index_groups=same, tile...  11.7 us
    ppermute x2, starting transfers between devices, to_left(): lax.ppermute(value, 'sub', [(j, (j - 1) % count) for j in range(count)])  6.36 us
    ppermute x8, starting transfers between devices, pass_on(): return lax.ppermute(value, 'sub', pairs)  5.99 us
    pallas_call x4, Pallas kernels, direction_chunk(): pl.pallas_call(functools.partial(direction_kernel, slice(begin, begin + s...  4.85 us
    pallas_call x4, Pallas kernels, image_chunk(): pl.pallas_call(image_kernel, out_shape=[pltpu.VMEM((rows, size), F32), sh...  4.05 us
  transfers between devices with their start and end apart: 26, of which 17 were waited for; matrix products, arithmetic and copies ran while one was open for 1% of the time, Pallas kernels for 9%

profile of v2, /device:TPU:0, one launch (start us, length us, event | category | flops | bytes accessed | tf_op | source)
XLA Modules:
  0.0 100.2 jit_solution(12668109884524461636)
XLA Ops:
  0.7 2.0 %first.1 = (bf16[256,512]{1,0:T(8,128)(2,1)S(1)}, f32[8,2048]{1,0:T(8,128)S(1)}) custom-call(s32[3]{0:T(128)S(1)} %pad_add_fusion.place_ref, s32[1,8]{1,0:T(1,128)} %index_ref.9, f32[256,2048]{1,0:T(8,128)} %right_ref.13), custom_call_target="tpu_custom_call" | custom-call | tf_op jit(solution)/shard_map/first/pallas_call | solution.py:119
  2.8 3.0 %collective-permute-start = (bf16[256,512]{1,0:T(8,128)(2,1)S(1)}, bf16[256,512]{1,0:T(8,128)(2,1)S(1)}, u32[]{:S(2)}, u32[]{:S(2)}) collective-permute-start(bf16[256,512]{1,0:T(8,128)(2,1)S(1)} %get-tuple-element.59.after_ref.own_ref), channel_id=1, source_target_pairs={{0,1},{1,0},{2,3},{3,2},{4,5},{5,4},{6,7},{7,6},{8,9},{9,8},{10,11... | collective-permute-start | bytes 786440 | tf_op jit(solution)/shard_map/ppermute | solution.py:63
  5.8 3.6 %collective-permute-start.3 = (f32[8,2048]{1,0:T(8,128)S(1)}, f32[8,2048]{1,0:T(8,128)S(1)}, u32[]{:S(2)}, u32[]{:S(2)}) collective-permute-start(f32[8,2048]{1,0:T(8,128)S(1)} %get-tuple-element.51.refs_0_), channel_id=1, source_target_pairs={{0,6},{1,7},{2,4},{3,5},{4,2},{5,3},{6,0},{7,1},{8,14},{9,15},{10,... | collective-permute-start | bytes 196616 | tf_op jit(solution)/shard_map/ppermute | solution.py:63
  10.3 1.9 %collective-permute-done.swapped_ref = bf16[256,512]{1,0:T(8,128)(2,1)S(1)} collective-permute-done((bf16[256,512]{1,0:T(8,128)(2,1)S(1)}, bf16[256,512]{1,0:T(8,128)(2,1)S(1)}, u32[]{:S(2)}, u32[]{:S(2)}) %collective-permute-start) | collective-permute-done | bytes 262176 | tf_op jit(solution)/shard_map/ppermute | solution.py:63
  12.2 1.7 %collective-permute-start.8 = (bf16[256,512]{1,0:T(8,128)(2,1)S(1)}, bf16[256,512]{1,0:T(8,128)(2,1)S(1)}, u32[]{:S(2)}, u32[]{:S(2)}) collective-permute-start(bf16[256,512]{1,0:T(8,128)(2,1)S(1)} %get-tuple-element.67.own_ref), channel_id=1, source_target_pairs={{0,1},{1,0},{2,3},{3,2},{4,5},{5,4},{6,7},{7,6},{8,9},{9,8},{10,11... | collective-permute-start | bytes 786440 | tf_op jit(solution)/shard_map/ppermute | solution.py:63
  17.3 3.9 %collective-permute-done.4 = f32[8,2048]{1,0:T(8,128)S(1)} collective-permute-done((f32[8,2048]{1,0:T(8,128)S(1)}, f32[8,2048]{1,0:T(8,128)S(1)}, u32[]{:S(2)}, u32[]{:S(2)}) %collective-permute-start.4) | collective-permute-done | bytes 65568 | tf_op jit(solution)/shard_map/ppermute | solution.py:63
  21.7 4.3 %collective-permute-start.5 = (bf16[256,512]{1,0:T(8,128)(2,1)S(1)}, bf16[256,512]{1,0:T(8,128)(2,1)S(1)}, u32[]{:S(2)}, u32[]{:S(2)}) collective-permute-start(bf16[256,512]{1,0:T(8,128)(2,1)S(1)} %get-tuple-element.56), channel_id=1, source_target_pairs={{0,7},{1,0},{2,1},{3,2},{4,3},{5,4},{6,5},{7,6},{8,15},{9,8},{10,9... | collective-permute-start | bytes 786440 | tf_op jit(solution)/shard_map/ppermute | solution.py:78
  27.3 1.6 %collective-permute-start.10 = (f32[8,2048]{1,0:T(8,128)S(1)}, f32[8,2048]{1,0:T(8,128)S(1)}, u32[]{:S(2)}, u32[]{:S(2)}) collective-permute-start(f32[8,2048]{1,0:T(8,128)S(1)} %add.25), channel_id=1, source_target_pairs={{0,16},{8,24},{16,0},{24,8},{1,17},{9,25},{17,1},{25,9},{2,18},{10... | collective-permute-start | bytes 196616 | tf_op jit(solution)/shard_map/ppermute | solution.py:63
  28.9 1.6 %collective-permute-done.5.up_ref = bf16[256,512]{1,0:T(8,128)(2,1)S(1)} collective-permute-done((bf16[256,512]{1,0:T(8,128)(2,1)S(1)}, bf16[256,512]{1,0:T(8,128)(2,1)S(1)}, u32[]{:S(2)}, u32[]{:S(2)}) %collective-permute-start.5) | collective-permute-done | bytes 262176 | tf_op jit(solution)/shard_map/ppermute | solution.py:78
  30.5 2.1 %collective-permute-start.13 = (bf16[256,512]{1,0:T(8,128)(2,1)S(1)}, bf16[256,512]{1,0:T(8,128)(2,1)S(1)}, u32[]{:S(2)}, u32[]{:S(2)}) collective-permute-start(bf16[256,512]{1,0:T(8,128)(2,1)S(1)} %get-tuple-element.77.own_ref), channel_id=1, source_target_pairs={{0,1},{1,0},{2,3},{3,2},{4,5},{5,4},{6,7},{7,6},{8,9},{9,8},{10,11... | collective-permute-start | bytes 786440 | tf_op jit(solution)/shard_map/ppermute | solution.py:63
  32.6 3.2 %collective-permute-done.6.swapped_ref = bf16[256,512]{1,0:T(8,128)(2,1)S(1)} collective-permute-done((bf16[256,512]{1,0:T(8,128)(2,1)S(1)}, bf16[256,512]{1,0:T(8,128)(2,1)S(1)}, u32[]{:S(2)}, u32[]{:S(2)}) %collective-permute-start.6) | collective-permute-done | bytes 262176 | tf_op jit(solution)/shard_map/ppermute | solution.py:63
  36.7 2.1 %collective-permute-done.11.passed_ref = bf16[256,512]{1,0:T(8,128)(2,1)S(1)} collective-permute-done((bf16[256,512]{1,0:T(8,128)(2,1)S(1)}, bf16[256,512]{1,0:T(8,128)(2,1)S(1)}, u32[]{:S(2)}, u32[]{:S(2)}) %collective-permute-start.11) | collective-permute-done | bytes 262176 | tf_op jit(solution)/shard_map/ppermute | solution.py:73
  38.8 2.0 %collective-permute-start.14 = (bf16[256,512]{1,0:T(8,128)(2,1)S(1)}, bf16[256,512]{1,0:T(8,128)(2,1)S(1)}, u32[]{:S(2)}, u32[]{:S(2)}) collective-permute-start(bf16[256,512]{1,0:T(8,128)(2,1)S(1)} %slice.13), channel_id=1, source_target_pairs={{0,7},{1,0},{2,1},{3,2},{4,3},{5,4},{6,5},{7,6},{8,15},{9,8},{10,9... | collective-permute-start | bytes 786440 | tf_op jit(solution)/shard_map/ppermute | solution.py:78
  41.0 1.9 %collective-permute-start.15 = (bf16[256,512]{1,0:T(8,128)(2,1)S(1)}, bf16[256,512]{1,0:T(8,128)(2,1)S(1)}, u32[]{:S(2)}, u32[]{:S(2)}) collective-permute-start(bf16[256,512]{1,0:T(8,128)(2,1)S(1)} %collective-permute-done.13.swapped_ref), channel_id=1, source_target_pairs={{0,2},{1,7},{2,4},{3,1},{4,6},{5,3},{6,0},{7,5},{8,10},{9,15},{10,... | collective-permute-start | bytes 786440 | tf_op jit(solution)/shard_map/ppermute | solution.py:73
  44.1 1.5 %collective-permute-start.16 = (bf16[256,512]{1,0:T(8,128)(2,1)S(1)}, bf16[256,512]{1,0:T(8,128)(2,1)S(1)}, u32[]{:S(2)}, u32[]{:S(2)}) collective-permute-start(bf16[256,512]{1,0:T(8,128)(2,1)S(1)} %get-tuple-element.80.own_ref.refs_0_), channel_id=1, source_target_pairs={{0,1},{1,0},{2,3},{3,2},{4,5},{5,4},{6,7},{7,6},{8,9},{9,8},{10,11... | collective-permute-start | bytes 786440 | tf_op jit(solution)/shard_map/ppermute | solution.py:63
  48.7 1.5 %collective-permute-start.19 = (bf16[256,512]{1,0:T(8,128)(2,1)S(1)}, bf16[256,512]{1,0:T(8,128)(2,1)S(1)}, u32[]{:S(2)}, u32[]{:S(2)}) collective-permute-start(bf16[256,512]{1,0:T(8,128)(2,1)S(1)} %get-tuple-element.88.own_ref.refs_2_), channel_id=1, source_target_pairs={{0,1},{1,0},{2,3},{3,2},{4,5},{5,4},{6,7},{7,6},{8,9},{9,8},{10,11... | collective-permute-start | bytes 786440 | tf_op jit(solution)/shard_map/ppermute | solution.py:63
  50.2 6.0 %collective-permute-done.15.passed_ref = bf16[256,512]{1,0:T(8,128)(2,1)S(1)} collective-permute-done((bf16[256,512]{1,0:T(8,128)(2,1)S(1)}, bf16[256,512]{1,0:T(8,128)(2,1)S(1)}, u32[]{:S(2)}, u32[]{:S(2)}) %collective-permute-start.15) | collective-permute-done | bytes 262176 | tf_op jit(solution)/shard_map/ppermute | solution.py:73
  57.6 3.3 %collective-permute-done.17.swapped_ref = bf16[256,512]{1,0:T(8,128)(2,1)S(1)} collective-permute-done((bf16[256,512]{1,0:T(8,128)(2,1)S(1)}, bf16[256,512]{1,0:T(8,128)(2,1)S(1)}, u32[]{:S(2)}, u32[]{:S(2)}) %collective-permute-start.17) | collective-permute-done | bytes 262176 | tf_op jit(solution)/shard_map/ppermute | solution.py:63
  61.4 5.1 %collective-permute-done.19.swapped_ref = bf16[256,512]{1,0:T(8,128)(2,1)S(1)} collective-permute-done((bf16[256,512]{1,0:T(8,128)(2,1)S(1)}, bf16[256,512]{1,0:T(8,128)(2,1)S(1)}, u32[]{:S(2)}, u32[]{:S(2)}) %collective-permute-start.19) | collective-permute-done | bytes 262176 | tf_op jit(solution)/shard_map/ppermute | solution.py:63
  67.0 4.3 %collective-permute-done.21.swapped_ref = bf16[256,512]{1,0:T(8,128)(2,1)S(1)} collective-permute-done((bf16[256,512]{1,0:T(8,128)(2,1)S(1)}, bf16[256,512]{1,0:T(8,128)(2,1)S(1)}, u32[]{:S(2)}, u32[]{:S(2)}) %collective-permute-start.21) | collective-permute-done | bytes 262176 | tf_op jit(solution)/shard_map/ppermute | solution.py:63
  75.9 3.1 %collective-permute-done.22.passed_ref = bf16[256,512]{1,0:T(8,128)(2,1)S(1)} collective-permute-done((bf16[256,512]{1,0:T(8,128)(2,1)S(1)}, bf16[256,512]{1,0:T(8,128)(2,1)S(1)}, u32[]{:S(2)}, u32[]{:S(2)}) %collective-permute-start.22) | collective-permute-done | bytes 262176 | tf_op jit(solution)/shard_map/ppermute | solution.py:73
  80.1 2.6 %collective-permute-done.23.passed_ref = bf16[256,512]{1,0:T(8,128)(2,1)S(1)} collective-permute-done((bf16[256,512]{1,0:T(8,128)(2,1)S(1)}, bf16[256,512]{1,0:T(8,128)(2,1)S(1)}, u32[]{:S(2)}, u32[]{:S(2)}) %collective-permute-start.23) | collective-permute-done | bytes 262176 | tf_op jit(solution)/shard_map/ppermute | solution.py:73
  85.0 11.7 %all_to_all.5.sums_ref = f32[16,2,1024]{2,1,0:T(2,128)S(1)} all-to-all(f32[16,2,1024]{2,1,0:T(2,128)S(1)} %broadcast_in_dim.30), channel_id=1, replica_groups={{0,1,2,3,4,5,6,7,16,17,18,19,20,21,22,23},{8,9,10,11,12,13,14,15,24,25,..., dimensions={0} | all-to-all | bytes 262144 | tf_op jit(solution)/shard_map/all_to_all | solution.py:93
  98.1 2.1 %update.1 = (f32[256,2048]{1,0:T(8,128)}, f32[256,2048]{1,0:T(8,128)}) custom-call(f32[1,2048]{1,0:T(1,128)S(1)} %pad_maximum_fusion.alpha_ref, f32[256,2048]{1,0:T(8,128)S(1)} %copy-done, bf16[256,512]{1,0:T(8,128)(2,1)S(1)} %get-tuple-element.80.own_ref.refs_0_, bf16[256,512]{1,0:T(8,128)(2,1)S(1)} %get-tuple-element.84.own_ref.refs_1_, ...), custom_call_target="tpu_custom_call" | custom-call | tf_op jit(solution)/shard_map/update/pallas_call | solution.py:314
  (69 shorter events, 22.3 us)
Async XLA Ops:
  2.8 9.4 %collective-permute-start = (bf16[256,512]{1,0:T(8,128)(2,1)S(1)}, bf16[256,512]{1,0:T(8,128)(2,1)S(1)}, u32[]{:S(2)}, u32[]{:S(2)}) collective-permute-start(bf16[256,512]{1,0:T(8,128)(2,1)S(1)} %get-tuple-element.59.after_ref.own_ref), channel_id=1, source_target_pairs={{0,1},{1,0},{2,3},{3,2},{4,5},{5,4},{6,7},{7,6},{8,9},{9,8},{10,11... | collective-permute-start | bytes 786440 | tf_op jit(solution)/shard_map/ppermute | solution.py:63
  5.8 8.1 %collective-permute-start.3 = (f32[8,2048]{1,0:T(8,128)S(1)}, f32[8,2048]{1,0:T(8,128)S(1)}, u32[]{:S(2)}, u32[]{:S(2)}) collective-permute-start(f32[8,2048]{1,0:T(8,128)S(1)} %get-tuple-element.51.refs_0_), channel_id=1, source_target_pairs={{0,6},{1,7},{2,4},{3,5},{4,2},{5,3},{6,0},{7,1},{8,14},{9,15},{10,... | collective-permute-start | bytes 196616 | tf_op jit(solution)/shard_map/ppermute | solution.py:63
  9.4 5.4 %collective-permute-start.2 = (f32[8,2048]{1,0:T(8,128)S(1)}, f32[8,2048]{1,0:T(8,128)S(1)}, u32[]{:S(2)}, u32[]{:S(2)}) collective-permute-start(f32[8,2048]{1,0:T(8,128)S(1)} %get-tuple-element.51.refs_0_), channel_id=1, source_target_pairs={{0,4},{1,5},{2,6},{3,7},{4,0},{5,1},{6,2},{7,3},{8,12},{9,13},{10,... | collective-permute-start | bytes 196616 | tf_op jit(solution)/shard_map/ppermute | solution.py:63
  9.4 5.5 %collective-permute-start.1 = (f32[8,2048]{1,0:T(8,128)S(1)}, f32[8,2048]{1,0:T(8,128)S(1)}, u32[]{:S(2)}, u32[]{:S(2)}) collective-permute-start(f32[8,2048]{1,0:T(8,128)S(1)} %get-tuple-element.51.refs_0_), channel_id=1, source_target_pairs={{0,2},{1,3},{2,0},{3,1},{4,6},{5,7},{6,4},{7,5},{8,10},{9,11},{10,... | collective-permute-start | bytes 196616 | tf_op jit(solution)/shard_map/ppermute | solution.py:63
  12.2 13.8 %collective-permute-start.8 = (bf16[256,512]{1,0:T(8,128)(2,1)S(1)}, bf16[256,512]{1,0:T(8,128)(2,1)S(1)}, u32[]{:S(2)}, u32[]{:S(2)}) collective-permute-start(bf16[256,512]{1,0:T(8,128)(2,1)S(1)} %get-tuple-element.67.own_ref), channel_id=1, source_target_pairs={{0,1},{1,0},{2,3},{3,2},{4,5},{5,4},{6,7},{7,6},{8,9},{9,8},{10,11... | collective-permute-start | bytes 786440 | tf_op jit(solution)/shard_map/ppermute | solution.py:63
  15.8 5.4 %collective-permute-start.4 = (f32[8,2048]{1,0:T(8,128)S(1)}, f32[8,2048]{1,0:T(8,128)S(1)}, u32[]{:S(2)}, u32[]{:S(2)}) collective-permute-start(f32[8,2048]{1,0:T(8,128)S(1)} %get-tuple-element.53), channel_id=1, source_target_pairs={{0,1},{1,0},{2,3},{3,2},{4,5},{5,4},{6,7},{7,6},{8,9},{9,8},{10,11... | collective-permute-start | bytes 196616 | tf_op jit(solution)/shard_map/ppermute | solution.py:63
  16.2 11.1 %collective-permute-start.7 = (bf16[256,512]{1,0:T(8,128)(2,1)S(1)}, bf16[256,512]{1,0:T(8,128)(2,1)S(1)}, u32[]{:S(2)}, u32[]{:S(2)}) collective-permute-start(bf16[256,512]{1,0:T(8,128)(2,1)S(1)} %collective-permute-done.swapped_ref), channel_id=1, source_target_pairs={{0,2},{1,7},{2,4},{3,1},{4,6},{5,3},{6,0},{7,5},{8,10},{9,15},{10,... | collective-permute-start | bytes 786440 | tf_op jit(solution)/shard_map/ppermute | solution.py:73
  21.7 8.9 %collective-permute-start.5 = (bf16[256,512]{1,0:T(8,128)(2,1)S(1)}, bf16[256,512]{1,0:T(8,128)(2,1)S(1)}, u32[]{:S(2)}, u32[]{:S(2)}) collective-permute-start(bf16[256,512]{1,0:T(8,128)(2,1)S(1)} %get-tuple-element.56), channel_id=1, source_target_pairs={{0,7},{1,0},{2,1},{3,2},{4,3},{5,4},{6,5},{7,6},{8,15},{9,8},{10,9... | collective-permute-start | bytes 786440 | tf_op jit(solution)/shard_map/ppermute | solution.py:78
  26.0 9.8 %collective-permute-start.6 = (bf16[256,512]{1,0:T(8,128)(2,1)S(1)}, bf16[256,512]{1,0:T(8,128)(2,1)S(1)}, u32[]{:S(2)}, u32[]{:S(2)}) collective-permute-start(bf16[256,512]{1,0:T(8,128)(2,1)S(1)} %get-tuple-element.70.own_ref), channel_id=1, source_target_pairs={{0,1},{1,0},{2,3},{3,2},{4,5},{5,4},{6,7},{7,6},{8,9},{9,8},{10,11... | collective-permute-start | bytes 786440 | tf_op jit(solution)/shard_map/ppermute | solution.py:63
  26.0 1.3 %collective-permute-start.9 = (f32[8,2048]{1,0:T(8,128)S(1)}, f32[8,2048]{1,0:T(8,128)S(1)}, u32[]{:S(2)}, u32[]{:S(2)}) collective-permute-start(f32[8,2048]{1,0:T(8,128)S(1)} %add.24), channel_id=1, source_target_pairs={{0,8},{8,0},{16,24},{24,16},{1,9},{9,1},{17,25},{25,17},{2,10},{10... | collective-permute-start | bytes 196616 | tf_op jit(solution)/shard_map/ppermute | solution.py:63
  27.3 9.4 %collective-permute-start.10 = (f32[8,2048]{1,0:T(8,128)S(1)}, f32[8,2048]{1,0:T(8,128)S(1)}, u32[]{:S(2)}, u32[]{:S(2)}) collective-permute-start(f32[8,2048]{1,0:T(8,128)S(1)} %add.25), channel_id=1, source_target_pairs={{0,16},{8,24},{16,0},{24,8},{1,17},{9,25},{17,1},{25,9},{2,18},{10... | collective-permute-start | bytes 196616 | tf_op jit(solution)/shard_map/ppermute | solution.py:63
  28.9 9.9 %collective-permute-start.11 = (bf16[256,512]{1,0:T(8,128)(2,1)S(1)}, bf16[256,512]{1,0:T(8,128)(2,1)S(1)}, u32[]{:S(2)}, u32[]{:S(2)}) collective-permute-start(bf16[256,512]{1,0:T(8,128)(2,1)S(1)} %collective-permute-done.8.swapped_ref), channel_id=1, source_target_pairs={{0,2},{1,7},{2,4},{3,1},{4,6},{5,3},{6,0},{7,5},{8,10},{9,15},{10,... | collective-permute-start | bytes 786440 | tf_op jit(solution)/shard_map/ppermute | solution.py:73
  30.5 10.5 %collective-permute-start.13 = (bf16[256,512]{1,0:T(8,128)(2,1)S(1)}, bf16[256,512]{1,0:T(8,128)(2,1)S(1)}, u32[]{:S(2)}, u32[]{:S(2)}) collective-permute-start(bf16[256,512]{1,0:T(8,128)(2,1)S(1)} %get-tuple-element.77.own_ref), channel_id=1, source_target_pairs={{0,1},{1,0},{2,3},{3,2},{4,5},{5,4},{6,7},{7,6},{8,9},{9,8},{10,11... | collective-permute-start | bytes 786440 | tf_op jit(solution)/shard_map/ppermute | solution.py:63
  35.8 11.7 %collective-permute-start.12 = (bf16[256,512]{1,0:T(8,128)(2,1)S(1)}, bf16[256,512]{1,0:T(8,128)(2,1)S(1)}, u32[]{:S(2)}, u32[]{:S(2)}) collective-permute-start(bf16[256,512]{1,0:T(8,128)(2,1)S(1)} %collective-permute-done.6.swapped_ref), channel_id=1, source_target_pairs={{0,2},{1,7},{2,4},{3,1},{4,6},{5,3},{6,0},{7,5},{8,10},{9,15},{10,... | collective-permute-start | bytes 786440 | tf_op jit(solution)/shard_map/ppermute | solution.py:73
  38.8 11.4 %collective-permute-start.14 = (bf16[256,512]{1,0:T(8,128)(2,1)S(1)}, bf16[256,512]{1,0:T(8,128)(2,1)S(1)}, u32[]{:S(2)}, u32[]{:S(2)}) collective-permute-start(bf16[256,512]{1,0:T(8,128)(2,1)S(1)} %slice.13), channel_id=1, source_target_pairs={{0,7},{1,0},{2,1},{3,2},{4,3},{5,4},{6,5},{7,6},{8,15},{9,8},{10,9... | collective-permute-start | bytes 786440 | tf_op jit(solution)/shard_map/ppermute | solution.py:78
  41.0 15.2 %collective-permute-start.15 = (bf16[256,512]{1,0:T(8,128)(2,1)S(1)}, bf16[256,512]{1,0:T(8,128)(2,1)S(1)}, u32[]{:S(2)}, u32[]{:S(2)}) collective-permute-start(bf16[256,512]{1,0:T(8,128)(2,1)S(1)} %collective-permute-done.13.swapped_ref), channel_id=1, source_target_pairs={{0,2},{1,7},{2,4},{3,1},{4,6},{5,3},{6,0},{7,5},{8,10},{9,15},{10,... | collective-permute-start | bytes 786440 | tf_op jit(solution)/shard_map/ppermute | solution.py:73
  44.1 13.4 %collective-permute-start.16 = (bf16[256,512]{1,0:T(8,128)(2,1)S(1)}, bf16[256,512]{1,0:T(8,128)(2,1)S(1)}, u32[]{:S(2)}, u32[]{:S(2)}) collective-permute-start(bf16[256,512]{1,0:T(8,128)(2,1)S(1)} %get-tuple-element.80.own_ref.refs_0_), channel_id=1, source_target_pairs={{0,1},{1,0},{2,3},{3,2},{4,5},{5,4},{6,7},{7,6},{8,9},{9,8},{10,11... | collective-permute-start | bytes 786440 | tf_op jit(solution)/shard_map/ppermute | solution.py:63
  46.8 14.1 %collective-permute-start.17 = (bf16[256,512]{1,0:T(8,128)(2,1)S(1)}, bf16[256,512]{1,0:T(8,128)(2,1)S(1)}, u32[]{:S(2)}, u32[]{:S(2)}) collective-permute-start(bf16[256,512]{1,0:T(8,128)(2,1)S(1)} %get-tuple-element.84.own_ref.refs_1_), channel_id=1, source_target_pairs={{0,1},{1,0},{2,3},{3,2},{4,5},{5,4},{6,7},{7,6},{8,9},{9,8},{10,11... | collective-permute-start | bytes 786440 | tf_op jit(solution)/shard_map/ppermute | solution.py:63
  48.7 17.8 %collective-permute-start.19 = (bf16[256,512]{1,0:T(8,128)(2,1)S(1)}, bf16[256,512]{1,0:T(8,128)(2,1)S(1)}, u32[]{:S(2)}, u32[]{:S(2)}) collective-permute-start(bf16[256,512]{1,0:T(8,128)(2,1)S(1)} %get-tuple-element.88.own_ref.refs_2_), channel_id=1, source_target_pairs={{0,1},{1,0},{2,3},{3,2},{4,5},{5,4},{6,7},{7,6},{8,9},{9,8},{10,11... | collective-permute-start | bytes 786440 | tf_op jit(solution)/shard_map/ppermute | solution.py:63
  57.5 13.8 %collective-permute-start.21 = (bf16[256,512]{1,0:T(8,128)(2,1)S(1)}, bf16[256,512]{1,0:T(8,128)(2,1)S(1)}, u32[]{:S(2)}, u32[]{:S(2)}) collective-permute-start(bf16[256,512]{1,0:T(8,128)(2,1)S(1)} %get-tuple-element.90.own_ref.refs_3_), channel_id=1, source_target_pairs={{0,1},{1,0},{2,3},{3,2},{4,5},{5,4},{6,7},{7,6},{8,9},{9,8},{10,11... | collective-permute-start | bytes 786440 | tf_op jit(solution)/shard_map/ppermute | solution.py:63
  57.5 16.3 %collective-permute-start.18 = (bf16[256,512]{1,0:T(8,128)(2,1)S(1)}, bf16[256,512]{1,0:T(8,128)(2,1)S(1)}, u32[]{:S(2)}, u32[]{:S(2)}) collective-permute-start(bf16[256,512]{1,0:T(8,128)(2,1)S(1)} %collective-permute-done.16.swapped_ref), channel_id=1, source_target_pairs={{0,2},{1,7},{2,4},{3,1},{4,6},{5,3},{6,0},{7,5},{8,10},{9,15},{10,... | collective-permute-start | bytes 786440 | tf_op jit(solution)/shard_map/ppermute | solution.py:73
  60.9 14.0 %collective-permute-start.20 = (bf16[256,512]{1,0:T(8,128)(2,1)S(1)}, bf16[256,512]{1,0:T(8,128)(2,1)S(1)}, u32[]{:S(2)}, u32[]{:S(2)}) collective-permute-start(bf16[256,512]{1,0:T(8,128)(2,1)S(1)} %collective-permute-done.17.swapped_ref), channel_id=1, source_target_pairs={{0,2},{1,7},{2,4},{3,1},{4,6},{5,3},{6,0},{7,5},{8,10},{9,15},{10,... | collective-permute-start | bytes 786440 | tf_op jit(solution)/shard_map/ppermute | solution.py:73
  66.5 12.5 %collective-permute-start.22 = (bf16[256,512]{1,0:T(8,128)(2,1)S(1)}, bf16[256,512]{1,0:T(8,128)(2,1)S(1)}, u32[]{:S(2)}, u32[]{:S(2)}) collective-permute-start(bf16[256,512]{1,0:T(8,128)(2,1)S(1)} %collective-permute-done.19.swapped_ref), channel_id=1, source_target_pairs={{0,2},{1,7},{2,4},{3,1},{4,6},{5,3},{6,0},{7,5},{8,10},{9,15},{10,... | collective-permute-start | bytes 786440 | tf_op jit(solution)/shard_map/ppermute | solution.py:73
  71.3 11.4 %collective-permute-start.23 = (bf16[256,512]{1,0:T(8,128)(2,1)S(1)}, bf16[256,512]{1,0:T(8,128)(2,1)S(1)}, u32[]{:S(2)}, u32[]{:S(2)}) collective-permute-start(bf16[256,512]{1,0:T(8,128)(2,1)S(1)} %collective-permute-done.21.swapped_ref), channel_id=1, source_target_pairs={{0,2},{1,7},{2,4},{3,1},{4,6},{5,3},{6,0},{7,5},{8,10},{9,15},{10,... | collective-permute-start | bytes 786440 | tf_op jit(solution)/shard_map/ppermute | solution.py:73
  (8 other events, 132.6 us)

commit v3 on v2

--- a/solution.py
+++ b/solution.py
@@ -16,21 +16,20 @@
 EIGHTHS = (2, 2, 2, 2)
 TIES = {
     "d0": ("s2",),
-    "d3": ("n",),
+    "d3": ("n", "x0"),
     "e": ("s0",),
-    "g": ("e", "c"),
-    "h": ("m", "p1", "s1"),
+    "g": ("c", "e"),
+    "h": ("m", "s1"),
     "i0": ("x1",),
     "i1": ("x2",),
     "i2": ("x3",),
-    "n": ("h",),
+    "n": ("s2",),
     "s1": ("s0",),
     "s2": ("c", "s0"),
     "s3": ("m",),
     "t": ("s1",),
     "u": ("p0",),
     "x0": ("s3",),
-    "y0": ("d1",),
 }
 
 
@@ -96,39 +95,52 @@
     return jnp.concatenate([jnp.where(odd, other, alpha), jnp.where(odd, alpha, other)], axis=1)
 
 
-def first_kernel(place_ref, index_ref, right_ref, chunk_ref, primal_ref, face, blocks, sems):
+def first_kernel(place_ref, right_ref, chunk_ref):
+    chunk_ref[...] = right_ref[...].astype(BF16)
+
+
+def first_chunk(place, right_side, size):
+    rows = right_side.shape[0]
+    block = pl.BlockSpec((rows, size), lambda i: (0, 0))
+    return pl.pallas_call(
+        first_kernel,
+        grid=(1,),
+        out_shape=shape(rows, size, BF16),
+        in_specs=[whole(SMEM), block],
+        out_specs=block,
+        compiler_params=params(8),
+        name="first",
+    )(place, right_side)
+
+
+def pick_kernel(index_ref, right_ref, after_ref, primal_ref, blocks, sems):
     rank = primal_ref.shape[0]
-    size = chunk_ref.shape[1]
-    copies = [pltpu.make_async_copy(right_ref.at[:, :size], face, sems.at[rank])]
+    copies = []
     for k in range(rank):
         begin = pl.multiple_of((index_ref[0, k] >> 3) << 3, 8)
         source = right_ref.at[pl.ds(begin, 8), :]
         copies.append(pltpu.make_async_copy(source, blocks.at[k], sems.at[k]))
-    for copy in copies:
-        copy.start()
-    copies[0].wait()
-    chunk_ref[...] = face[...].astype(BF16)
+        copies[-1].start()
     for k in range(rank):
-        copies[k + 1].wait()
+        copies[k].wait()
         primal_ref[k : k + 1, :] = blocks[k, pl.ds(index_ref[0, k] & 7, 1), :]
 
 
-def first_chunk(place, right_side, primal_index, size):
-    rows, columns = right_side.shape
+def pick(right_side, primal_index, first):
+    columns = right_side.shape[1]
     rank = primal_index.shape[1]
     return pl.pallas_call(
-        first_kernel,
-        out_shape=[shape(rows, size, BF16), shape(rank, columns, F32)],
-        in_specs=[whole(SMEM), whole(SMEM), whole(pl.ANY)],
-        out_specs=[whole(), whole()],
+        pick_kernel,
+        out_shape=shape(rank, columns, F32),
+        in_specs=[whole(SMEM), whole(pl.ANY), whole(pl.ANY)],
+        out_specs=whole(),
         scratch_shapes=[
-            pltpu.VMEM((rows, size), F32),
             pltpu.VMEM((rank, 8, columns), F32),
-            pltpu.SemaphoreType.DMA((rank + 1,)),
+            pltpu.SemaphoreType.DMA((rank,)),
         ],
         compiler_params=params(8),
-        name="first",
-    )(place, primal_index, pltpu.with_memory_space_constraint(right_side, pltpu.HBM))
+        name="pick",
+    )(primal_index, right_side, first)
 
 
 def split_kernel(sizes, right_ref, after_ref, *chunk_refs):
@@ -348,7 +360,9 @@
         return after(value, *others) if others else value
 
     primal_index = pltpu.with_memory_space_constraint(primal_index, pltpu.HBM)
-    first, own_primal = first_chunk(place, right_side, primal_index, sizes[0])
+    in_hbm = pltpu.with_memory_space_constraint(right_side, pltpu.HBM)
+    first = first_chunk(place, in_hbm, sizes[0])
+    own_primal = pick(in_hbm, primal_index, first)
     resid = split(right_side, first, sizes)
 
     masks = range(0, subs, 2)

time: 100 us -> 99.5 us (level)
  waiting for transfers between devices: 41.9 us -> 40.1 us
  Pallas kernels: 14.6 us -> 15.7 us
    ppermute x8, starting transfers between devices: 5.99 us -> 1.1 us  [pass_on(): return lax.ppermute(value, 'sub', pairs)]
    ppermute x8, waiting for transfers between devices: 13.9 us -> 11.4 us  [pass_on(): return lax.ppermute(value, 'sub', pairs)]
    ppermute x16, starting transfers between devices: 17.1 us -> 19.2 us  [exchange(): return lax.ppermute(value, axis, [(i, i ^ step) for i in range(count)])]
    ppermute x2, starting transfers between devices: 6.36 us -> 8.29 us  [to_left(): lax.ppermute(value, 'sub', [(j, (j - 1) % count) for j in range(count)])]
    ppermute x16, waiting for transfers between devices: 26.4 us -> 27.9 us  [exchange(): return lax.ppermute(value, axis, [(i, i ^ step) for i in range(count)])]
    pallas_call x1 -> x2, Pallas kernels: 2.03 us -> 3.03 us  [the longest x1 1.8 us: pick(): pl.pallas_call(pick_kernel, out_shape=shape(rank, columns, F32), in_specs...]
  transfers between devices with their start and end apart: 26 -> 26, of which waited for: 17 -> 20; matrix products, arithmetic and copies ran while one was open for 1% -> 1% of each run, Pallas kernels for 9% -> 11%
where the time goes in v3:
time: 99.5 us; the launch traced here: 99.2 us
  waiting for transfers between devices  40.1 us (40%)
  starting transfers between devices  28.6 us (29%)
  Pallas kernels  15.7 us (16%)
  blocking collectives  12.2 us (12%)
  between operations  1.57 us (2%)
    ppermute x16, waiting for transfers between devices, exchange(): return lax.ppermute(value, axis, [(i, i ^ step) for i in range(count)])  27.9 us
    ppermute x16, starting transfers between devices, exchange(): return lax.ppermute(value, axis, [(i, i ^ step) for i in range(count)])  19.2 us
    all_to_all x1, blocking collectives, step_length(): lax.all_to_all(copies, ('grp', 'sub'), 0, 0, axis_index_groups=same, tile...  12.2 us
    ppermute x8, waiting for transfers between devices, pass_on(): return lax.ppermute(value, 'sub', pairs)  11.4 us
    ppermute x2, starting transfers between devices, to_left(): lax.ppermute(value, 'sub', [(j, (j - 1) % count) for j in range(count)])  8.29 us
    pallas_call x4, Pallas kernels, direction_chunk(): pl.pallas_call(functools.partial(direction_kernel, slice(begin, begin + s...  4.94 us
    pallas_call x4, Pallas kernels, image_chunk(): pl.pallas_call(image_kernel, out_shape=[pltpu.VMEM((rows, size), F32), sh...  4.04 us
    pallas_call x1, Pallas kernels, update(): pl.pallas_call(functools.partial(update_kernel, sizes), out_shape=[out, o...  2.16 us
  transfers between devices with their start and end apart: 26, of which 20 were waited for; matrix products, arithmetic and copies ran while one was open for 1% of the time, Pallas kernels for 11%

profile of v3, /device:TPU:0, one launch (start us, length us, event | category | flops | bytes accessed | tf_op | source)
XLA Modules:
  0.0 99.2 jit_solution(11810033745579117463)
XLA Ops:
  2.0 3.0 %collective-permute-start = (bf16[256,512]{1,0:T(8,128)(2,1)S(1)}, bf16[256,512]{1,0:T(8,128)(2,1)S(1)}, u32[]{:S(2)}, u32[]{:S(2)}) collective-permute-start(bf16[256,512]{1,0:T(8,128)(2,1)S(1)} %first.1.after_ref.own_ref), channel_id=1, source_target_pairs={{0,1},{1,0},{2,3},{3,2},{4,5},{5,4},{6,7},{7,6},{8,9},{9,8},{10,11... | collective-permute-start | bytes 786440 | tf_op jit(solution)/shard_map/ppermute | solution.py:62
  5.0 1.8 %pick.1.refs_0_ = f32[8,2048]{1,0:T(8,128)S(1)} custom-call(s32[1,8]{1,0:T(1,128)} %index_ref.9, f32[256,2048]{1,0:T(8,128)} %right_ref.15, bf16[256,512]{1,0:T(8,128)(2,1)S(1)} %first.1.after_ref.own_ref), custom_call_target="tpu_custom_call" | custom-call | tf_op jit(solution)/shard_map/pick/pallas_call | solution.py:132
  6.8 3.7 %collective-permute-start.3 = (f32[8,2048]{1,0:T(8,128)S(1)}, f32[8,2048]{1,0:T(8,128)S(1)}, u32[]{:S(2)}, u32[]{:S(2)}) collective-permute-start(f32[8,2048]{1,0:T(8,128)S(1)} %pick.1.refs_0_), channel_id=1, source_target_pairs={{0,6},{1,7},{2,4},{3,5},{4,2},{5,3},{6,0},{7,1},{8,14},{9,15},{10,... | collective-permute-start | bytes 196616 | tf_op jit(solution)/shard_map/ppermute | solution.py:62
  11.4 1.7 %collective-permute-start.8 = (bf16[256,512]{1,0:T(8,128)(2,1)S(1)}, bf16[256,512]{1,0:T(8,128)(2,1)S(1)}, u32[]{:S(2)}, u32[]{:S(2)}) collective-permute-start(bf16[256,512]{1,0:T(8,128)(2,1)S(1)} %get-tuple-element.62.own_ref), channel_id=1, source_target_pairs={{0,1},{1,0},{2,3},{3,2},{4,5},{5,4},{6,7},{7,6},{8,9},{9,8},{10,11... | collective-permute-start | bytes 786440 | tf_op jit(solution)/shard_map/ppermute | solution.py:62
  13.7 2.1 %collective-permute-done.2.refs_2_ = f32[8,2048]{1,0:T(8,128)S(1)} collective-permute-done((f32[8,2048]{1,0:T(8,128)S(1)}, f32[8,2048]{1,0:T(8,128)S(1)}, u32[]{:S(2)}, u32[]{:S(2)}) %collective-permute-start.2) | collective-permute-done | bytes 65568 | tf_op jit(solution)/shard_map/ppermute | solution.py:62
  18.4 2.8 %collective-permute-done.4 = f32[8,2048]{1,0:T(8,128)S(1)} collective-permute-done((f32[8,2048]{1,0:T(8,128)S(1)}, f32[8,2048]{1,0:T(8,128)S(1)}, u32[]{:S(2)}, u32[]{:S(2)}) %collective-permute-start.4) | collective-permute-done | bytes 65568 | tf_op jit(solution)/shard_map/ppermute | solution.py:62
  21.6 3.6 %collective-permute-start.5 = (bf16[256,512]{1,0:T(8,128)(2,1)S(1)}, bf16[256,512]{1,0:T(8,128)(2,1)S(1)}, u32[]{:S(2)}, u32[]{:S(2)}) collective-permute-start(bf16[256,512]{1,0:T(8,128)(2,1)S(1)} %get-tuple-element.51), channel_id=1, source_target_pairs={{0,7},{1,0},{2,1},{3,2},{4,3},{5,4},{6,5},{7,6},{8,15},{9,8},{10,9... | collective-permute-start | bytes 786440 | tf_op jit(solution)/shard_map/ppermute | solution.py:77
  25.2 1.2 %collective-permute-done.9 = f32[8,2048]{1,0:T(8,128)S(1)} collective-permute-done((f32[8,2048]{1,0:T(8,128)S(1)}, f32[8,2048]{1,0:T(8,128)S(1)}, u32[]{:S(2)}, u32[]{:S(2)}) %collective-permute-start.9) | collective-permute-done | bytes 65568 | tf_op jit(solution)/shard_map/ppermute | solution.py:62
  26.5 1.9 %collective-permute-done.7.passed_ref = bf16[256,512]{1,0:T(8,128)(2,1)S(1)} collective-permute-done((bf16[256,512]{1,0:T(8,128)(2,1)S(1)}, bf16[256,512]{1,0:T(8,128)(2,1)S(1)}, u32[]{:S(2)}, u32[]{:S(2)}) %collective-permute-start.7) | collective-permute-done | bytes 262176 | tf_op jit(solution)/shard_map/ppermute | solution.py:72
  28.3 1.6 %collective-permute-start.10 = (f32[8,2048]{1,0:T(8,128)S(1)}, f32[8,2048]{1,0:T(8,128)S(1)}, u32[]{:S(2)}, u32[]{:S(2)}) collective-permute-start(f32[8,2048]{1,0:T(8,128)S(1)} %add.25), channel_id=1, source_target_pairs={{0,16},{8,24},{16,0},{24,8},{1,17},{9,25},{17,1},{25,9},{2,18},{10... | collective-permute-start | bytes 196616 | tf_op jit(solution)/shard_map/ppermute | solution.py:62
  30.7 3.0 %collective-permute-start.13 = (bf16[256,512]{1,0:T(8,128)(2,1)S(1)}, bf16[256,512]{1,0:T(8,128)(2,1)S(1)}, u32[]{:S(2)}, u32[]{:S(2)}) collective-permute-start(bf16[256,512]{1,0:T(8,128)(2,1)S(1)} %get-tuple-element.73.own_ref), channel_id=1, source_target_pairs={{0,1},{1,0},{2,3},{3,2},{4,5},{5,4},{6,7},{7,6},{8,9},{9,8},{10,11... | collective-permute-start | bytes 786440 | tf_op jit(solution)/shard_map/ppermute | solution.py:62
  33.7 1.5 %collective-permute-done.6.swapped_ref = bf16[256,512]{1,0:T(8,128)(2,1)S(1)} collective-permute-done((bf16[256,512]{1,0:T(8,128)(2,1)S(1)}, bf16[256,512]{1,0:T(8,128)(2,1)S(1)}, u32[]{:S(2)}, u32[]{:S(2)}) %collective-permute-start.6) | collective-permute-done | bytes 262176 | tf_op jit(solution)/shard_map/ppermute | solution.py:62
  35.3 4.7 %collective-permute-start.14 = (bf16[256,512]{1,0:T(8,128)(2,1)S(1)}, bf16[256,512]{1,0:T(8,128)(2,1)S(1)}, u32[]{:S(2)}, u32[]{:S(2)}) collective-permute-start(bf16[256,512]{1,0:T(8,128)(2,1)S(1)} %slice.13), channel_id=1, source_target_pairs={{0,7},{1,0},{2,1},{3,2},{4,3},{5,4},{6,5},{7,6},{8,15},{9,8},{10,9... | collective-permute-start | bytes 786440 | tf_op jit(solution)/shard_map/ppermute | solution.py:77
  41.3 3.3 %collective-permute-done.13.swapped_ref = bf16[256,512]{1,0:T(8,128)(2,1)S(1)} collective-permute-done((bf16[256,512]{1,0:T(8,128)(2,1)S(1)}, bf16[256,512]{1,0:T(8,128)(2,1)S(1)}, u32[]{:S(2)}, u32[]{:S(2)}) %collective-permute-start.13) | collective-permute-done | bytes 262176 | tf_op jit(solution)/shard_map/ppermute | solution.py:62
  44.6 2.6 %collective-permute-start.15 = (bf16[256,512]{1,0:T(8,128)(2,1)S(1)}, bf16[256,512]{1,0:T(8,128)(2,1)S(1)}, u32[]{:S(2)}, u32[]{:S(2)}) collective-permute-start(bf16[256,512]{1,0:T(8,128)(2,1)S(1)} %get-tuple-element.75.own_ref.refs_0_), channel_id=1, source_target_pairs={{0,1},{1,0},{2,3},{3,2},{4,5},{5,4},{6,7},{7,6},{8,9},{9,8},{10,11... | collective-permute-start | bytes 786440 | tf_op jit(solution)/shard_map/ppermute | solution.py:62
  51.9 2.6 %collective-permute-done.15.swapped_ref = bf16[256,512]{1,0:T(8,128)(2,1)S(1)} collective-permute-done((bf16[256,512]{1,0:T(8,128)(2,1)S(1)}, bf16[256,512]{1,0:T(8,128)(2,1)S(1)}, u32[]{:S(2)}, u32[]{:S(2)}) %collective-permute-start.15) | collective-permute-done | bytes 262176 | tf_op jit(solution)/shard_map/ppermute | solution.py:62
  57.8 2.2 %collective-permute-done.17.swapped_ref = bf16[256,512]{1,0:T(8,128)(2,1)S(1)} collective-permute-done((bf16[256,512]{1,0:T(8,128)(2,1)S(1)}, bf16[256,512]{1,0:T(8,128)(2,1)S(1)}, u32[]{:S(2)}, u32[]{:S(2)}) %collective-permute-start.17) | collective-permute-done | bytes 262176 | tf_op jit(solution)/shard_map/ppermute | solution.py:62
  60.1 5.6 %collective-permute-done.19.swapped_ref = bf16[256,512]{1,0:T(8,128)(2,1)S(1)} collective-permute-done((bf16[256,512]{1,0:T(8,128)(2,1)S(1)}, bf16[256,512]{1,0:T(8,128)(2,1)S(1)}, u32[]{:S(2)}, u32[]{:S(2)}) %collective-permute-start.19) | collective-permute-done | bytes 262176 | tf_op jit(solution)/shard_map/ppermute | solution.py:62
  65.7 3.4 %collective-permute-done.21.swapped_ref = bf16[256,512]{1,0:T(8,128)(2,1)S(1)} collective-permute-done((bf16[256,512]{1,0:T(8,128)(2,1)S(1)}, bf16[256,512]{1,0:T(8,128)(2,1)S(1)}, u32[]{:S(2)}, u32[]{:S(2)}) %collective-permute-start.21) | collective-permute-done | bytes 262176 | tf_op jit(solution)/shard_map/ppermute | solution.py:62
  71.6 2.3 %collective-permute-done.20.passed_ref = bf16[256,512]{1,0:T(8,128)(2,1)S(1)} collective-permute-done((bf16[256,512]{1,0:T(8,128)(2,1)S(1)}, bf16[256,512]{1,0:T(8,128)(2,1)S(1)}, u32[]{:S(2)}, u32[]{:S(2)}) %collective-permute-start.20) | collective-permute-done | bytes 262176 | tf_op jit(solution)/shard_map/ppermute | solution.py:72
  74.9 3.4 %collective-permute-done.22.passed_ref = bf16[256,512]{1,0:T(8,128)(2,1)S(1)} collective-permute-done((bf16[256,512]{1,0:T(8,128)(2,1)S(1)}, bf16[256,512]{1,0:T(8,128)(2,1)S(1)}, u32[]{:S(2)}, u32[]{:S(2)}) %collective-permute-start.22) | collective-permute-done | bytes 262176 | tf_op jit(solution)/shard_map/ppermute | solution.py:72
  79.3 1.8 %collective-permute-done.23.passed_ref = bf16[256,512]{1,0:T(8,128)(2,1)S(1)} collective-permute-done((bf16[256,512]{1,0:T(8,128)(2,1)S(1)}, bf16[256,512]{1,0:T(8,128)(2,1)S(1)}, u32[]{:S(2)}, u32[]{:S(2)}) %collective-permute-start.23) | collective-permute-done | bytes 262176 | tf_op jit(solution)/shard_map/ppermute | solution.py:72
  83.5 12.2 %all_to_all.5.sums_ref = f32[16,2,1024]{2,1,0:T(2,128)S(1)} all-to-all(f32[16,2,1024]{2,1,0:T(2,128)S(1)} %broadcast_in_dim.30), channel_id=1, replica_groups={{0,1,2,3,4,5,6,7,16,17,18,19,20,21,22,23},{8,9,10,11,12,13,14,15,24,25,..., dimensions={0} | all-to-all | bytes 262144 | tf_op jit(solution)/shard_map/all_to_all | solution.py:92
  97.0 2.2 %update.1 = (f32[256,2048]{1,0:T(8,128)}, f32[256,2048]{1,0:T(8,128)}) custom-call(f32[1,2048]{1,0:T(1,128)S(1)} %pad_maximum_fusion.alpha_ref, f32[256,2048]{1,0:T(8,128)S(1)} %copy-done, bf16[256,512]{1,0:T(8,128)(2,1)S(1)} %get-tuple-element.75.own_ref.refs_0_, bf16[256,512]{1,0:T(8,128)(2,1)S(1)} %get-tuple-element.78.own_ref.refs_1_, ...), custom_call_target="tpu_custom_call" | custom-call | tf_op jit(solution)/shard_map/update/pallas_call | solution.py:326
  (70 shorter events, 23.4 us)
Async XLA Ops:
  2.0 9.4 %collective-permute-start = (bf16[256,512]{1,0:T(8,128)(2,1)S(1)}, bf16[256,512]{1,0:T(8,128)(2,1)S(1)}, u32[]{:S(2)}, u32[]{:S(2)}) collective-permute-start(bf16[256,512]{1,0:T(8,128)(2,1)S(1)} %first.1.after_ref.own_ref), channel_id=1, source_target_pairs={{0,1},{1,0},{2,3},{3,2},{4,5},{5,4},{6,7},{7,6},{8,9},{9,8},{10,11... | collective-permute-start | bytes 786440 | tf_op jit(solution)/shard_map/ppermute | solution.py:62
  6.8 6.9 %collective-permute-start.3 = (f32[8,2048]{1,0:T(8,128)S(1)}, f32[8,2048]{1,0:T(8,128)S(1)}, u32[]{:S(2)}, u32[]{:S(2)}) collective-permute-start(f32[8,2048]{1,0:T(8,128)S(1)} %pick.1.refs_0_), channel_id=1, source_target_pairs={{0,6},{1,7},{2,4},{3,5},{4,2},{5,3},{6,0},{7,1},{8,14},{9,15},{10,... | collective-permute-start | bytes 196616 | tf_op jit(solution)/shard_map/ppermute | solution.py:62
  10.5 5.4 %collective-permute-start.2 = (f32[8,2048]{1,0:T(8,128)S(1)}, f32[8,2048]{1,0:T(8,128)S(1)}, u32[]{:S(2)}, u32[]{:S(2)}) collective-permute-start(f32[8,2048]{1,0:T(8,128)S(1)} %pick.1.refs_0_), channel_id=1, source_target_pairs={{0,4},{1,5},{2,6},{3,7},{4,0},{5,1},{6,2},{7,3},{8,12},{9,13},{10,... | collective-permute-start | bytes 196616 | tf_op jit(solution)/shard_map/ppermute | solution.py:62
  10.5 5.4 %collective-permute-start.1 = (f32[8,2048]{1,0:T(8,128)S(1)}, f32[8,2048]{1,0:T(8,128)S(1)}, u32[]{:S(2)}, u32[]{:S(2)}) collective-permute-start(f32[8,2048]{1,0:T(8,128)S(1)} %pick.1.refs_0_), channel_id=1, source_target_pairs={{0,2},{1,3},{2,0},{3,1},{4,6},{5,7},{6,4},{7,5},{8,10},{9,11},{10,... | collective-permute-start | bytes 196616 | tf_op jit(solution)/shard_map/ppermute | solution.py:62
  11.4 13.8 %collective-permute-start.8 = (bf16[256,512]{1,0:T(8,128)(2,1)S(1)}, bf16[256,512]{1,0:T(8,128)(2,1)S(1)}, u32[]{:S(2)}, u32[]{:S(2)}) collective-permute-start(bf16[256,512]{1,0:T(8,128)(2,1)S(1)} %get-tuple-element.62.own_ref), channel_id=1, source_target_pairs={{0,1},{1,0},{2,3},{3,2},{4,5},{5,4},{6,7},{7,6},{8,9},{9,8},{10,11... | collective-permute-start | bytes 786440 | tf_op jit(solution)/shard_map/ppermute | solution.py:62
  16.8 4.3 %collective-permute-start.4 = (f32[8,2048]{1,0:T(8,128)S(1)}, f32[8,2048]{1,0:T(8,128)S(1)}, u32[]{:S(2)}, u32[]{:S(2)}) collective-permute-start(f32[8,2048]{1,0:T(8,128)S(1)} %get-tuple-element.48), channel_id=1, source_target_pairs={{0,1},{1,0},{2,3},{3,2},{4,5},{5,4},{6,7},{7,6},{8,9},{9,8},{10,11... | collective-permute-start | bytes 196616 | tf_op jit(solution)/shard_map/ppermute | solution.py:62
  17.3 11.0 %collective-permute-start.7 = (bf16[256,512]{1,0:T(8,128)(2,1)S(1)}, bf16[256,512]{1,0:T(8,128)(2,1)S(1)}, u32[]{:S(2)}, u32[]{:S(2)}) collective-permute-start(bf16[256,512]{1,0:T(8,128)(2,1)S(1)} %collective-permute-done.swapped_ref), channel_id=1, source_target_pairs={{0,2},{1,7},{2,4},{3,1},{4,6},{5,3},{6,0},{7,5},{8,10},{9,15},{10,... | collective-permute-start | bytes 786440 | tf_op jit(solution)/shard_map/ppermute | solution.py:72
  21.6 9.1 %collective-permute-start.5 = (bf16[256,512]{1,0:T(8,128)(2,1)S(1)}, bf16[256,512]{1,0:T(8,128)(2,1)S(1)}, u32[]{:S(2)}, u32[]{:S(2)}) collective-permute-start(bf16[256,512]{1,0:T(8,128)(2,1)S(1)} %get-tuple-element.51), channel_id=1, source_target_pairs={{0,7},{1,0},{2,1},{3,2},{4,3},{5,4},{6,5},{7,6},{8,15},{9,8},{10,9... | collective-permute-start | bytes 786440 | tf_op jit(solution)/shard_map/ppermute | solution.py:77
  25.2 10.1 %collective-permute-start.6 = (bf16[256,512]{1,0:T(8,128)(2,1)S(1)}, bf16[256,512]{1,0:T(8,128)(2,1)S(1)}, u32[]{:S(2)}, u32[]{:S(2)}) collective-permute-start(bf16[256,512]{1,0:T(8,128)(2,1)S(1)} %get-tuple-element.65.own_ref), channel_id=1, source_target_pairs={{0,1},{1,0},{2,3},{3,2},{4,5},{5,4},{6,7},{7,6},{8,9},{9,8},{10,11... | collective-permute-start | bytes 786440 | tf_op jit(solution)/shard_map/ppermute | solution.py:62
  25.2 1.3 %collective-permute-start.9 = (f32[8,2048]{1,0:T(8,128)S(1)}, f32[8,2048]{1,0:T(8,128)S(1)}, u32[]{:S(2)}, u32[]{:S(2)}) collective-permute-start(f32[8,2048]{1,0:T(8,128)S(1)} %add.24), channel_id=1, source_target_pairs={{0,8},{8,0},{16,24},{24,16},{1,9},{9,1},{17,25},{25,17},{2,10},{10... | collective-permute-start | bytes 196616 | tf_op jit(solution)/shard_map/ppermute | solution.py:62
  28.3 11.7 %collective-permute-start.10 = (f32[8,2048]{1,0:T(8,128)S(1)}, f32[8,2048]{1,0:T(8,128)S(1)}, u32[]{:S(2)}, u32[]{:S(2)}) collective-permute-start(f32[8,2048]{1,0:T(8,128)S(1)} %add.25), channel_id=1, source_target_pairs={{0,16},{8,24},{16,0},{24,8},{1,17},{9,25},{17,1},{25,9},{2,18},{10... | collective-permute-start | bytes 196616 | tf_op jit(solution)/shard_map/ppermute | solution.py:62
  29.9 17.3 %collective-permute-start.11 = (bf16[256,512]{1,0:T(8,128)(2,1)S(1)}, bf16[256,512]{1,0:T(8,128)(2,1)S(1)}, u32[]{:S(2)}, u32[]{:S(2)}) collective-permute-start(bf16[256,512]{1,0:T(8,128)(2,1)S(1)} %collective-permute-done.8.swapped_ref), channel_id=1, source_target_pairs={{0,2},{1,7},{2,4},{3,1},{4,6},{5,3},{6,0},{7,5},{8,10},{9,15},{10,... | collective-permute-start | bytes 786440 | tf_op jit(solution)/shard_map/ppermute | solution.py:72
  30.7 13.9 %collective-permute-start.13 = (bf16[256,512]{1,0:T(8,128)(2,1)S(1)}, bf16[256,512]{1,0:T(8,128)(2,1)S(1)}, u32[]{:S(2)}, u32[]{:S(2)}) collective-permute-start(bf16[256,512]{1,0:T(8,128)(2,1)S(1)} %get-tuple-element.73.own_ref), channel_id=1, source_target_pairs={{0,1},{1,0},{2,3},{3,2},{4,5},{5,4},{6,7},{7,6},{8,9},{9,8},{10,11... | collective-permute-start | bytes 786440 | tf_op jit(solution)/shard_map/ppermute | solution.py:62
  35.3 16.6 %collective-permute-start.14 = (bf16[256,512]{1,0:T(8,128)(2,1)S(1)}, bf16[256,512]{1,0:T(8,128)(2,1)S(1)}, u32[]{:S(2)}, u32[]{:S(2)}) collective-permute-start(bf16[256,512]{1,0:T(8,128)(2,1)S(1)} %slice.13), channel_id=1, source_target_pairs={{0,7},{1,0},{2,1},{3,2},{4,3},{5,4},{6,5},{7,6},{8,15},{9,8},{10,9... | collective-permute-start | bytes 786440 | tf_op jit(solution)/shard_map/ppermute | solution.py:77
  40.0 9.5 %collective-permute-start.12 = (bf16[256,512]{1,0:T(8,128)(2,1)S(1)}, bf16[256,512]{1,0:T(8,128)(2,1)S(1)}, u32[]{:S(2)}, u32[]{:S(2)}) collective-permute-start(bf16[256,512]{1,0:T(8,128)(2,1)S(1)} %collective-permute-done.6.swapped_ref), channel_id=1, source_target_pairs={{0,2},{1,7},{2,4},{3,1},{4,6},{5,3},{6,0},{7,5},{8,10},{9,15},{10,... | collective-permute-start | bytes 786440 | tf_op jit(solution)/shard_map/ppermute | solution.py:72
  44.6 9.8 %collective-permute-start.15 = (bf16[256,512]{1,0:T(8,128)(2,1)S(1)}, bf16[256,512]{1,0:T(8,128)(2,1)S(1)}, u32[]{:S(2)}, u32[]{:S(2)}) collective-permute-start(bf16[256,512]{1,0:T(8,128)(2,1)S(1)} %get-tuple-element.75.own_ref.refs_0_), channel_id=1, source_target_pairs={{0,1},{1,0},{2,3},{3,2},{4,5},{5,4},{6,7},{7,6},{8,9},{9,8},{10,11... | collective-permute-start | bytes 786440 | tf_op jit(solution)/shard_map/ppermute | solution.py:62
  47.2 8.3 %collective-permute-start.16 = (bf16[256,512]{1,0:T(8,128)(2,1)S(1)}, bf16[256,512]{1,0:T(8,128)(2,1)S(1)}, u32[]{:S(2)}, u32[]{:S(2)}) collective-permute-start(bf16[256,512]{1,0:T(8,128)(2,1)S(1)} %collective-permute-done.13.swapped_ref), channel_id=1, source_target_pairs={{0,2},{1,7},{2,4},{3,1},{4,6},{5,3},{6,0},{7,5},{8,10},{9,15},{10,... | collective-permute-start | bytes 786440 | tf_op jit(solution)/shard_map/ppermute | solution.py:72
  48.5 11.6 %collective-permute-start.17 = (bf16[256,512]{1,0:T(8,128)(2,1)S(1)}, bf16[256,512]{1,0:T(8,128)(2,1)S(1)}, u32[]{:S(2)}, u32[]{:S(2)}) collective-permute-start(bf16[256,512]{1,0:T(8,128)(2,1)S(1)} %get-tuple-element.78.own_ref.refs_1_), channel_id=1, source_target_pairs={{0,1},{1,0},{2,3},{3,2},{4,5},{5,4},{6,7},{7,6},{8,9},{9,8},{10,11... | collective-permute-start | bytes 786440 | tf_op jit(solution)/shard_map/ppermute | solution.py:62
  50.8 14.9 %collective-permute-start.19 = (bf16[256,512]{1,0:T(8,128)(2,1)S(1)}, bf16[256,512]{1,0:T(8,128)(2,1)S(1)}, u32[]{:S(2)}, u32[]{:S(2)}) collective-permute-start(bf16[256,512]{1,0:T(8,128)(2,1)S(1)} %get-tuple-element.82.own_ref.refs_2_), channel_id=1, source_target_pairs={{0,1},{1,0},{2,3},{3,2},{4,5},{5,4},{6,7},{7,6},{8,9},{9,8},{10,11... | collective-permute-start | bytes 786440 | tf_op jit(solution)/shard_map/ppermute | solution.py:62
  56.8 12.4 %collective-permute-start.21 = (bf16[256,512]{1,0:T(8,128)(2,1)S(1)}, bf16[256,512]{1,0:T(8,128)(2,1)S(1)}, u32[]{:S(2)}, u32[]{:S(2)}) collective-permute-start(bf16[256,512]{1,0:T(8,128)(2,1)S(1)} %get-tuple-element.84.own_ref.refs_3_), channel_id=1, source_target_pairs={{0,1},{1,0},{2,3},{3,2},{4,5},{5,4},{6,7},{7,6},{8,9},{9,8},{10,11... | collective-permute-start | bytes 786440 | tf_op jit(solution)/shard_map/ppermute | solution.py:62
  57.8 12.6 %collective-permute-start.18 = (bf16[256,512]{1,0:T(8,128)(2,1)S(1)}, bf16[256,512]{1,0:T(8,128)(2,1)S(1)}, u32[]{:S(2)}, u32[]{:S(2)}) collective-permute-start(bf16[256,512]{1,0:T(8,128)(2,1)S(1)} %collective-permute-done.15.swapped_ref), channel_id=1, source_target_pairs={{0,2},{1,7},{2,4},{3,1},{4,6},{5,3},{6,0},{7,5},{8,10},{9,15},{10,... | collective-permute-start | bytes 786440 | tf_op jit(solution)/shard_map/ppermute | solution.py:72
  60.0 13.8 %collective-permute-start.20 = (bf16[256,512]{1,0:T(8,128)(2,1)S(1)}, bf16[256,512]{1,0:T(8,128)(2,1)S(1)}, u32[]{:S(2)}, u32[]{:S(2)}) collective-permute-start(bf16[256,512]{1,0:T(8,128)(2,1)S(1)} %collective-permute-done.17.swapped_ref), channel_id=1, source_target_pairs={{0,2},{1,7},{2,4},{3,1},{4,6},{5,3},{6,0},{7,5},{8,10},{9,15},{10,... | collective-permute-start | bytes 786440 | tf_op jit(solution)/shard_map/ppermute | solution.py:72
  65.7 12.7 %collective-permute-start.22 = (bf16[256,512]{1,0:T(8,128)(2,1)S(1)}, bf16[256,512]{1,0:T(8,128)(2,1)S(1)}, u32[]{:S(2)}, u32[]{:S(2)}) collective-permute-start(bf16[256,512]{1,0:T(8,128)(2,1)S(1)} %collective-permute-done.19.swapped_ref), channel_id=1, source_target_pairs={{0,2},{1,7},{2,4},{3,1},{4,6},{5,3},{6,0},{7,5},{8,10},{9,15},{10,... | collective-permute-start | bytes 786440 | tf_op jit(solution)/shard_map/ppermute | solution.py:72
  69.1 12.0 %collective-permute-start.23 = (bf16[256,512]{1,0:T(8,128)(2,1)S(1)}, bf16[256,512]{1,0:T(8,128)(2,1)S(1)}, u32[]{:S(2)}, u32[]{:S(2)}) collective-permute-start(bf16[256,512]{1,0:T(8,128)(2,1)S(1)} %collective-permute-done.21.swapped_ref), channel_id=1, source_target_pairs={{0,2},{1,7},{2,4},{3,1},{4,6},{5,3},{6,0},{7,5},{8,10},{9,15},{10,... | collective-permute-start | bytes 786440 | tf_op jit(solution)/shard_map/ppermute | solution.py:72
  (8 other events, 113.8 us)

commit v4 on v3

--- a/solution.py
+++ b/solution.py
@@ -15,7 +15,7 @@
 
 EIGHTHS = (2, 2, 2, 2)
 TIES = {
-    "d0": ("s2",),
+    "d0": ("p1", "s2"),
     "d3": ("n", "x0"),
     "e": ("s0",),
     "g": ("c", "e"),
@@ -24,12 +24,13 @@
     "i1": ("x2",),
     "i2": ("x3",),
     "n": ("s2",),
+    "p2": ("p0",),
+    "p3": ("p2",),
     "s1": ("s0",),
     "s2": ("c", "s0"),
     "s3": ("m",),
     "t": ("s1",),
     "u": ("p0",),
-    "x0": ("s3",),
 }
 
 

time: 99.5 us -> 99.1 us (level)
    ppermute x16, waiting for transfers between devices: 27.9 us -> 23.3 us  [exchange(): return lax.ppermute(value, axis, [(i, i ^ step) for i in range(count)])]
    ppermute x8, waiting for transfers between devices: 11.4 us -> 15.9 us  [pass_on(): return lax.ppermute(value, 'sub', pairs)]
    ppermute x8, starting transfers between devices: 1.1 us -> 3.24 us  [pass_on(): return lax.ppermute(value, 'sub', pairs)]
    ppermute x16, starting transfers between devices: 19.2 us -> 17.3 us  [exchange(): return lax.ppermute(value, axis, [(i, i ^ step) for i in range(count)])]
  transfers between devices with their start and end apart: 26 -> 26, of which waited for: 20 -> 19; matrix products, arithmetic and copies ran while one was open for 1% -> 1% of each run, Pallas kernels for 11% -> 11%
where the time goes in v4:
time: 99.1 us; the launch traced here: 98.8 us
  waiting for transfers between devices  39.9 us (40%)
  starting transfers between devices  28.8 us (29%)
  Pallas kernels  15.7 us (16%)
  blocking collectives  11.8 us (12%)
  between operations  1.58 us (2%)
    ppermute x16, waiting for transfers between devices, exchange(): return lax.ppermute(value, axis, [(i, i ^ step) for i in range(count)])  23.3 us
    ppermute x16, starting transfers between devices, exchange(): return lax.ppermute(value, axis, [(i, i ^ step) for i in range(count)])  17.3 us
    ppermute x8, waiting for transfers between devices, pass_on(): return lax.ppermute(value, 'sub', pairs)  15.9 us
    all_to_all x1, blocking collectives, step_length(): lax.all_to_all(copies, ('grp', 'sub'), 0, 0, axis_index_groups=same, tile...  11.8 us
    ppermute x2, starting transfers between devices, to_left(): lax.ppermute(value, 'sub', [(j, (j - 1) % count) for j in range(count)])  8.29 us
    pallas_call x4, Pallas kernels, direction_chunk(): pl.pallas_call(functools.partial(direction_kernel, slice(begin, begin + s...  4.92 us
    pallas_call x4, Pallas kernels, image_chunk(): pl.pallas_call(image_kernel, out_shape=[pltpu.VMEM((rows, size), F32), sh...  4.04 us
    ppermute x8, starting transfers between devices, pass_on(): return lax.ppermute(value, 'sub', pairs)  3.24 us
  transfers between devices with their start and end apart: 26, of which 19 were waited for; matrix products, arithmetic and copies ran while one was open for 1% of the time, Pallas kernels for 11%

profile of v4, /device:TPU:0, one launch (start us, length us, event | category | flops | bytes accessed | tf_op | source)
XLA Modules:
  0.0 98.8 jit_solution(17930988460393066007)
XLA Ops:
  2.0 3.0 %collective-permute-start = (bf16[256,512]{1,0:T(8,128)(2,1)S(1)}, bf16[256,512]{1,0:T(8,128)(2,1)S(1)}, u32[]{:S(2)}, u32[]{:S(2)}) collective-permute-start(bf16[256,512]{1,0:T(8,128)(2,1)S(1)} %first.1.after_ref.own_ref), channel_id=1, source_target_pairs={{0,1},{1,0},{2,3},{3,2},{4,5},{5,4},{6,7},{7,6},{8,9},{9,8},{10,11... | collective-permute-start | bytes 786440 | tf_op jit(solution)/shard_map/ppermute | solution.py:63
  5.0 1.8 %pick.1.refs_0_ = f32[8,2048]{1,0:T(8,128)S(1)} custom-call(s32[1,8]{1,0:T(1,128)} %index_ref.9, f32[256,2048]{1,0:T(8,128)} %right_ref.15, bf16[256,512]{1,0:T(8,128)(2,1)S(1)} %first.1.after_ref.own_ref), custom_call_target="tpu_custom_call" | custom-call | tf_op jit(solution)/shard_map/pick/pallas_call | solution.py:133
  6.8 3.7 %collective-permute-start.3 = (f32[8,2048]{1,0:T(8,128)S(1)}, f32[8,2048]{1,0:T(8,128)S(1)}, u32[]{:S(2)}, u32[]{:S(2)}) collective-permute-start(f32[8,2048]{1,0:T(8,128)S(1)} %pick.1.refs_0_), channel_id=1, source_target_pairs={{0,6},{1,7},{2,4},{3,5},{4,2},{5,3},{6,0},{7,1},{8,14},{9,15},{10,... | collective-permute-start | bytes 196616 | tf_op jit(solution)/shard_map/ppermute | solution.py:63
  11.4 1.7 %collective-permute-start.6 = (bf16[256,512]{1,0:T(8,128)(2,1)S(1)}, bf16[256,512]{1,0:T(8,128)(2,1)S(1)}, u32[]{:S(2)}, u32[]{:S(2)}) collective-permute-start(bf16[256,512]{1,0:T(8,128)(2,1)S(1)} %get-tuple-element.63.own_ref), channel_id=1, source_target_pairs={{0,1},{1,0},{2,3},{3,2},{4,5},{5,4},{6,7},{7,6},{8,9},{9,8},{10,11... | collective-permute-start | bytes 786440 | tf_op jit(solution)/shard_map/ppermute | solution.py:63
  13.7 2.1 %collective-permute-done.2.refs_2_ = f32[8,2048]{1,0:T(8,128)S(1)} collective-permute-done((f32[8,2048]{1,0:T(8,128)S(1)}, f32[8,2048]{1,0:T(8,128)S(1)}, u32[]{:S(2)}, u32[]{:S(2)}) %collective-permute-start.2) | collective-permute-done | bytes 65568 | tf_op jit(solution)/shard_map/ppermute | solution.py:63
  18.4 2.8 %collective-permute-done.4 = f32[8,2048]{1,0:T(8,128)S(1)} collective-permute-done((f32[8,2048]{1,0:T(8,128)S(1)}, f32[8,2048]{1,0:T(8,128)S(1)}, u32[]{:S(2)}, u32[]{:S(2)}) %collective-permute-start.4) | collective-permute-done | bytes 65568 | tf_op jit(solution)/shard_map/ppermute | solution.py:63
  21.6 3.6 %collective-permute-start.5 = (bf16[256,512]{1,0:T(8,128)(2,1)S(1)}, bf16[256,512]{1,0:T(8,128)(2,1)S(1)}, u32[]{:S(2)}, u32[]{:S(2)}) collective-permute-start(bf16[256,512]{1,0:T(8,128)(2,1)S(1)} %get-tuple-element.52), channel_id=1, source_target_pairs={{0,7},{1,0},{2,1},{3,2},{4,3},{5,4},{6,5},{7,6},{8,15},{9,8},{10,9... | collective-permute-start | bytes 786440 | tf_op jit(solution)/shard_map/ppermute | solution.py:78
  25.2 1.2 %collective-permute-done.10 = f32[8,2048]{1,0:T(8,128)S(1)} collective-permute-done((f32[8,2048]{1,0:T(8,128)S(1)}, f32[8,2048]{1,0:T(8,128)S(1)}, u32[]{:S(2)}, u32[]{:S(2)}) %collective-permute-start.10) | collective-permute-done | bytes 65568 | tf_op jit(solution)/shard_map/ppermute | solution.py:63
  26.5 1.9 %collective-permute-done.9.passed_ref = bf16[256,512]{1,0:T(8,128)(2,1)S(1)} collective-permute-done((bf16[256,512]{1,0:T(8,128)(2,1)S(1)}, bf16[256,512]{1,0:T(8,128)(2,1)S(1)}, u32[]{:S(2)}, u32[]{:S(2)}) %collective-permute-start.9) | collective-permute-done | bytes 262176 | tf_op jit(solution)/shard_map/ppermute | solution.py:73
  28.3 1.6 %collective-permute-start.11 = (f32[8,2048]{1,0:T(8,128)S(1)}, f32[8,2048]{1,0:T(8,128)S(1)}, u32[]{:S(2)}, u32[]{:S(2)}) collective-permute-start(f32[8,2048]{1,0:T(8,128)S(1)} %add.25), channel_id=1, source_target_pairs={{0,16},{8,24},{16,0},{24,8},{1,17},{9,25},{17,1},{25,9},{2,18},{10... | collective-permute-start | bytes 196616 | tf_op jit(solution)/shard_map/ppermute | solution.py:63
  30.7 3.0 %collective-permute-start.13 = (bf16[256,512]{1,0:T(8,128)(2,1)S(1)}, bf16[256,512]{1,0:T(8,128)(2,1)S(1)}, u32[]{:S(2)}, u32[]{:S(2)}) collective-permute-start(bf16[256,512]{1,0:T(8,128)(2,1)S(1)} %get-tuple-element.74.own_ref), channel_id=1, source_target_pairs={{0,1},{1,0},{2,3},{3,2},{4,5},{5,4},{6,7},{7,6},{8,9},{9,8},{10,11... | collective-permute-start | bytes 786440 | tf_op jit(solution)/shard_map/ppermute | solution.py:63
  33.7 1.5 %collective-permute-done.8.swapped_ref = bf16[256,512]{1,0:T(8,128)(2,1)S(1)} collective-permute-done((bf16[256,512]{1,0:T(8,128)(2,1)S(1)}, bf16[256,512]{1,0:T(8,128)(2,1)S(1)}, u32[]{:S(2)}, u32[]{:S(2)}) %collective-permute-start.8) | collective-permute-done | bytes 262176 | tf_op jit(solution)/shard_map/ppermute | solution.py:63
  35.3 4.7 %collective-permute-start.14 = (bf16[256,512]{1,0:T(8,128)(2,1)S(1)}, bf16[256,512]{1,0:T(8,128)(2,1)S(1)}, u32[]{:S(2)}, u32[]{:S(2)}) collective-permute-start(bf16[256,512]{1,0:T(8,128)(2,1)S(1)} %slice.13), channel_id=1, source_target_pairs={{0,7},{1,0},{2,1},{3,2},{4,3},{5,4},{6,5},{7,6},{8,15},{9,8},{10,9... | collective-permute-start | bytes 786440 | tf_op jit(solution)/shard_map/ppermute | solution.py:78
  42.0 4.3 %collective-permute-done.13.swapped_ref = bf16[256,512]{1,0:T(8,128)(2,1)S(1)} collective-permute-done((bf16[256,512]{1,0:T(8,128)(2,1)S(1)}, bf16[256,512]{1,0:T(8,128)(2,1)S(1)}, u32[]{:S(2)}, u32[]{:S(2)}) %collective-permute-start.13) | collective-permute-done | bytes 262176 | tf_op jit(solution)/shard_map/ppermute | solution.py:63
  46.3 3.2 %collective-permute-done.12.passed_ref = bf16[256,512]{1,0:T(8,128)(2,1)S(1)} collective-permute-done((bf16[256,512]{1,0:T(8,128)(2,1)S(1)}, bf16[256,512]{1,0:T(8,128)(2,1)S(1)}, u32[]{:S(2)}, u32[]{:S(2)}) %collective-permute-start.12) | collective-permute-done | bytes 262176 | tf_op jit(solution)/shard_map/ppermute | solution.py:73
  51.0 2.1 %collective-permute-start.17 = (bf16[256,512]{1,0:T(8,128)(2,1)S(1)}, bf16[256,512]{1,0:T(8,128)(2,1)S(1)}, u32[]{:S(2)}, u32[]{:S(2)}) collective-permute-start(bf16[256,512]{1,0:T(8,128)(2,1)S(1)} %get-tuple-element.80.own_ref.refs_1_), channel_id=1, source_target_pairs={{0,1},{1,0},{2,3},{3,2},{4,5},{5,4},{6,7},{7,6},{8,9},{9,8},{10,11... | collective-permute-start | bytes 786440 | tf_op jit(solution)/shard_map/ppermute | solution.py:63
  54.4 3.3 %collective-permute-done.16.passed_ref = bf16[256,512]{1,0:T(8,128)(2,1)S(1)} collective-permute-done((bf16[256,512]{1,0:T(8,128)(2,1)S(1)}, bf16[256,512]{1,0:T(8,128)(2,1)S(1)}, u32[]{:S(2)}, u32[]{:S(2)}) %collective-permute-start.16) | collective-permute-done | bytes 262176 | tf_op jit(solution)/shard_map/ppermute | solution.py:73
  60.5 4.9 %collective-permute-done.19.swapped_ref = bf16[256,512]{1,0:T(8,128)(2,1)S(1)} collective-permute-done((bf16[256,512]{1,0:T(8,128)(2,1)S(1)}, bf16[256,512]{1,0:T(8,128)(2,1)S(1)}, u32[]{:S(2)}, u32[]{:S(2)}) %collective-permute-start.19) | collective-permute-done | bytes 262176 | tf_op jit(solution)/shard_map/ppermute | solution.py:63
  66.1 2.1 %collective-permute-done.21.swapped_ref = bf16[256,512]{1,0:T(8,128)(2,1)S(1)} collective-permute-done((bf16[256,512]{1,0:T(8,128)(2,1)S(1)}, bf16[256,512]{1,0:T(8,128)(2,1)S(1)}, u32[]{:S(2)}, u32[]{:S(2)}) %collective-permute-start.21) | collective-permute-done | bytes 262176 | tf_op jit(solution)/shard_map/ppermute | solution.py:63
  71.6 3.8 %collective-permute-done.20.passed_ref = bf16[256,512]{1,0:T(8,128)(2,1)S(1)} collective-permute-done((bf16[256,512]{1,0:T(8,128)(2,1)S(1)}, bf16[256,512]{1,0:T(8,128)(2,1)S(1)}, u32[]{:S(2)}, u32[]{:S(2)}) %collective-permute-start.20) | collective-permute-done | bytes 262176 | tf_op jit(solution)/shard_map/ppermute | solution.py:73
  76.5 1.9 %collective-permute-done.22.passed_ref = bf16[256,512]{1,0:T(8,128)(2,1)S(1)} collective-permute-done((bf16[256,512]{1,0:T(8,128)(2,1)S(1)}, bf16[256,512]{1,0:T(8,128)(2,1)S(1)}, u32[]{:S(2)}, u32[]{:S(2)}) %collective-permute-start.22) | collective-permute-done | bytes 262176 | tf_op jit(solution)/shard_map/ppermute | solution.py:73
  79.3 1.8 %collective-permute-done.23.passed_ref = bf16[256,512]{1,0:T(8,128)(2,1)S(1)} collective-permute-done((bf16[256,512]{1,0:T(8,128)(2,1)S(1)}, bf16[256,512]{1,0:T(8,128)(2,1)S(1)}, u32[]{:S(2)}, u32[]{:S(2)}) %collective-permute-start.23) | collective-permute-done | bytes 262176 | tf_op jit(solution)/shard_map/ppermute | solution.py:73
  83.5 11.8 %all_to_all.5.sums_ref = f32[16,2,1024]{2,1,0:T(2,128)S(1)} all-to-all(f32[16,2,1024]{2,1,0:T(2,128)S(1)} %broadcast_in_dim.30), channel_id=1, replica_groups={{0,1,2,3,4,5,6,7,16,17,18,19,20,21,22,23},{8,9,10,11,12,13,14,15,24,25,..., dimensions={0} | all-to-all | bytes 262144 | tf_op jit(solution)/shard_map/all_to_all | solution.py:93
  96.6 2.2 %update.1 = (f32[256,2048]{1,0:T(8,128)}, f32[256,2048]{1,0:T(8,128)}) custom-call(f32[1,2048]{1,0:T(1,128)S(1)} %pad_maximum_fusion.alpha_ref, f32[256,2048]{1,0:T(8,128)S(1)} %copy-done, bf16[256,512]{1,0:T(8,128)(2,1)S(1)} %get-tuple-element.77.own_ref.refs_0_, bf16[256,512]{1,0:T(8,128)(2,1)S(1)} %get-tuple-element.80.own_ref.refs_1_, ...), custom_call_target="tpu_custom_call" | custom-call | tf_op jit(solution)/shard_map/update/pallas_call | solution.py:327
  (70 shorter events, 23.3 us)
Async XLA Ops:
  2.0 9.4 %collective-permute-start = (bf16[256,512]{1,0:T(8,128)(2,1)S(1)}, bf16[256,512]{1,0:T(8,128)(2,1)S(1)}, u32[]{:S(2)}, u32[]{:S(2)}) collective-permute-start(bf16[256,512]{1,0:T(8,128)(2,1)S(1)} %first.1.after_ref.own_ref), channel_id=1, source_target_pairs={{0,1},{1,0},{2,3},{3,2},{4,5},{5,4},{6,7},{7,6},{8,9},{9,8},{10,11... | collective-permute-start | bytes 786440 | tf_op jit(solution)/shard_map/ppermute | solution.py:63
  6.8 6.9 %collective-permute-start.3 = (f32[8,2048]{1,0:T(8,128)S(1)}, f32[8,2048]{1,0:T(8,128)S(1)}, u32[]{:S(2)}, u32[]{:S(2)}) collective-permute-start(f32[8,2048]{1,0:T(8,128)S(1)} %pick.1.refs_0_), channel_id=1, source_target_pairs={{0,6},{1,7},{2,4},{3,5},{4,2},{5,3},{6,0},{7,1},{8,14},{9,15},{10,... | collective-permute-start | bytes 196616 | tf_op jit(solution)/shard_map/ppermute | solution.py:63
  10.5 5.4 %collective-permute-start.2 = (f32[8,2048]{1,0:T(8,128)S(1)}, f32[8,2048]{1,0:T(8,128)S(1)}, u32[]{:S(2)}, u32[]{:S(2)}) collective-permute-start(f32[8,2048]{1,0:T(8,128)S(1)} %pick.1.refs_0_), channel_id=1, source_target_pairs={{0,4},{1,5},{2,6},{3,7},{4,0},{5,1},{6,2},{7,3},{8,12},{9,13},{10,... | collective-permute-start | bytes 196616 | tf_op jit(solution)/shard_map/ppermute | solution.py:63
  10.5 5.4 %collective-permute-start.1 = (f32[8,2048]{1,0:T(8,128)S(1)}, f32[8,2048]{1,0:T(8,128)S(1)}, u32[]{:S(2)}, u32[]{:S(2)}) collective-permute-start(f32[8,2048]{1,0:T(8,128)S(1)} %pick.1.refs_0_), channel_id=1, source_target_pairs={{0,2},{1,3},{2,0},{3,1},{4,6},{5,7},{6,4},{7,5},{8,10},{9,11},{10,... | collective-permute-start | bytes 196616 | tf_op jit(solution)/shard_map/ppermute | solution.py:63
  11.4 13.8 %collective-permute-start.6 = (bf16[256,512]{1,0:T(8,128)(2,1)S(1)}, bf16[256,512]{1,0:T(8,128)(2,1)S(1)}, u32[]{:S(2)}, u32[]{:S(2)}) collective-permute-start(bf16[256,512]{1,0:T(8,128)(2,1)S(1)} %get-tuple-element.63.own_ref), channel_id=1, source_target_pairs={{0,1},{1,0},{2,3},{3,2},{4,5},{5,4},{6,7},{7,6},{8,9},{9,8},{10,11... | collective-permute-start | bytes 786440 | tf_op jit(solution)/shard_map/ppermute | solution.py:63
  16.8 4.3 %collective-permute-start.4 = (f32[8,2048]{1,0:T(8,128)S(1)}, f32[8,2048]{1,0:T(8,128)S(1)}, u32[]{:S(2)}, u32[]{:S(2)}) collective-permute-start(f32[8,2048]{1,0:T(8,128)S(1)} %get-tuple-element.49), channel_id=1, source_target_pairs={{0,1},{1,0},{2,3},{3,2},{4,5},{5,4},{6,7},{7,6},{8,9},{9,8},{10,11... | collective-permute-start | bytes 196616 | tf_op jit(solution)/shard_map/ppermute | solution.py:63
  17.3 11.0 %collective-permute-start.9 = (bf16[256,512]{1,0:T(8,128)(2,1)S(1)}, bf16[256,512]{1,0:T(8,128)(2,1)S(1)}, u32[]{:S(2)}, u32[]{:S(2)}) collective-permute-start(bf16[256,512]{1,0:T(8,128)(2,1)S(1)} %collective-permute-done.swapped_ref), channel_id=1, source_target_pairs={{0,2},{1,7},{2,4},{3,1},{4,6},{5,3},{6,0},{7,5},{8,10},{9,15},{10,... | collective-permute-start | bytes 786440 | tf_op jit(solution)/shard_map/ppermute | solution.py:73
  21.6 9.1 %collective-permute-start.5 = (bf16[256,512]{1,0:T(8,128)(2,1)S(1)}, bf16[256,512]{1,0:T(8,128)(2,1)S(1)}, u32[]{:S(2)}, u32[]{:S(2)}) collective-permute-start(bf16[256,512]{1,0:T(8,128)(2,1)S(1)} %get-tuple-element.52), channel_id=1, source_target_pairs={{0,7},{1,0},{2,1},{3,2},{4,3},{5,4},{6,5},{7,6},{8,15},{9,8},{10,9... | collective-permute-start | bytes 786440 | tf_op jit(solution)/shard_map/ppermute | solution.py:78
  25.2 10.1 %collective-permute-start.8 = (bf16[256,512]{1,0:T(8,128)(2,1)S(1)}, bf16[256,512]{1,0:T(8,128)(2,1)S(1)}, u32[]{:S(2)}, u32[]{:S(2)}) collective-permute-start(bf16[256,512]{1,0:T(8,128)(2,1)S(1)} %get-tuple-element.66.own_ref), channel_id=1, source_target_pairs={{0,1},{1,0},{2,3},{3,2},{4,5},{5,4},{6,7},{7,6},{8,9},{9,8},{10,11... | collective-permute-start | bytes 786440 | tf_op jit(solution)/shard_map/ppermute | solution.py:63
  25.2 1.3 %collective-permute-start.10 = (f32[8,2048]{1,0:T(8,128)S(1)}, f32[8,2048]{1,0:T(8,128)S(1)}, u32[]{:S(2)}, u32[]{:S(2)}) collective-permute-start(f32[8,2048]{1,0:T(8,128)S(1)} %add.24), channel_id=1, source_target_pairs={{0,8},{8,0},{16,24},{24,16},{1,9},{9,1},{17,25},{25,17},{2,10},{10... | collective-permute-start | bytes 196616 | tf_op jit(solution)/shard_map/ppermute | solution.py:63
  28.3 11.7 %collective-permute-start.11 = (f32[8,2048]{1,0:T(8,128)S(1)}, f32[8,2048]{1,0:T(8,128)S(1)}, u32[]{:S(2)}, u32[]{:S(2)}) collective-permute-start(f32[8,2048]{1,0:T(8,128)S(1)} %add.25), channel_id=1, source_target_pairs={{0,16},{8,24},{16,0},{24,8},{1,17},{9,25},{17,1},{25,9},{2,18},{10... | collective-permute-start | bytes 196616 | tf_op jit(solution)/shard_map/ppermute | solution.py:63
  29.9 10.1 %collective-permute-start.7 = (bf16[256,512]{1,0:T(8,128)(2,1)S(1)}, bf16[256,512]{1,0:T(8,128)(2,1)S(1)}, u32[]{:S(2)}, u32[]{:S(2)}) collective-permute-start(bf16[256,512]{1,0:T(8,128)(2,1)S(1)} %collective-permute-done.6.swapped_ref), channel_id=1, source_target_pairs={{0,2},{1,7},{2,4},{3,1},{4,6},{5,3},{6,0},{7,5},{8,10},{9,15},{10,... | collective-permute-start | bytes 786440 | tf_op jit(solution)/shard_map/ppermute | solution.py:73
  30.7 15.6 %collective-permute-start.13 = (bf16[256,512]{1,0:T(8,128)(2,1)S(1)}, bf16[256,512]{1,0:T(8,128)(2,1)S(1)}, u32[]{:S(2)}, u32[]{:S(2)}) collective-permute-start(bf16[256,512]{1,0:T(8,128)(2,1)S(1)} %get-tuple-element.74.own_ref), channel_id=1, source_target_pairs={{0,1},{1,0},{2,3},{3,2},{4,5},{5,4},{6,7},{7,6},{8,9},{9,8},{10,11... | collective-permute-start | bytes 786440 | tf_op jit(solution)/shard_map/ppermute | solution.py:63
  35.3 19.1 %collective-permute-start.14 = (bf16[256,512]{1,0:T(8,128)(2,1)S(1)}, bf16[256,512]{1,0:T(8,128)(2,1)S(1)}, u32[]{:S(2)}, u32[]{:S(2)}) collective-permute-start(bf16[256,512]{1,0:T(8,128)(2,1)S(1)} %slice.13), channel_id=1, source_target_pairs={{0,7},{1,0},{2,1},{3,2},{4,3},{5,4},{6,5},{7,6},{8,15},{9,8},{10,9... | collective-permute-start | bytes 786440 | tf_op jit(solution)/shard_map/ppermute | solution.py:78
  40.0 9.5 %collective-permute-start.12 = (bf16[256,512]{1,0:T(8,128)(2,1)S(1)}, bf16[256,512]{1,0:T(8,128)(2,1)S(1)}, u32[]{:S(2)}, u32[]{:S(2)}) collective-permute-start(bf16[256,512]{1,0:T(8,128)(2,1)S(1)} %collective-permute-done.8.swapped_ref), channel_id=1, source_target_pairs={{0,2},{1,7},{2,4},{3,1},{4,6},{5,3},{6,0},{7,5},{8,10},{9,15},{10,... | collective-permute-start | bytes 786440 | tf_op jit(solution)/shard_map/ppermute | solution.py:73
  41.3 13.1 %collective-permute-start.15 = (bf16[256,512]{1,0:T(8,128)(2,1)S(1)}, bf16[256,512]{1,0:T(8,128)(2,1)S(1)}, u32[]{:S(2)}, u32[]{:S(2)}) collective-permute-start(bf16[256,512]{1,0:T(8,128)(2,1)S(1)} %get-tuple-element.77.own_ref.refs_0_), channel_id=1, source_target_pairs={{0,1},{1,0},{2,3},{3,2},{4,5},{5,4},{6,7},{7,6},{8,9},{9,8},{10,11... | collective-permute-start | bytes 786440 | tf_op jit(solution)/shard_map/ppermute | solution.py:63
  49.5 8.2 %collective-permute-start.16 = (bf16[256,512]{1,0:T(8,128)(2,1)S(1)}, bf16[256,512]{1,0:T(8,128)(2,1)S(1)}, u32[]{:S(2)}, u32[]{:S(2)}) collective-permute-start(bf16[256,512]{1,0:T(8,128)(2,1)S(1)} %collective-permute-done.13.swapped_ref), channel_id=1, source_target_pairs={{0,2},{1,7},{2,4},{3,1},{4,6},{5,3},{6,0},{7,5},{8,10},{9,15},{10,... | collective-permute-start | bytes 786440 | tf_op jit(solution)/shard_map/ppermute | solution.py:73
  51.0 9.3 %collective-permute-start.17 = (bf16[256,512]{1,0:T(8,128)(2,1)S(1)}, bf16[256,512]{1,0:T(8,128)(2,1)S(1)}, u32[]{:S(2)}, u32[]{:S(2)}) collective-permute-start(bf16[256,512]{1,0:T(8,128)(2,1)S(1)} %get-tuple-element.80.own_ref.refs_1_), channel_id=1, source_target_pairs={{0,1},{1,0},{2,3},{3,2},{4,5},{5,4},{6,7},{7,6},{8,9},{9,8},{10,11... | collective-permute-start | bytes 786440 | tf_op jit(solution)/shard_map/ppermute | solution.py:63
  54.3 11.1 %collective-permute-start.19 = (bf16[256,512]{1,0:T(8,128)(2,1)S(1)}, bf16[256,512]{1,0:T(8,128)(2,1)S(1)}, u32[]{:S(2)}, u32[]{:S(2)}) collective-permute-start(bf16[256,512]{1,0:T(8,128)(2,1)S(1)} %get-tuple-element.84.own_ref.refs_2_), channel_id=1, source_target_pairs={{0,1},{1,0},{2,3},{3,2},{4,5},{5,4},{6,7},{7,6},{8,9},{9,8},{10,11... | collective-permute-start | bytes 786440 | tf_op jit(solution)/shard_map/ppermute | solution.py:63
  58.9 9.3 %collective-permute-start.21 = (bf16[256,512]{1,0:T(8,128)(2,1)S(1)}, bf16[256,512]{1,0:T(8,128)(2,1)S(1)}, u32[]{:S(2)}, u32[]{:S(2)}) collective-permute-start(bf16[256,512]{1,0:T(8,128)(2,1)S(1)} %get-tuple-element.86.own_ref.refs_3_), channel_id=1, source_target_pairs={{0,1},{1,0},{2,3},{3,2},{4,5},{5,4},{6,7},{7,6},{8,9},{9,8},{10,11... | collective-permute-start | bytes 786440 | tf_op jit(solution)/shard_map/ppermute | solution.py:63
  59.0 11.5 %collective-permute-start.18 = (bf16[256,512]{1,0:T(8,128)(2,1)S(1)}, bf16[256,512]{1,0:T(8,128)(2,1)S(1)}, u32[]{:S(2)}, u32[]{:S(2)}) collective-permute-start(bf16[256,512]{1,0:T(8,128)(2,1)S(1)} %collective-permute-done.15.swapped_ref), channel_id=1, source_target_pairs={{0,2},{1,7},{2,4},{3,1},{4,6},{5,3},{6,0},{7,5},{8,10},{9,15},{10,... | collective-permute-start | bytes 786440 | tf_op jit(solution)/shard_map/ppermute | solution.py:73
  60.3 15.2 %collective-permute-start.20 = (bf16[256,512]{1,0:T(8,128)(2,1)S(1)}, bf16[256,512]{1,0:T(8,128)(2,1)S(1)}, u32[]{:S(2)}, u32[]{:S(2)}) collective-permute-start(bf16[256,512]{1,0:T(8,128)(2,1)S(1)} %collective-permute-done.17.swapped_ref), channel_id=1, source_target_pairs={{0,2},{1,7},{2,4},{3,1},{4,6},{5,3},{6,0},{7,5},{8,10},{9,15},{10,... | collective-permute-start | bytes 786440 | tf_op jit(solution)/shard_map/ppermute | solution.py:73
  65.4 12.9 %collective-permute-start.22 = (bf16[256,512]{1,0:T(8,128)(2,1)S(1)}, bf16[256,512]{1,0:T(8,128)(2,1)S(1)}, u32[]{:S(2)}, u32[]{:S(2)}) collective-permute-start(bf16[256,512]{1,0:T(8,128)(2,1)S(1)} %collective-permute-done.19.swapped_ref), channel_id=1, source_target_pairs={{0,2},{1,7},{2,4},{3,1},{4,6},{5,3},{6,0},{7,5},{8,10},{9,15},{10,... | collective-permute-start | bytes 786440 | tf_op jit(solution)/shard_map/ppermute | solution.py:73
  68.2 12.9 %collective-permute-start.23 = (bf16[256,512]{1,0:T(8,128)(2,1)S(1)}, bf16[256,512]{1,0:T(8,128)(2,1)S(1)}, u32[]{:S(2)}, u32[]{:S(2)}) collective-permute-start(bf16[256,512]{1,0:T(8,128)(2,1)S(1)} %collective-permute-done.21.swapped_ref), channel_id=1, source_target_pairs={{0,2},{1,7},{2,4},{3,1},{4,6},{5,3},{6,0},{7,5},{8,10},{9,15},{10,... | collective-permute-start | bytes 786440 | tf_op jit(solution)/shard_map/ppermute | solution.py:73
  (8 other events, 106.9 us)

commit v5 on v4

--- a/solution.py
+++ b/solution.py
@@ -114,17 +114,14 @@
     )(place, right_side)
 
 
-def pick_kernel(index_ref, right_ref, after_ref, primal_ref, blocks, sems):
-    rank = primal_ref.shape[0]
+def pick_kernel(index_ref, right_ref, after_ref, primal_ref, sems):
     copies = []
-    for k in range(rank):
-        begin = pl.multiple_of((index_ref[0, k] >> 3) << 3, 8)
-        source = right_ref.at[pl.ds(begin, 8), :]
-        copies.append(pltpu.make_async_copy(source, blocks.at[k], sems.at[k]))
+    for k in range(primal_ref.shape[0]):
+        source = right_ref.at[pl.ds(index_ref[0, k], 1), :]
+        copies.append(pltpu.make_async_copy(source, primal_ref.at[k : k + 1, :], sems.at[k]))
         copies[-1].start()
-    for k in range(rank):
-        copies[k].wait()
-        primal_ref[k : k + 1, :] = blocks[k, pl.ds(index_ref[0, k] & 7, 1), :]
+    for copy in copies:
+        copy.wait()
 
 
 def pick(right_side, primal_index, first):
@@ -135,10 +132,7 @@
         out_shape=shape(rank, columns, F32),
         in_specs=[whole(SMEM), whole(pl.ANY), whole(pl.ANY)],
         out_specs=whole(),
-        scratch_shapes=[
-            pltpu.VMEM((rank, 8, columns), F32),
-            pltpu.SemaphoreType.DMA((rank,)),
-        ],
+        scratch_shapes=[pltpu.SemaphoreType.DMA((rank,))],
         compiler_params=params(8),
         name="pick",
     )(primal_index, right_side, first)

time: 99.1 us -> 99.7 us (level)
    ppermute x16, waiting for transfers between devices: 23.3 us -> 25 us  [exchange(): return lax.ppermute(value, axis, [(i, i ^ step) for i in range(count)])]
  transfers between devices with their start and end apart: 26 -> 26, of which waited for: 19 -> 20; matrix products, arithmetic and copies ran while one was open for 1% -> 1% of each run, Pallas kernels for 11% -> 11%
where the time goes in v5:
time: 99.7 us; the launch traced here: 99.5 us
  waiting for transfers between devices  40.8 us (41%)
  starting transfers between devices  28.2 us (28%)
  Pallas kernels  15.4 us (15%)
  blocking collectives  12.5 us (13%)
  between operations  1.57 us (2%)
    ppermute x16, waiting for transfers between devices, exchange(): return lax.ppermute(value, axis, [(i, i ^ step) for i in range(count)])  25 us
    ppermute x16, starting transfers between devices, exchange(): return lax.ppermute(value, axis, [(i, i ^ step) for i in range(count)])  17.2 us
    ppermute x8, waiting for transfers between devices, pass_on(): return lax.ppermute(value, 'sub', pairs)  14.9 us
    all_to_all x1, blocking collectives, step_length(): lax.all_to_all(copies, ('grp', 'sub'), 0, 0, axis_index_groups=same, tile...  12.5 us
    ppermute x2, starting transfers between devices, to_left(): lax.ppermute(value, 'sub', [(j, (j - 1) % count) for j in range(count)])  8.08 us
    pallas_call x4, Pallas kernels, direction_chunk(): pl.pallas_call(functools.partial(direction_kernel, slice(begin, begin + s...  4.92 us
    pallas_call x4, Pallas kernels, image_chunk(): pl.pallas_call(image_kernel, out_shape=[pltpu.VMEM((rows, size), F32), sh...  4.04 us
    ppermute x8, starting transfers between devices, pass_on(): return lax.ppermute(value, 'sub', pairs)  2.89 us
  transfers between devices with their start and end apart: 26, of which 20 were waited for; matrix products, arithmetic and copies ran while one was open for 1% of the time, Pallas kernels for 11%

profile of v5, /device:TPU:0, one launch (start us, length us, event | category | flops | bytes accessed | tf_op | source)
XLA Modules:
  0.0 99.5 jit_solution(10902685861685710722)
XLA Ops:
  2.0 3.0 %collective-permute-start = (bf16[256,512]{1,0:T(8,128)(2,1)S(1)}, bf16[256,512]{1,0:T(8,128)(2,1)S(1)}, u32[]{:S(2)}, u32[]{:S(2)}) collective-permute-start(bf16[256,512]{1,0:T(8,128)(2,1)S(1)} %first.1.after_ref.own_ref), channel_id=1, source_target_pairs={{0,1},{1,0},{2,3},{3,2},{4,5},{5,4},{6,7},{7,6},{8,9},{9,8},{10,11... | collective-permute-start | bytes 786440 | tf_op jit(solution)/shard_map/ppermute | solution.py:63
  5.0 1.5 %pick.1.refs_0_ = f32[8,2048]{1,0:T(8,128)S(1)} custom-call(s32[1,8]{1,0:T(1,128)} %index_ref.9, f32[256,2048]{1,0:T(8,128)} %right_ref.15, bf16[256,512]{1,0:T(8,128)(2,1)S(1)} %first.1.after_ref.own_ref), custom_call_target="tpu_custom_call" | custom-call | tf_op jit(solution)/shard_map/pick/pallas_call | solution.py:130
  6.6 3.7 %collective-permute-start.3 = (f32[8,2048]{1,0:T(8,128)S(1)}, f32[8,2048]{1,0:T(8,128)S(1)}, u32[]{:S(2)}, u32[]{:S(2)}) collective-permute-start(f32[8,2048]{1,0:T(8,128)S(1)} %pick.1.refs_0_), channel_id=1, source_target_pairs={{0,6},{1,7},{2,4},{3,5},{4,2},{5,3},{6,0},{7,1},{8,14},{9,15},{10,... | collective-permute-start | bytes 196616 | tf_op jit(solution)/shard_map/ppermute | solution.py:63
  11.3 1.7 %collective-permute-start.6 = (bf16[256,512]{1,0:T(8,128)(2,1)S(1)}, bf16[256,512]{1,0:T(8,128)(2,1)S(1)}, u32[]{:S(2)}, u32[]{:S(2)}) collective-permute-start(bf16[256,512]{1,0:T(8,128)(2,1)S(1)} %get-tuple-element.63.own_ref), channel_id=1, source_target_pairs={{0,1},{1,0},{2,3},{3,2},{4,5},{5,4},{6,7},{7,6},{8,9},{9,8},{10,11... | collective-permute-start | bytes 786440 | tf_op jit(solution)/shard_map/ppermute | solution.py:63
  13.5 2.1 %collective-permute-done.2.refs_2_ = f32[8,2048]{1,0:T(8,128)S(1)} collective-permute-done((f32[8,2048]{1,0:T(8,128)S(1)}, f32[8,2048]{1,0:T(8,128)S(1)}, u32[]{:S(2)}, u32[]{:S(2)}) %collective-permute-start.2) | collective-permute-done | bytes 65568 | tf_op jit(solution)/shard_map/ppermute | solution.py:63
  18.1 2.8 %collective-permute-done.4 = f32[8,2048]{1,0:T(8,128)S(1)} collective-permute-done((f32[8,2048]{1,0:T(8,128)S(1)}, f32[8,2048]{1,0:T(8,128)S(1)}, u32[]{:S(2)}, u32[]{:S(2)}) %collective-permute-start.4) | collective-permute-done | bytes 65568 | tf_op jit(solution)/shard_map/ppermute | solution.py:63
  21.4 3.8 %collective-permute-start.5 = (bf16[256,512]{1,0:T(8,128)(2,1)S(1)}, bf16[256,512]{1,0:T(8,128)(2,1)S(1)}, u32[]{:S(2)}, u32[]{:S(2)}) collective-permute-start(bf16[256,512]{1,0:T(8,128)(2,1)S(1)} %get-tuple-element.52), channel_id=1, source_target_pairs={{0,7},{1,0},{2,1},{3,2},{4,3},{5,4},{6,5},{7,6},{8,15},{9,8},{10,9... | collective-permute-start | bytes 786440 | tf_op jit(solution)/shard_map/ppermute | solution.py:78
  26.5 1.6 %collective-permute-done.9.passed_ref = bf16[256,512]{1,0:T(8,128)(2,1)S(1)} collective-permute-done((bf16[256,512]{1,0:T(8,128)(2,1)S(1)}, bf16[256,512]{1,0:T(8,128)(2,1)S(1)}, u32[]{:S(2)}, u32[]{:S(2)}) %collective-permute-start.9) | collective-permute-done | bytes 262176 | tf_op jit(solution)/shard_map/ppermute | solution.py:73
  28.1 1.6 %collective-permute-start.11 = (f32[8,2048]{1,0:T(8,128)S(1)}, f32[8,2048]{1,0:T(8,128)S(1)}, u32[]{:S(2)}, u32[]{:S(2)}) collective-permute-start(f32[8,2048]{1,0:T(8,128)S(1)} %add.25), channel_id=1, source_target_pairs={{0,16},{8,24},{16,0},{24,8},{1,17},{9,25},{17,1},{25,9},{2,18},{10... | collective-permute-start | bytes 196616 | tf_op jit(solution)/shard_map/ppermute | solution.py:63
  30.6 2.9 %collective-permute-start.13 = (bf16[256,512]{1,0:T(8,128)(2,1)S(1)}, bf16[256,512]{1,0:T(8,128)(2,1)S(1)}, u32[]{:S(2)}, u32[]{:S(2)}) collective-permute-start(bf16[256,512]{1,0:T(8,128)(2,1)S(1)} %get-tuple-element.74.own_ref), channel_id=1, source_target_pairs={{0,1},{1,0},{2,3},{3,2},{4,5},{5,4},{6,7},{7,6},{8,9},{9,8},{10,11... | collective-permute-start | bytes 786440 | tf_op jit(solution)/shard_map/ppermute | solution.py:63
  33.4 2.3 %collective-permute-done.8.swapped_ref = bf16[256,512]{1,0:T(8,128)(2,1)S(1)} collective-permute-done((bf16[256,512]{1,0:T(8,128)(2,1)S(1)}, bf16[256,512]{1,0:T(8,128)(2,1)S(1)}, u32[]{:S(2)}, u32[]{:S(2)}) %collective-permute-start.8) | collective-permute-done | bytes 262176 | tf_op jit(solution)/shard_map/ppermute | solution.py:63
  35.8 4.2 %collective-permute-start.14 = (bf16[256,512]{1,0:T(8,128)(2,1)S(1)}, bf16[256,512]{1,0:T(8,128)(2,1)S(1)}, u32[]{:S(2)}, u32[]{:S(2)}) collective-permute-start(bf16[256,512]{1,0:T(8,128)(2,1)S(1)} %slice.13), channel_id=1, source_target_pairs={{0,7},{1,0},{2,1},{3,2},{4,3},{5,4},{6,5},{7,6},{8,15},{9,8},{10,9... | collective-permute-start | bytes 786440 | tf_op jit(solution)/shard_map/ppermute | solution.py:78
  42.0 4.7 %collective-permute-done.13.swapped_ref = bf16[256,512]{1,0:T(8,128)(2,1)S(1)} collective-permute-done((bf16[256,512]{1,0:T(8,128)(2,1)S(1)}, bf16[256,512]{1,0:T(8,128)(2,1)S(1)}, u32[]{:S(2)}, u32[]{:S(2)}) %collective-permute-start.13) | collective-permute-done | bytes 262176 | tf_op jit(solution)/shard_map/ppermute | solution.py:63
  46.7 2.7 %collective-permute-done.12.passed_ref = bf16[256,512]{1,0:T(8,128)(2,1)S(1)} collective-permute-done((bf16[256,512]{1,0:T(8,128)(2,1)S(1)}, bf16[256,512]{1,0:T(8,128)(2,1)S(1)}, u32[]{:S(2)}, u32[]{:S(2)}) %collective-permute-start.12) | collective-permute-done | bytes 262176 | tf_op jit(solution)/shard_map/ppermute | solution.py:73
  51.4 1.7 %collective-permute-start.17 = (bf16[256,512]{1,0:T(8,128)(2,1)S(1)}, bf16[256,512]{1,0:T(8,128)(2,1)S(1)}, u32[]{:S(2)}, u32[]{:S(2)}) collective-permute-start(bf16[256,512]{1,0:T(8,128)(2,1)S(1)} %get-tuple-element.80.own_ref.refs_1_), channel_id=1, source_target_pairs={{0,1},{1,0},{2,3},{3,2},{4,5},{5,4},{6,7},{7,6},{8,9},{9,8},{10,11... | collective-permute-start | bytes 786440 | tf_op jit(solution)/shard_map/ppermute | solution.py:63
  54.8 2.7 %collective-permute-done.16.passed_ref = bf16[256,512]{1,0:T(8,128)(2,1)S(1)} collective-permute-done((bf16[256,512]{1,0:T(8,128)(2,1)S(1)}, bf16[256,512]{1,0:T(8,128)(2,1)S(1)}, u32[]{:S(2)}, u32[]{:S(2)}) %collective-permute-start.16) | collective-permute-done | bytes 262176 | tf_op jit(solution)/shard_map/ppermute | solution.py:73
  58.9 1.8 %collective-permute-done.17.swapped_ref = bf16[256,512]{1,0:T(8,128)(2,1)S(1)} collective-permute-done((bf16[256,512]{1,0:T(8,128)(2,1)S(1)}, bf16[256,512]{1,0:T(8,128)(2,1)S(1)}, u32[]{:S(2)}, u32[]{:S(2)}) %collective-permute-start.17) | collective-permute-done | bytes 262176 | tf_op jit(solution)/shard_map/ppermute | solution.py:63
  60.7 4.7 %collective-permute-done.19.swapped_ref = bf16[256,512]{1,0:T(8,128)(2,1)S(1)} collective-permute-done((bf16[256,512]{1,0:T(8,128)(2,1)S(1)}, bf16[256,512]{1,0:T(8,128)(2,1)S(1)}, u32[]{:S(2)}, u32[]{:S(2)}) %collective-permute-start.19) | collective-permute-done | bytes 262176 | tf_op jit(solution)/shard_map/ppermute | solution.py:63
  65.9 2.3 %collective-permute-done.21.swapped_ref = bf16[256,512]{1,0:T(8,128)(2,1)S(1)} collective-permute-done((bf16[256,512]{1,0:T(8,128)(2,1)S(1)}, bf16[256,512]{1,0:T(8,128)(2,1)S(1)}, u32[]{:S(2)}, u32[]{:S(2)}) %collective-permute-start.21) | collective-permute-done | bytes 262176 | tf_op jit(solution)/shard_map/ppermute | solution.py:63
  71.2 4.2 %collective-permute-done.20.passed_ref = bf16[256,512]{1,0:T(8,128)(2,1)S(1)} collective-permute-done((bf16[256,512]{1,0:T(8,128)(2,1)S(1)}, bf16[256,512]{1,0:T(8,128)(2,1)S(1)}, u32[]{:S(2)}, u32[]{:S(2)}) %collective-permute-start.20) | collective-permute-done | bytes 262176 | tf_op jit(solution)/shard_map/ppermute | solution.py:73
  76.4 1.9 %collective-permute-done.22.passed_ref = bf16[256,512]{1,0:T(8,128)(2,1)S(1)} collective-permute-done((bf16[256,512]{1,0:T(8,128)(2,1)S(1)}, bf16[256,512]{1,0:T(8,128)(2,1)S(1)}, u32[]{:S(2)}, u32[]{:S(2)}) %collective-permute-start.22) | collective-permute-done | bytes 262176 | tf_op jit(solution)/shard_map/ppermute | solution.py:73
  79.3 1.8 %collective-permute-done.23.passed_ref = bf16[256,512]{1,0:T(8,128)(2,1)S(1)} collective-permute-done((bf16[256,512]{1,0:T(8,128)(2,1)S(1)}, bf16[256,512]{1,0:T(8,128)(2,1)S(1)}, u32[]{:S(2)}, u32[]{:S(2)}) %collective-permute-start.23) | collective-permute-done | bytes 262176 | tf_op jit(solution)/shard_map/ppermute | solution.py:73
  83.4 12.5 %all_to_all.5.sums_ref = f32[16,2,1024]{2,1,0:T(2,128)S(1)} all-to-all(f32[16,2,1024]{2,1,0:T(2,128)S(1)} %broadcast_in_dim.30), channel_id=1, replica_groups={{0,1,2,3,4,5,6,7,16,17,18,19,20,21,22,23},{8,9,10,11,12,13,14,15,24,25,..., dimensions={0} | all-to-all | bytes 262144 | tf_op jit(solution)/shard_map/all_to_all | solution.py:93
  97.3 2.2 %update.1 = (f32[256,2048]{1,0:T(8,128)}, f32[256,2048]{1,0:T(8,128)}) custom-call(f32[1,2048]{1,0:T(1,128)S(1)} %pad_maximum_fusion.alpha_ref, f32[256,2048]{1,0:T(8,128)S(1)} %copy-done, bf16[256,512]{1,0:T(8,128)(2,1)S(1)} %get-tuple-element.77.own_ref.refs_0_, bf16[256,512]{1,0:T(8,128)(2,1)S(1)} %get-tuple-element.80.own_ref.refs_1_, ...), custom_call_target="tpu_custom_call" | custom-call | tf_op jit(solution)/shard_map/update/pallas_call | solution.py:321
  (70 shorter events, 23.4 us)
Async XLA Ops:
  2.0 9.3 %collective-permute-start = (bf16[256,512]{1,0:T(8,128)(2,1)S(1)}, bf16[256,512]{1,0:T(8,128)(2,1)S(1)}, u32[]{:S(2)}, u32[]{:S(2)}) collective-permute-start(bf16[256,512]{1,0:T(8,128)(2,1)S(1)} %first.1.after_ref.own_ref), channel_id=1, source_target_pairs={{0,1},{1,0},{2,3},{3,2},{4,5},{5,4},{6,7},{7,6},{8,9},{9,8},{10,11... | collective-permute-start | bytes 786440 | tf_op jit(solution)/shard_map/ppermute | solution.py:63
  6.6 6.9 %collective-permute-start.3 = (f32[8,2048]{1,0:T(8,128)S(1)}, f32[8,2048]{1,0:T(8,128)S(1)}, u32[]{:S(2)}, u32[]{:S(2)}) collective-permute-start(f32[8,2048]{1,0:T(8,128)S(1)} %pick.1.refs_0_), channel_id=1, source_target_pairs={{0,6},{1,7},{2,4},{3,5},{4,2},{5,3},{6,0},{7,1},{8,14},{9,15},{10,... | collective-permute-start | bytes 196616 | tf_op jit(solution)/shard_map/ppermute | solution.py:63
  10.2 5.4 %collective-permute-start.2 = (f32[8,2048]{1,0:T(8,128)S(1)}, f32[8,2048]{1,0:T(8,128)S(1)}, u32[]{:S(2)}, u32[]{:S(2)}) collective-permute-start(f32[8,2048]{1,0:T(8,128)S(1)} %pick.1.refs_0_), channel_id=1, source_target_pairs={{0,4},{1,5},{2,6},{3,7},{4,0},{5,1},{6,2},{7,3},{8,12},{9,13},{10,... | collective-permute-start | bytes 196616 | tf_op jit(solution)/shard_map/ppermute | solution.py:63
  10.2 5.4 %collective-permute-start.1 = (f32[8,2048]{1,0:T(8,128)S(1)}, f32[8,2048]{1,0:T(8,128)S(1)}, u32[]{:S(2)}, u32[]{:S(2)}) collective-permute-start(f32[8,2048]{1,0:T(8,128)S(1)} %pick.1.refs_0_), channel_id=1, source_target_pairs={{0,2},{1,3},{2,0},{3,1},{4,6},{5,7},{6,4},{7,5},{8,10},{9,11},{10,... | collective-permute-start | bytes 196616 | tf_op jit(solution)/shard_map/ppermute | solution.py:63
  11.3 13.9 %collective-permute-start.6 = (bf16[256,512]{1,0:T(8,128)(2,1)S(1)}, bf16[256,512]{1,0:T(8,128)(2,1)S(1)}, u32[]{:S(2)}, u32[]{:S(2)}) collective-permute-start(bf16[256,512]{1,0:T(8,128)(2,1)S(1)} %get-tuple-element.63.own_ref), channel_id=1, source_target_pairs={{0,1},{1,0},{2,3},{3,2},{4,5},{5,4},{6,7},{7,6},{8,9},{9,8},{10,11... | collective-permute-start | bytes 786440 | tf_op jit(solution)/shard_map/ppermute | solution.py:63
  16.6 4.3 %collective-permute-start.4 = (f32[8,2048]{1,0:T(8,128)S(1)}, f32[8,2048]{1,0:T(8,128)S(1)}, u32[]{:S(2)}, u32[]{:S(2)}) collective-permute-start(f32[8,2048]{1,0:T(8,128)S(1)} %get-tuple-element.49), channel_id=1, source_target_pairs={{0,1},{1,0},{2,3},{3,2},{4,5},{5,4},{6,7},{7,6},{8,9},{9,8},{10,11... | collective-permute-start | bytes 196616 | tf_op jit(solution)/shard_map/ppermute | solution.py:63
  17.0 11.0 %collective-permute-start.9 = (bf16[256,512]{1,0:T(8,128)(2,1)S(1)}, bf16[256,512]{1,0:T(8,128)(2,1)S(1)}, u32[]{:S(2)}, u32[]{:S(2)}) collective-permute-start(bf16[256,512]{1,0:T(8,128)(2,1)S(1)} %collective-permute-done.swapped_ref), channel_id=1, source_target_pairs={{0,2},{1,7},{2,4},{3,1},{4,6},{5,3},{6,0},{7,5},{8,10},{9,15},{10,... | collective-permute-start | bytes 786440 | tf_op jit(solution)/shard_map/ppermute | solution.py:73
  21.4 9.2 %collective-permute-start.5 = (bf16[256,512]{1,0:T(8,128)(2,1)S(1)}, bf16[256,512]{1,0:T(8,128)(2,1)S(1)}, u32[]{:S(2)}, u32[]{:S(2)}) collective-permute-start(bf16[256,512]{1,0:T(8,128)(2,1)S(1)} %get-tuple-element.52), channel_id=1, source_target_pairs={{0,7},{1,0},{2,1},{3,2},{4,3},{5,4},{6,5},{7,6},{8,15},{9,8},{10,9... | collective-permute-start | bytes 786440 | tf_op jit(solution)/shard_map/ppermute | solution.py:78
  25.2 10.5 %collective-permute-start.8 = (bf16[256,512]{1,0:T(8,128)(2,1)S(1)}, bf16[256,512]{1,0:T(8,128)(2,1)S(1)}, u32[]{:S(2)}, u32[]{:S(2)}) collective-permute-start(bf16[256,512]{1,0:T(8,128)(2,1)S(1)} %get-tuple-element.66.own_ref), channel_id=1, source_target_pairs={{0,1},{1,0},{2,3},{3,2},{4,5},{5,4},{6,7},{7,6},{8,9},{9,8},{10,11... | collective-permute-start | bytes 786440 | tf_op jit(solution)/shard_map/ppermute | solution.py:63
  25.2 1.3 %collective-permute-start.10 = (f32[8,2048]{1,0:T(8,128)S(1)}, f32[8,2048]{1,0:T(8,128)S(1)}, u32[]{:S(2)}, u32[]{:S(2)}) collective-permute-start(f32[8,2048]{1,0:T(8,128)S(1)} %add.24), channel_id=1, source_target_pairs={{0,8},{8,0},{16,24},{24,16},{1,9},{9,1},{17,25},{25,17},{2,10},{10... | collective-permute-start | bytes 196616 | tf_op jit(solution)/shard_map/ppermute | solution.py:63
  28.1 11.9 %collective-permute-start.11 = (f32[8,2048]{1,0:T(8,128)S(1)}, f32[8,2048]{1,0:T(8,128)S(1)}, u32[]{:S(2)}, u32[]{:S(2)}) collective-permute-start(f32[8,2048]{1,0:T(8,128)S(1)} %add.25), channel_id=1, source_target_pairs={{0,16},{8,24},{16,0},{24,8},{1,17},{9,25},{17,1},{25,9},{2,18},{10... | collective-permute-start | bytes 196616 | tf_op jit(solution)/shard_map/ppermute | solution.py:63
  29.7 10.3 %collective-permute-start.7 = (bf16[256,512]{1,0:T(8,128)(2,1)S(1)}, bf16[256,512]{1,0:T(8,128)(2,1)S(1)}, u32[]{:S(2)}, u32[]{:S(2)}) collective-permute-start(bf16[256,512]{1,0:T(8,128)(2,1)S(1)} %collective-permute-done.6.swapped_ref), channel_id=1, source_target_pairs={{0,2},{1,7},{2,4},{3,1},{4,6},{5,3},{6,0},{7,5},{8,10},{9,15},{10,... | collective-permute-start | bytes 786440 | tf_op jit(solution)/shard_map/ppermute | solution.py:73
  30.6 16.1 %collective-permute-start.13 = (bf16[256,512]{1,0:T(8,128)(2,1)S(1)}, bf16[256,512]{1,0:T(8,128)(2,1)S(1)}, u32[]{:S(2)}, u32[]{:S(2)}) collective-permute-start(bf16[256,512]{1,0:T(8,128)(2,1)S(1)} %get-tuple-element.74.own_ref), channel_id=1, source_target_pairs={{0,1},{1,0},{2,3},{3,2},{4,5},{5,4},{6,7},{7,6},{8,9},{9,8},{10,11... | collective-permute-start | bytes 786440 | tf_op jit(solution)/shard_map/ppermute | solution.py:63
  35.8 19.0 %collective-permute-start.14 = (bf16[256,512]{1,0:T(8,128)(2,1)S(1)}, bf16[256,512]{1,0:T(8,128)(2,1)S(1)}, u32[]{:S(2)}, u32[]{:S(2)}) collective-permute-start(bf16[256,512]{1,0:T(8,128)(2,1)S(1)} %slice.13), channel_id=1, source_target_pairs={{0,7},{1,0},{2,1},{3,2},{4,3},{5,4},{6,5},{7,6},{8,15},{9,8},{10,9... | collective-permute-start | bytes 786440 | tf_op jit(solution)/shard_map/ppermute | solution.py:78
  40.0 9.3 %collective-permute-start.12 = (bf16[256,512]{1,0:T(8,128)(2,1)S(1)}, bf16[256,512]{1,0:T(8,128)(2,1)S(1)}, u32[]{:S(2)}, u32[]{:S(2)}) collective-permute-start(bf16[256,512]{1,0:T(8,128)(2,1)S(1)} %collective-permute-done.8.swapped_ref), channel_id=1, source_target_pairs={{0,2},{1,7},{2,4},{3,1},{4,6},{5,3},{6,0},{7,5},{8,10},{9,15},{10,... | collective-permute-start | bytes 786440 | tf_op jit(solution)/shard_map/ppermute | solution.py:73
  41.3 13.5 %collective-permute-start.15 = (bf16[256,512]{1,0:T(8,128)(2,1)S(1)}, bf16[256,512]{1,0:T(8,128)(2,1)S(1)}, u32[]{:S(2)}, u32[]{:S(2)}) collective-permute-start(bf16[256,512]{1,0:T(8,128)(2,1)S(1)} %get-tuple-element.77.own_ref.refs_0_), channel_id=1, source_target_pairs={{0,1},{1,0},{2,3},{3,2},{4,5},{5,4},{6,7},{7,6},{8,9},{9,8},{10,11... | collective-permute-start | bytes 786440 | tf_op jit(solution)/shard_map/ppermute | solution.py:63
  49.3 8.2 %collective-permute-start.16 = (bf16[256,512]{1,0:T(8,128)(2,1)S(1)}, bf16[256,512]{1,0:T(8,128)(2,1)S(1)}, u32[]{:S(2)}, u32[]{:S(2)}) collective-permute-start(bf16[256,512]{1,0:T(8,128)(2,1)S(1)} %collective-permute-done.13.swapped_ref), channel_id=1, source_target_pairs={{0,2},{1,7},{2,4},{3,1},{4,6},{5,3},{6,0},{7,5},{8,10},{9,15},{10,... | collective-permute-start | bytes 786440 | tf_op jit(solution)/shard_map/ppermute | solution.py:73
  51.4 9.3 %collective-permute-start.17 = (bf16[256,512]{1,0:T(8,128)(2,1)S(1)}, bf16[256,512]{1,0:T(8,128)(2,1)S(1)}, u32[]{:S(2)}, u32[]{:S(2)}) collective-permute-start(bf16[256,512]{1,0:T(8,128)(2,1)S(1)} %get-tuple-element.80.own_ref.refs_1_), channel_id=1, source_target_pairs={{0,1},{1,0},{2,3},{3,2},{4,5},{5,4},{6,7},{7,6},{8,9},{9,8},{10,11... | collective-permute-start | bytes 786440 | tf_op jit(solution)/shard_map/ppermute | solution.py:63
  54.3 11.1 %collective-permute-start.19 = (bf16[256,512]{1,0:T(8,128)(2,1)S(1)}, bf16[256,512]{1,0:T(8,128)(2,1)S(1)}, u32[]{:S(2)}, u32[]{:S(2)}) collective-permute-start(bf16[256,512]{1,0:T(8,128)(2,1)S(1)} %get-tuple-element.84.own_ref.refs_2_), channel_id=1, source_target_pairs={{0,1},{1,0},{2,3},{3,2},{4,5},{5,4},{6,7},{7,6},{8,9},{9,8},{10,11... | collective-permute-start | bytes 786440 | tf_op jit(solution)/shard_map/ppermute | solution.py:63
  58.7 9.4 %collective-permute-start.21 = (bf16[256,512]{1,0:T(8,128)(2,1)S(1)}, bf16[256,512]{1,0:T(8,128)(2,1)S(1)}, u32[]{:S(2)}, u32[]{:S(2)}) collective-permute-start(bf16[256,512]{1,0:T(8,128)(2,1)S(1)} %get-tuple-element.86.own_ref.refs_3_), channel_id=1, source_target_pairs={{0,1},{1,0},{2,3},{3,2},{4,5},{5,4},{6,7},{7,6},{8,9},{9,8},{10,11... | collective-permute-start | bytes 786440 | tf_op jit(solution)/shard_map/ppermute | solution.py:63
  58.8 11.2 %collective-permute-start.18 = (bf16[256,512]{1,0:T(8,128)(2,1)S(1)}, bf16[256,512]{1,0:T(8,128)(2,1)S(1)}, u32[]{:S(2)}, u32[]{:S(2)}) collective-permute-start(bf16[256,512]{1,0:T(8,128)(2,1)S(1)} %collective-permute-done.15.swapped_ref), channel_id=1, source_target_pairs={{0,2},{1,7},{2,4},{3,1},{4,6},{5,3},{6,0},{7,5},{8,10},{9,15},{10,... | collective-permute-start | bytes 786440 | tf_op jit(solution)/shard_map/ppermute | solution.py:73
  60.7 14.7 %collective-permute-start.20 = (bf16[256,512]{1,0:T(8,128)(2,1)S(1)}, bf16[256,512]{1,0:T(8,128)(2,1)S(1)}, u32[]{:S(2)}, u32[]{:S(2)}) collective-permute-start(bf16[256,512]{1,0:T(8,128)(2,1)S(1)} %collective-permute-done.17.swapped_ref), channel_id=1, source_target_pairs={{0,2},{1,7},{2,4},{3,1},{4,6},{5,3},{6,0},{7,5},{8,10},{9,15},{10,... | collective-permute-start | bytes 786440 | tf_op jit(solution)/shard_map/ppermute | solution.py:73
  65.4 12.9 %collective-permute-start.22 = (bf16[256,512]{1,0:T(8,128)(2,1)S(1)}, bf16[256,512]{1,0:T(8,128)(2,1)S(1)}, u32[]{:S(2)}, u32[]{:S(2)}) collective-permute-start(bf16[256,512]{1,0:T(8,128)(2,1)S(1)} %collective-permute-done.19.swapped_ref), channel_id=1, source_target_pairs={{0,2},{1,7},{2,4},{3,1},{4,6},{5,3},{6,0},{7,5},{8,10},{9,15},{10,... | collective-permute-start | bytes 786440 | tf_op jit(solution)/shard_map/ppermute | solution.py:73
  68.2 12.9 %collective-permute-start.23 = (bf16[256,512]{1,0:T(8,128)(2,1)S(1)}, bf16[256,512]{1,0:T(8,128)(2,1)S(1)}, u32[]{:S(2)}, u32[]{:S(2)}) collective-permute-start(bf16[256,512]{1,0:T(8,128)(2,1)S(1)} %collective-permute-done.21.swapped_ref), channel_id=1, source_target_pairs={{0,2},{1,7},{2,4},{3,1},{4,6},{5,3},{6,0},{7,5},{8,10},{9,15},{10,... | collective-permute-start | bytes 786440 | tf_op jit(solution)/shard_map/ppermute | solution.py:73
  (8 other events, 105.9 us)
